TPU v7x, 32 devices: a whole 2x2x4 slice. The times are simulated.
32 devices in a mesh: img: 2 (over x), row: 4 (over y, core), col: 4 (over z).
Axes of the slice: x: 2, y: 2, z: 4, core: 2. Of those that a mesh axis runs over, the one named last changes fastest.
Arguments:
- grid_elements: bfloat16 [256, 128, 768], P(('img', 'row'), 'col'), parts along dimension 0, may hold values from -6 to 6
- summary_vectors: bfloat16 [16, 8, 768], P(('img', 'row'), 'col'), parts along dimension 0, may hold values from -6 to 6
- triple_projection: bfloat16 [768, 2304], P(None, 'row'), may hold values from -0.375 to 0.375
- final_projection: bfloat16 [768, 768], P(None, 'row'), may hold values from -0.21875 to 0.21875
- genuine_flags: int32 [256, 128], P(('img', 'row'), 'col'), parts along dimension 0, may hold values 0 or 1
Outputs:
- element_result: bfloat16 [256, 128, 768], P(('img', 'row'), 'col'), parts along dimension 0
- summary_result: bfloat16 [16, 8, 768], P(('img', 'row'), 'col'), parts along dimension 0
There are 2 independent parts, one for each index of `img`. A program takes and returns all parts, laid end to end along the dimension named above; an argument that names none is the same for every part. Nothing has to cross between parts.
All inputs are finite; a program needn't handle non-finite values. No bound on the sum of `genuine_flags` on one device may be relied on, other than what follows from the above.
Results may differ from a plain program's by a relative error of at most 0.0096.
Values may be sent and summed in bfloat16 or wider, within the bound.
No kernel may reach another device: no remote copies, remote signals or barrier semaphores. Data moves between devices by JAX's collectives and lax.ppermute only.
A program may use at most 64 MiB of HBM per device.

v0:
```python
import functools

import jax
import jax.numpy as jnp
from jax import lax
from jax.experimental import pallas as pl
from jax.experimental.pallas import tpu as pltpu
from jax.sharding import PartitionSpec as P

HEAD_DIM = 64
PATCH_SIDE = 16
RADIUS = 4
TILE = 2 * RADIUS
LANES = 128
GROUP = 256
INVALID = 100.0
HIDDEN = -1e30
LOG2_E = 1.4426950408889634
EVEN_ROW, EVEN_COL, ROW, HALF, STARTS = 4, 5, 6, 7, 8
VMEM_BYTES = 26 * 1024 * 1024


def nt(a, b):
    return lax.dot_general(a, b, (((1,), (1,)), ((), ())), preferred_element_type=jnp.float32)


def nn(a, b):
    return lax.dot_general(a, b, (((1,), (0,)), ((), ())), preferred_element_type=jnp.float32)


def layer_normalise(lines):
    center = lines - jnp.mean(lines, axis=-1, keepdims=True)
    spread = jnp.mean(center * center, axis=-1, keepdims=True)
    return center * lax.rsqrt(spread + 1e-05)


def pair_swapped(even_block, odd_block, axis):
    count = lax.axis_size(axis)
    got = []
    for first, block in ((0, even_block), (1, odd_block)):
        pairs = [(i, i + 1) for i in range(first, count - 1, 2)]
        got.append(lax.ppermute(block, axis, pairs + [(b, a) for a, b in pairs]))
    return got


def swapped(block, axis, bit):
    count = lax.axis_size(axis)
    return lax.ppermute(block, axis, [(i, i ^ bit) for i in range(count)])


def after(block, *others):
    return lax.optimization_barrier((block, *others))[0]


def bits_of(count):
    bits, bit = [], count // 2
    while bit:
        bits.append(bit)
        bit //= 2
    return bits


def marked_lanes(lines, hidden):
    first = jnp.where(hidden, INVALID, lines[:, :, :LANES])
    return jnp.concatenate([first, lines[:, :, LANES:]], axis=2)


def edge_kernel(place_ref, flags_hbm, x_hbm, mark_ref, even_ref, odd_ref, x_ref, *scratch):
    flags_ref, spread, sems = scratch
    rows, cols = flags_ref.shape
    flags_copy = pltpu.make_async_copy(flags_hbm, flags_ref, sems.at[0])
    x_copy = pltpu.make_async_copy(x_hbm, x_ref, sems.at[1])
    flags_copy.start()
    x_copy.start()
    flags_copy.wait()
    row_at = lax.broadcasted_iota(jnp.int32, (cols, cols), 0)
    diagonal = row_at == lax.broadcasted_iota(jnp.int32, (cols, cols), 1)
    for r in range(rows):
        hidden = jnp.where(flags_ref[r : r + 1, :] > 0, 0.0, INVALID)
        spread[r * cols : (r + 1) * cols, :] = jnp.where(diagonal, hidden, 0.0).astype(jnp.bfloat16)
    marks = nn(spread[...], jnp.ones((cols, LANES), jnp.bfloat16)).reshape(rows, cols, LANES)
    mark_ref[...] = marks.astype(jnp.bfloat16)
    x_copy.wait()
    first, last = [
        marked_lanes(x_ref[at].astype(jnp.float32), marks[at] > INVALID / 2)
        for at in (slice(0, RADIUS), slice(rows - RADIUS, rows))
    ]
    even = place_ref[EVEN_ROW] > 0
    even_ref[...] = jnp.where(even, last, first).astype(jnp.bfloat16)
    odd_ref[...] = jnp.where(even, first, last).astype(jnp.bfloat16)


def piece_kernel(place_ref, triple_hbm, mine_ref, last_ref, sems):
    start = pl.multiple_of(place_ref[STARTS], 16)
    last = triple_hbm.shape[0] - last_ref.shape[0]
    copies = [
        pltpu.make_async_copy(triple_hbm.at[pl.ds(start, mine_ref.shape[0]), :], mine_ref, sems.at[0]),
        pltpu.make_async_copy(triple_hbm.at[last:, :], last_ref, sems.at[1]),
    ]
    for copy in copies:
        copy.start()
    for copy in copies:
        copy.wait()


def strip_kernel(place_ref, x_ref, mark_ref, even_rows_ref, odd_rows_ref, carriers_ref, even_ref, odd_ref, carriers_s):
    per_row = carriers_ref.shape[1]
    carriers_s[...] = jnp.zeros_like(carriers_s)
    for i in range(carriers_ref.shape[0]):
        carriers_s[i * per_row : (i + 1) * per_row, :] = carriers_ref[i].astype(jnp.float32)
    for i in range(carriers_s.shape[0] // TILE):
        even_ref[odd_ref.shape[0] + i] = carriers_s[i * TILE : (i + 1) * TILE, :].astype(jnp.bfloat16)
    rows, cols, channels = x_ref.shape
    middle = rows // 2
    low = lax.broadcasted_iota(jnp.int32, (1, TILE, 1), 1) < RADIUS
    even_row, even_col = place_ref[EVEN_ROW] > 0, place_ref[EVEN_COL] > 0
    for lane in range(0, channels, LANES):
        lanes = slice(lane, lane + LANES)
        strips = []
        for columns, last in ((slice(0, TILE), False), (slice(cols - TILE, cols), True)):

            def own(part):
                lines = x_ref[part, columns, lanes].astype(jnp.float32)
                if lane == 0:
                    lines = jnp.where(mark_ref[part, columns, :].astype(jnp.float32) > INVALID / 2, INVALID, lines)
                return lines

            even_rows = even_rows_ref[:, columns, lanes].astype(jnp.float32)
            odd_rows = odd_rows_ref[:, columns, lanes].astype(jnp.float32)
            top, bottom = jnp.where(even_row, odd_rows, even_rows), jnp.where(even_row, even_rows, odd_rows)
            upper = jnp.concatenate([top, own(slice(0, middle))], axis=0)
            lower = jnp.concatenate([own(slice(middle, rows)), bottom], axis=0)
            if last:
                upper = jnp.roll(upper, RADIUS, axis=1)
            else:
                lower = jnp.roll(lower, RADIUS, axis=1)
            strips.append(jnp.where(low, upper, lower))
        first, last = strips
        even_ref[: odd_ref.shape[0], :, lanes] = jnp.where(even_col, last, first).astype(jnp.bfloat16)
        odd_ref[:, :, lanes] = jnp.where(even_col, first, last).astype(jnp.bfloat16)


def carrier_pair_kernel(own_ref, got_hbm, out_ref, got_s, pair_s, sem):
    per_row, here = own_ref.shape[1], own_ref.shape[0] * own_ref.shape[1]
    tiles = got_s.shape[0]
    copy = pltpu.make_async_copy(got_hbm.at[got_hbm.shape[0] - tiles :], got_s, sem)
    copy.start()
    for i in range(own_ref.shape[0]):
        pair_s[i * per_row : (i + 1) * per_row, :] = own_ref[i].astype(jnp.float32)
    copy.wait()
    pair_s[here:, :] = got_s[...].astype(jnp.float32).reshape(tiles * TILE, -1)[:here]
    out_ref[...] = pair_s[...].astype(jnp.bfloat16)


def pack_kernel(final_ref, *refs):
    parts, out_ref = refs[:-1], refs[-1]
    rows = final_ref.shape[0]
    out_ref[:rows, :] = final_ref[...]
    carriers = jnp.concatenate([part[...].astype(jnp.float32) for part in parts], axis=0)
    out_ref[rows:, :] = carriers.astype(jnp.bfloat16)


def own_kernel(x_ref, xq_ref):
    rows, cols, _ = x_ref.shape
    step = 4

    def own(i, _):
        at = pl.multiple_of(i * step, step)
        y = layer_normalise(x_ref[pl.ds(at, step)].astype(jnp.float32))
        for c in range(cols // TILE):
            piece = y[:, c * TILE : (c + 1) * TILE, :].reshape(step * TILE, -1)
            to = pl.multiple_of(c * rows * TILE + at * TILE, step * TILE)
            xq_ref[pl.ds(to, step * TILE), :] = piece.astype(jnp.bfloat16)
        return 0

    lax.fori_loop(0, rows // step, own, 0)


def columns_of(lines):
    return [lines[:, c : c + TILE, :] for c in range(0, lines.shape[1], TILE)]


def tile_of(xq_ref, column, rows, at, step):
    first = pl.multiple_of(column * rows * TILE + at * TILE, step * TILE)
    return xq_ref[pl.ds(first, step * TILE), :].astype(jnp.float32).reshape(step, TILE, -1)


def store_lines(ref, block, wide_rows, at, lines):
    size = lines.shape[0] * TILE
    to = block * wide_rows * TILE + at * TILE
    to = to if isinstance(to, int) else pl.multiple_of(to, size)
    ref[pl.ds(to, size), :] = lines.reshape(size, -1).astype(jnp.bfloat16)


def middle_kernel(place_ref, xq_ref, even_rows_ref, odd_rows_ref, mid_ref, top_s, bottom_s):
    cols = even_rows_ref.shape[1]
    rows, step = xq_ref.shape[0] // cols, 2
    wide_rows = rows + 2 * RADIUS
    flip = place_ref[EVEN_ROW] > 0
    for i in range(0, RADIUS, step):
        a, b = even_rows_ref[i : i + step].astype(jnp.float32), odd_rows_ref[i : i + step].astype(jnp.float32)
        top_s[i : i + step] = layer_normalise(jnp.where(flip, b, a))
        bottom_s[i : i + step] = layer_normalise(jnp.where(flip, a, b))
    low = lax.broadcasted_iota(jnp.int32, (1, TILE, 1), 1) < RADIUS

    def merge(at, blocks):
        moved = [jnp.roll(block, RADIUS, axis=1) for block in blocks]
        for c in range(1, len(blocks)):
            store_lines(mid_ref, c - 1, wide_rows, at, jnp.where(low, moved[c - 1], moved[c]))

    for i in range(0, RADIUS, step):
        merge(i, columns_of(top_s[i : i + step]))
        merge(RADIUS + rows + i, columns_of(bottom_s[i : i + step]))

    def middle(i, _):
        at = pl.multiple_of(i * step, step)
        merge(RADIUS + at, [tile_of(xq_ref, c, rows, at, step) for c in range(cols // TILE)])
        return 0

    lax.fori_loop(0, rows // step, middle, 0)


def outer_kernel(place_ref, xq_ref, mark_ref, even_rows_ref, odd_rows_ref, even_cols_ref, odd_cols_ref, outer_ref, hide_ref, *scratch):
    rows, cols, _ = mark_ref.shape
    wide_rows, wide_cols = rows + 2 * RADIUS, cols + 2 * RADIUS
    half = wide_rows // 2
    step = 2
    top_s, bottom_s, left_s, right_s, top_ref, bottom_ref, left_ref, right_ref, flag_s = scratch
    flip = place_ref[EVEN_ROW] > 0
    a, b = even_rows_ref[...].astype(jnp.float32), odd_rows_ref[...].astype(jnp.float32)
    for lines, out, flags in ((jnp.where(flip, b, a), top_s, top_ref), (jnp.where(flip, a, b), bottom_s, bottom_ref)):
        ends = jnp.concatenate([lines[:, :TILE, :], lines[:, cols - TILE :, :]], axis=1)
        out[...] = layer_normalise(ends)
        flags[...] = lines[:, :, :LANES]
    flip = place_ref[EVEN_COL] > 0
    size = 5
    for i in range(0, odd_cols_ref.shape[0], size):
        a, b = even_cols_ref[i : i + size].astype(jnp.float32), odd_cols_ref[i : i + size].astype(jnp.float32)
        for lines, out, flags in ((jnp.where(flip, b, a), left_s, left_ref), (jnp.where(flip, a, b), right_s, right_ref)):
            out[i : i + size] = layer_normalise(lines)
            flags[i : i + size] = lines[:, :, :LANES]
    low = lax.broadcasted_iota(jnp.int32, (1, TILE, 1), 1) < RADIUS

    def lines_of(ref):
        return ref.astype(jnp.float32)

    def merge(at, blocks, left, right, to_ref):
        moved = [left] + [jnp.roll(block, RADIUS, axis=1) for block in blocks] + [right]
        for c in range(len(blocks) + 1):
            store_lines(to_ref, c, wide_rows, at, jnp.where(low, moved[c], moved[c + 1]))

    def merge_ends(at, first, last, left, right):
        store_lines(outer_ref, 0, wide_rows, at, jnp.where(low, left, jnp.roll(first, RADIUS, axis=1)))
        store_lines(outer_ref, 1, wide_rows, at, jnp.where(low, jnp.roll(last, RADIUS, axis=1), right))

    def sides(at, upper, left_ref, right_ref, lanes):
        if upper:
            at = at - half
            left, right = jnp.roll(lines_of(left_ref[pl.ds(at, step), :, lanes]), RADIUS, axis=1), lines_of(
                right_ref[pl.ds(at, step), :, lanes]
            )
        else:
            left, right = lines_of(left_ref[pl.ds(at, step), :, lanes]), jnp.roll(
                lines_of(right_ref[pl.ds(at, step), :, lanes]), RADIUS, axis=1
            )
        return left, right

    every, few = slice(None), slice(0, LANES)

    def hide_if(border, lines):
        return jnp.where(place_ref[border] > 0, INVALID, lines)

    def mark_sides(at, upper):
        left, right = sides(at, upper, left_ref, right_ref, few)
        return hide_if(2, left), hide_if(3, right)

    def band(at, ref, ref_s, first, upper):
        merge_ends(at, *columns_of(ref_s[first : first + step]), *sides(at, upper, left_s, right_s, every))
        marks = hide_if(int(upper), ref[first : first + step])
        beside = [hide_if(int(upper), side) for side in mark_sides(at, upper)]
        merge(at, columns_of(marks), *beside, flag_s)

    for i in range(0, RADIUS, step):
        band(i, top_ref, top_s, i, False)
        band(RADIUS + rows + i, bottom_ref, bottom_s, i, True)

    def middle(i, upper):
        at = pl.multiple_of(i * step, step)
        own = at - RADIUS
        ends = [tile_of(xq_ref, c, rows, own, step) for c in (0, cols // TILE - 1)]
        merge_ends(at, *ends, *sides(at, upper, left_s, right_s, every))
        merge(at, columns_of(mark_ref[pl.ds(own, step)].astype(jnp.float32)), *mark_sides(at, upper), flag_s)
        return 0

    lax.fori_loop(RADIUS // step, half // step, lambda i, _: middle(i, False), 0)
    lax.fori_loop(half // step, (RADIUS + rows) // step, lambda i, _: middle(i, True), 0)

    first_lane = (lax.broadcasted_iota(jnp.int32, (8, LANES), 1) == 0).astype(jnp.bfloat16)
    spans = []
    for c in range(wide_cols // TILE):
        lines = flag_s[c * wide_rows * TILE : (c + 1) * wide_rows * TILE, :]
        spans.append(jnp.where(nt(first_lane, lines) > INVALID / 2, HIDDEN, 0.0))
    tall = rows // TILE
    for c in range(cols // TILE):
        for r in range(tall):
            at = slice(r * TILE * TILE, r * TILE * TILE + 2 * TILE * TILE)
            hide_ref[c * tall + r] = jnp.concatenate([spans[c][:, at], spans[c + 1][:, at]], axis=1)


def column_chunks(channels, half):
    at, end = half * 3 * channels // 2, (half + 1) * 3 * channels // 2
    chunks = []
    while at < end:
        width = min(GROUP - at % GROUP, end - at)
        chunks.append((at, at // channels, at % channels // GROUP, at % GROUP, width))
        at += width
    return chunks


def numbered_chunks(channels, half):
    number, chunks = 0, []
    for chunk in column_chunks(channels, half):
        chunks.append((number, *chunk))
        number += chunk[-1] == GROUP
    return chunks


def project_lines(source, w, parts, factor, put):
    size = source.shape[0] // parts
    for m in range(0, source.shape[0], size):
        y = nt(source[m : m + size, :], w)
        put(slice(m, m + size), (y if factor == 1 else y * factor).astype(jnp.bfloat16))


QUERY_FACTOR = HEAD_DIM ** (-0.5) * LOG2_E


def early_kernel(offsets, place_ref, *refs):
    triples, refs = refs[: len(offsets)], refs[len(offsets) :]
    xq_ref, mid_ref, whole_ref, part_ref, near, sems = refs
    channels = near.shape[1]
    triple_rows = near.shape[0] // len(offsets)
    copies = []
    for j, off in enumerate(offsets):
        to = pl.multiple_of(((place_ref[ROW] ^ off) % len(offsets)) * triple_rows, 16)
        copies.append(pltpu.make_async_copy(triples[j], near.at[pl.ds(to, triple_rows), :], sems.at[j]))
        copies[-1].start()
    for copy in copies:
        copy.wait()

    def run(half):
        for number, at, section, _, _, width in numbered_chunks(channels, half):
            w = near[at - half * near.shape[0] : at - half * near.shape[0] + width, :]

            def put(lines, value, number=number, width=width):
                if width == GROUP:
                    whole_ref[number, lines, :] = value
                else:
                    part_ref[lines, :] = value

            if section == 0:
                project_lines(xq_ref, w, 2, QUERY_FACTOR, put)
            else:
                project_lines(mid_ref, w, 2, 1, put)

    for half in range(2):
        pl.when(place_ref[HALF] == half)(functools.partial(run, half))


def project_rest(half, sections, channels, near_at, far_at, sources, take, put):
    xq_ref, mid_ref, outer_ref = sources
    edge, mid = outer_ref.shape[0] // 2, mid_ref.shape[0]
    for number, at, section, group, lane, width in numbered_chunks(channels, half):
        if section in sections and section > 0:
            w = near_at(at, width)
            for first, to in ((0, 0), (edge, edge + mid)):
                put(section, group, lane, width, slice(to, to + edge), nt(outer_ref[first : first + edge, :], w).astype(jnp.bfloat16))
    take()
    for at, section, group, lane, width in column_chunks(channels, 1 - half):
        if section not in sections:
            continue
        w = far_at(at, width)
        if section == 0:
            project_lines(xq_ref, w, 2, QUERY_FACTOR, functools.partial(put, section, group, lane, width))
            continue
        for first, to in ((0, 0), (edge, edge + mid)):
            put(section, group, lane, width, slice(to, to + edge), nt(outer_ref[first : first + edge, :], w).astype(jnp.bfloat16))

        def put_mid(lines, value, section=section, group=group, lane=lane, width=width):
            put(section, group, lane, width, slice(edge + lines.start, edge + lines.stop), value)

        project_lines(mid_ref, w, 2, 1, put_mid)


def late_kernel(pieces, triple_rows, place_ref, *refs):
    sources, refs = refs[: len(pieces)], refs[len(pieces) :]
    near, whole_ref, part_ref, xq_ref, mid_ref, outer_ref, q_s, k_s, wt, sems, early_sems, near_sem = refs
    channels = wt.shape[1]
    edge, mid = outer_ref.shape[0] // 2, mid_ref.shape[0]
    coming = []
    for j, (off, start) in enumerate(pieces):
        to = pl.multiple_of((place_ref[ROW] ^ off) * triple_rows + place_ref[STARTS + start], 16)
        coming.append(pltpu.make_async_copy(sources[j], wt.at[pl.ds(to, sources[j].shape[0]), :], sems.at[j]))
        coming[-1].start()
    to = pl.multiple_of(place_ref[HALF] * near.shape[0], 16)
    near_copy = pltpu.make_async_copy(near, wt.at[pl.ds(to, near.shape[0]), :], near_sem)
    near_copy.start()

    def put(section, group, lane, width, lines, value):
        if section == 0:
            q_s[group, lines, :] = value
        else:
            k_s[group, lines, lane : lane + width] = value

    def take():
        for copy in coming:
            copy.wait()

    def run(half):
        moves = []
        for number, at, section, group, lane, width in numbered_chunks(channels, half):
            if section == 0:
                move = (whole_ref.at[number], q_s.at[group])
            elif section == 1 and width == GROUP:
                move = (whole_ref.at[number, 0:mid, :], k_s.at[group, edge : edge + mid, :])
            elif section == 1:
                move = (part_ref, k_s.at[group, edge : edge + mid, lane : lane + width])
            else:
                continue
            moves.append(pltpu.make_async_copy(*move, early_sems.at[len(moves)]))
            moves[-1].start()
        base = half * near.shape[0]
        project_rest(
            half, (0, 1), channels, lambda at, width: near[at - base : at - base + width, :], lambda at, width: wt[at : at + width, :],
            (xq_ref, mid_ref, outer_ref), take, put,
        )
        for move in moves:
            move.wait()

    for half in range(2):
        pl.when(place_ref[HALF] == half)(functools.partial(run, half))
    near_copy.wait()


def value_kernel(place_ref, wt, whole_ref, mid_ref, outer_ref, v_s, early_sems):
    channels = wt.shape[1]
    edge, mid = outer_ref.shape[0] // 2, mid_ref.shape[0]

    def put(section, group, lane, width, lines, value):
        v_s[group, lines, lane : lane + width] = value

    def run(half):
        moves = []
        for number, at, section, group, lane, width in numbered_chunks(channels, half):
            if section == 2:
                target = v_s.at[group, edge : edge + mid, :]
                moves.append(pltpu.make_async_copy(whole_ref.at[number, 0:mid, :], target, early_sems.at[len(moves)]))
                moves[-1].start()
        weights = lambda at, width: wt[at : at + width, :]
        project_rest(half, (2,), channels, weights, weights, (None, mid_ref, outer_ref), lambda: None, put)
        for move in moves:
            move.wait()

    for half in range(2):
        pl.when(place_ref[HALF] == half)(functools.partial(run, half))


def carrier_kernel(offsets, place_ref, wt, *refs):
    shards = len(offsets)
    finals, refs = refs[:shards], refs[shards:]
    summary_ref, wo, kce, vc_s, carriers_s, sems = refs
    per_row = summary_ref.shape[1]
    channels = wt.shape[1]
    groups = channels // GROUP
    heads = channels // HEAD_DIM
    factor = HEAD_DIM ** (-0.5)
    carriers_here = vc_s.shape[0]
    final_rows = wo.shape[0] // shards
    copies = []
    for j, off in enumerate(offsets):
        to = pl.multiple_of((place_ref[ROW] ^ off) * final_rows, 16)
        copy = pltpu.make_async_copy(finals[j].at[0:final_rows, :], wo.at[pl.ds(to, final_rows), :], sems.at[j])
        copy.start()
        copies.append(copy)
    coming = []
    sent = carriers_s.shape[0] // shards
    for j in range(shards):
        source = finals[j].at[final_rows : final_rows + sent, :]
        copy = pltpu.make_async_copy(source, carriers_s.at[j * sent : (j + 1) * sent, :], sems.at[shards + j])
        copy.start()
        coming.append(copy)
    for copy in coming:
        copy.wait()
    carriers = carriers_s[...].astype(jnp.float32)
    own = carriers[:carriers_here]
    carriers = layer_normalise(carriers).astype(jnp.bfloat16)
    own_norm = layer_normalise(own).astype(jnp.bfloat16)
    qc = (nt(own_norm, wt[:channels, :]) * factor).astype(jnp.bfloat16).astype(jnp.float32)
    kc = nt(carriers, wt[channels : 2 * channels, :]).astype(jnp.bfloat16)
    vc = nt(carriers, wt[2 * channels :, :]).astype(jnp.bfloat16)
    head_of = lax.broadcasted_iota(jnp.int32, (1, channels), 1) // HEAD_DIM
    stacked = jnp.concatenate([jnp.where(head_of == h, qc, 0.0) for h in range(heads)], axis=0)
    e = jnp.exp(nt(stacked.astype(jnp.bfloat16), kc))
    weights = (e / jnp.sum(e, axis=-1, keepdims=True)).astype(jnp.bfloat16)
    o = nn(weights, vc)
    mix = jnp.zeros((carriers_here, channels), jnp.float32)
    for h in range(heads):
        mix = jnp.where(head_of == h, o[h * carriers_here : (h + 1) * carriers_here, :], mix)
    for copy in copies:
        copy.wait()
    renewed = own + nt(mix.astype(jnp.bfloat16), wo[...])
    for i in range(summary_ref.shape[0]):
        summary_ref[i] = renewed[i * per_row : (i + 1) * per_row, :].astype(jnp.bfloat16)
    fresh = nt(layer_normalise(renewed).astype(jnp.bfloat16), wt[channels:, :]).astype(jnp.bfloat16).astype(jnp.float32)
    vc_s[...] = fresh[:, channels:]
    same = (
        lax.broadcasted_iota(jnp.int32, (GROUP, GROUP), 0) // HEAD_DIM
        == lax.broadcasted_iota(jnp.int32, (GROUP, GROUP), 1) // HEAD_DIM
    )
    windows = kce.shape[0] // groups
    for w in range(windows):
        for g in range(groups):
            kce[w * groups + g] = jnp.where(same, fresh[w : w + 1, g * GROUP : (g + 1) * GROUP], 0.0).astype(jnp.bfloat16)


def attend_kernel(tall, broad, q_s, k_s, v_s, hide_ref, kce, vc_s, mix_s, pc_s, even_s, odd_s):
    groups, tiles = q_s.shape[0], hide_ref.shape[0]
    heads_in = GROUP // HEAD_DIM
    queries, span = TILE * TILE, 2 * TILE * TILE
    side = PATCH_SIDE // TILE
    wide = (tall + 1) * queries
    qi = lax.broadcasted_iota(jnp.int32, (queries, 2 * span), 0)
    ki = lax.broadcasted_iota(jnp.int32, (queries, 2 * span), 1)
    row_step = (ki % span) // TILE - qi // TILE
    col_step = (ki // span) * TILE + ki % TILE - qi % TILE
    seen = (row_step >= 0) & (row_step <= 2 * RADIUS) & (col_step >= 0) & (col_step <= 2 * RADIUS)
    band = jnp.where(seen, 0.0, HIDDEN)
    group_head = lax.broadcasted_iota(jnp.int32, (1, GROUP), 1) // HEAD_DIM
    only = [jnp.where(group_head == h, 1.0, 0.0).astype(jnp.bfloat16) for h in range(heads_in)]
    in_pair = LANES // HEAD_DIM
    pair_head = lax.broadcasted_iota(jnp.int32, (1, LANES), 1) // HEAD_DIM

    for c in range(broad):
        for w in range(tall // side):
            at = slice((c * tall + w * side) * queries, (c * tall + (w + 1) * side) * queries)
            window = w * (broad // side) + c // side
            for g in range(groups):
                pc_s[at, g * GROUP : (g + 1) * GROUP] = jnp.exp2(nt(q_s[g, at, :], kce[window * groups + g]))

    def keys_at(t):
        k0 = pl.multiple_of(t // tall * wide + t % tall * queries, queries)
        return k0, pl.multiple_of(k0 + wide, queries)

    def scores(t, ref):
        q_at = pl.multiple_of(t * queries, queries)
        k0, k1 = keys_at(t)
        for g in range(groups):
            q = q_s[g, pl.ds(q_at, queries), :]
            qq = jnp.concatenate([q * mask for mask in only], axis=0)
            k = jnp.concatenate([k_s[g, pl.ds(k0, span), :], k_s[g, pl.ds(k1, span), :]], axis=0)
            ref[g] = nt(qq, k)

    def finish(t, ref):
        q_at = pl.multiple_of(t * queries, queries)
        k0, k1 = keys_at(t)
        window = t % tall // side * (broad // side) + t // tall // side
        bias = band + hide_ref[t][0:1, :]
        for g in range(groups):
            p = jnp.exp2(ref[g].reshape(heads_in, queries, 2 * span) + bias[None])
            total = jnp.sum(p, axis=-1, keepdims=True)
            v = jnp.concatenate([v_s[g, pl.ds(k0, span), :], v_s[g, pl.ds(k1, span), :]], axis=0)
            o = nn(p.reshape(heads_in * queries, 2 * span).astype(jnp.bfloat16), v).reshape(heads_in, queries, GROUP)
            v_new = vc_s[pl.ds(window, 1), g * GROUP : (g + 1) * GROUP]
            for j in range(GROUP // LANES):
                lanes = slice(j * LANES, (j + 1) * LANES)
                at = slice(g * GROUP + j * LANES, g * GROUP + (j + 1) * LANES)
                kept, kept_total = o[j * in_pair, :, lanes], total[j * in_pair]
                for h in range(1, in_pair):
                    kept = jnp.where(pair_head == h, o[j * in_pair + h, :, lanes], kept)
                    kept_total = jnp.where(pair_head == h, total[j * in_pair + h], kept_total)
                new = pc_s[pl.ds(q_at, queries), at]
                mixed = (kept + new * v_new[:, lanes]) / (kept_total + new)
                mix_s[pl.ds(q_at, queries), at] = mixed.astype(jnp.bfloat16)

    scores(0, even_s)

    def two(i, _):
        t = 2 * i
        scores(t + 1, odd_s)
        finish(t, even_s)
        scores(jnp.minimum(t + 2, tiles - 1), even_s)
        finish(t + 1, odd_s)
        return 0

    lax.fori_loop(0, tiles // 2, two, 0)


def out_kernel(x_ref, mix_s, wo, out_hbm, out_ref, out_sems):
    rows, cols, channels = x_ref.shape
    going = []
    for pair in range(cols // (2 * TILE)):
        both = slice(2 * pair * TILE, 2 * (pair + 1) * TILE)
        for g in range(channels // GROUP):
            at = slice(g * GROUP, (g + 1) * GROUP)
            w = wo[at, :]
            y = nt(mix_s[2 * pair * rows * TILE : 2 * (pair + 1) * rows * TILE, :], w).reshape(2, rows, TILE, GROUP)
            y = jnp.concatenate([y[0], y[1]], axis=1) + x_ref[:, both, at].astype(jnp.float32)
            out_ref[pair, :, :, at] = y.astype(jnp.bfloat16)
        copy = pltpu.make_async_copy(out_ref.at[pair], out_hbm.at[:, both, :], out_sems.at[pair])
        copy.start()
        going.append(copy)
    for copy in going:
        copy.wait()


def local(grid_elements, summary_vectors, triple_projection, final_projection, genuine_flags):
    rows, cols, channels = grid_elements.shape
    wide_rows, wide_cols = rows + 2 * RADIUS, cols + 2 * RADIUS

    triple_t, final_t = triple_projection.T, final_projection.T
    vmem = pl.BlockSpec(memory_space=pltpu.VMEM)
    anywhere = pl.BlockSpec(memory_space=pl.ANY)
    scalars = pl.BlockSpec(memory_space=pltpu.SMEM)
    hbm = pl.BlockSpec(memory_space=pltpu.HBM)
    small = pltpu.CompilerParams(vmem_limit_bytes=8 * 1024 * 1024)
    row_strip = jax.ShapeDtypeStruct((RADIUS, cols, channels), jnp.bfloat16)
    col_strip = jax.ShapeDtypeStruct((wide_rows // 2, 2 * RADIUS, channels), jnp.bfloat16)

    row, col, img = lax.axis_size("row"), lax.axis_size("col"), lax.axis_size("img")
    row_at, col_at, img_at = lax.axis_index("row"), lax.axis_index("col"), lax.axis_index("img")
    row_bits = bits_of(row)
    far, rest = row_bits[0], row_bits[1:]
    piece_rows = triple_t.shape[0] // (1 + img) // 16 * 16
    relays = img if piece_rows else 0
    starts = [(img_at - k) % img for k in range(relays)] + [jnp.int32(relays)]
    place = [row_at == 0, row_at == row - 1, col_at == 0, col_at == col - 1, row_at % 2 == 0, col_at % 2 == 0, row_at, row_at // far]
    place = jnp.stack([jnp.asarray(p).astype(jnp.int32) for p in place + [start * piece_rows for start in starts]])

    mark, even_rows, odd_rows, x = pl.pallas_call(
        edge_kernel,
        out_shape=(
            pltpu.VMEM((rows, cols, LANES), jnp.bfloat16),
            pltpu.VMEM(row_strip.shape, jnp.bfloat16),
            pltpu.VMEM(row_strip.shape, jnp.bfloat16),
            pltpu.VMEM(grid_elements.shape, jnp.bfloat16),
        ),
        in_specs=[scalars, hbm, hbm],
        out_specs=(vmem,) * 4,
        scratch_shapes=[
            pltpu.VMEM((rows, cols), jnp.int32),
            pltpu.VMEM((rows * cols, cols), jnp.bfloat16),
            pltpu.SemaphoreType.DMA((2,)),
        ],
        compiler_params=small,
        cost_estimate=pl.CostEstimate(flops=1_000_000, bytes_accessed=1_000_000, transcendentals=0),
        name="edge_rows",
    )(place, *(pltpu.with_memory_space_constraint(a, pltpu.HBM) for a in (genuine_flags, grid_elements)))
    mine, last = pl.pallas_call(
        piece_kernel,
        out_shape=(
            pltpu.VMEM((max(piece_rows, 16), channels), jnp.bfloat16),
            pltpu.VMEM((triple_t.shape[0] - relays * piece_rows, channels), jnp.bfloat16),
        ),
        in_specs=[scalars, hbm],
        out_specs=(vmem, vmem),
        scratch_shapes=[pltpu.SemaphoreType.DMA((2,))],
        compiler_params=small,
        cost_estimate=pl.CostEstimate(flops=1_000_000, bytes_accessed=1_000_000, transcendentals=0),
        name="pieces",
    )(place, pltpu.with_memory_space_constraint(after(triple_t, even_rows), pltpu.HBM))
    xq = pl.pallas_call(
        own_kernel,
        out_shape=pltpu.VMEM((rows * cols, channels), jnp.bfloat16),
        in_specs=[vmem],
        out_specs=vmem,
        compiler_params=small,
        cost_estimate=pl.CostEstimate(flops=1_000_000, bytes_accessed=1_000_000, transcendentals=0),
        name="own_norm",
    )(x)
    even_rows, odd_rows = pair_swapped(even_rows, odd_rows, "row")

    far_pieces = []
    if relays:
        first = swapped(mine, "row", far)
    far_last = swapped(after(last, even_rows, odd_rows), "row", far)

    own_rows = summary_vectors.shape[0] * summary_vectors.shape[1]
    carrier_tiles = -(-own_rows // TILE)
    even_cols, odd_cols = pl.pallas_call(
        strip_kernel,
        out_shape=(
            pltpu.VMEM((col_strip.shape[0] + carrier_tiles, *col_strip.shape[1:]), jnp.bfloat16),
            pltpu.VMEM(col_strip.shape, jnp.bfloat16),
        ),
        in_specs=[scalars] + [vmem] * 5,
        out_specs=(vmem,) * 2,
        scratch_shapes=[pltpu.VMEM((carrier_tiles * TILE, channels), jnp.float32)],
        compiler_params=small,
        cost_estimate=pl.CostEstimate(flops=1_000_000, bytes_accessed=2_000_000, transcendentals=0),
        name="edge_columns",
    )(place, x, after(mark, xq), even_rows, odd_rows, summary_vectors)
    even_cols, odd_cols = pair_swapped(even_cols, odd_cols, "col")
    groups = channels // GROUP
    triples, offsets = [triple_t], [0]
    for bit in rest:
        triples = triples + [swapped(p, "row", bit) for p in triples]
        offsets = offsets + [o ^ bit for o in offsets]
    mid = pl.pallas_call(
        middle_kernel,
        out_shape=pltpu.VMEM(((wide_cols // TILE - 2) * wide_rows * TILE, channels), jnp.bfloat16),
        in_specs=[scalars] + [vmem] * 3,
        out_specs=vmem,
        scratch_shapes=[pltpu.VMEM(row_strip.shape, jnp.float32)] * 2,
        compiler_params=small,
        cost_estimate=pl.CostEstimate(flops=1_000_000, bytes_accessed=1_000_000, transcendentals=0),
        name="middle_blocks",
    )(place, xq, even_rows, odd_rows)
    whole, part, near = pl.pallas_call(
        functools.partial(early_kernel, offsets),
        out_shape=(
            pltpu.VMEM((3 * groups // 2, rows * cols, GROUP), jnp.bfloat16),
            pltpu.VMEM((mid.shape[0], GROUP // 2), jnp.bfloat16),
            pltpu.VMEM((3 * channels // 2, channels), jnp.bfloat16),
        ),
        in_specs=[scalars] + [anywhere] * len(triples) + [vmem] * 2,
        out_specs=(vmem,) * 3,
        scratch_shapes=[pltpu.SemaphoreType.DMA((len(triples),))],
        compiler_params=pltpu.CompilerParams(vmem_limit_bytes=16 * 1024 * 1024),
        cost_estimate=pl.CostEstimate(flops=1_000_000, bytes_accessed=1_000_000, transcendentals=0),
        name="project_early",
    )(place, *triples, xq, mid)

    carriers = pl.pallas_call(
        carrier_pair_kernel,
        out_shape=pltpu.VMEM((2 * own_rows, channels), jnp.bfloat16),
        in_specs=[vmem, anywhere],
        out_specs=vmem,
        scratch_shapes=[
            pltpu.VMEM((carrier_tiles, TILE, channels), jnp.bfloat16),
            pltpu.VMEM((2 * own_rows, channels), jnp.float32),
            pltpu.SemaphoreType.DMA,
        ],
        compiler_params=small,
        cost_estimate=pl.CostEstimate(flops=1_000, bytes_accessed=1_000, transcendentals=0),
        name="carrier_pair",
    )(summary_vectors, after(even_cols, near))
    parts = [carriers]
    for bit in bits_of(col)[:-1]:
        carriers = carriers if len(parts) == 1 else jnp.concatenate(parts, axis=0)
        got = swapped(carriers, "col", 2 * bit - 1)
        parts.append(got)
    if relays:
        first = after(first, even_cols, odd_cols, parts[0])
        others = [lax.ppermute(first, "img", [(i, (i + k) % img) for i in range(img)]) for k in range(1, relays)]
        far_pieces = [first] + others
    far_pieces.append(far_last)

    final_pack = pl.pallas_call(
        pack_kernel,
        out_shape=pltpu.VMEM((final_t.shape[0] + col * own_rows, channels), jnp.bfloat16),
        in_specs=[vmem] * (1 + len(parts)),
        out_specs=vmem,
        compiler_params=small,
        cost_estimate=pl.CostEstimate(flops=1_000, bytes_accessed=1_000, transcendentals=0),
        name="final_pack",
    )(final_t, *parts)
    finals = [final_pack]
    for bit in rest:
        finals = finals + [swapped(p, "row", bit) for p in finals]
    tiles = (rows // TILE) * (cols // TILE)
    keys = 4 * TILE * TILE
    outer, hide = pl.pallas_call(
        outer_kernel,
        out_shape=(
            pltpu.VMEM((2 * wide_rows * TILE, channels), jnp.bfloat16),
            pltpu.VMEM((tiles, 8, keys), jnp.float32),
        ),
        in_specs=[scalars] + [vmem] * 6,
        out_specs=(vmem,) * 2,
        scratch_shapes=[
            *[pltpu.VMEM((RADIUS, 2 * TILE, channels), jnp.float32)] * 2,
            *[pltpu.VMEM(col_strip.shape, jnp.float32)] * 2,
            *[pltpu.VMEM((*shape.shape[:2], LANES), jnp.float32) for shape in (row_strip, row_strip, col_strip, col_strip)],
            pltpu.VMEM((wide_rows * wide_cols, LANES), jnp.bfloat16),
        ],
        compiler_params=pltpu.CompilerParams(vmem_limit_bytes=12 * 1024 * 1024),
        cost_estimate=pl.CostEstimate(flops=10_000_000, bytes_accessed=6_000_000, transcendentals=1000),
        name="outer_blocks",
    )(place, after(xq, got), mark, even_rows, odd_rows, even_cols, odd_cols)

    far_final = swapped(final_pack, "row", far)

    far_offsets = [far]
    far_pieces = [[after(piece, outer)] for piece in far_pieces]
    for bit in rest:
        far_pieces = [same + [swapped(p, "row", bit) for p in same] for same in far_pieces]
        far_offsets = far_offsets + [o ^ bit for o in far_offsets]

    numbered = [(off, number) for number in range(len(far_pieces)) for off in far_offsets]
    sources = [piece for same in far_pieces for piece in same]
    q, k, wt = pl.pallas_call(
        functools.partial(late_kernel, numbered, triple_t.shape[0]),
        out_shape=(
            jax.ShapeDtypeStruct((groups, rows * cols, GROUP), jnp.bfloat16),
            jax.ShapeDtypeStruct((groups, wide_rows * wide_cols, GROUP), jnp.bfloat16),
            jax.ShapeDtypeStruct((3 * channels, channels), jnp.bfloat16),
        ),
        in_specs=[scalars] + [anywhere] * len(sources) + [vmem] * 6,
        out_specs=(vmem,) * 3,
        scratch_shapes=[
            pltpu.SemaphoreType.DMA((len(sources),)),
            pltpu.SemaphoreType.DMA((3 * groups,)),
            pltpu.SemaphoreType.DMA,
        ],
        compiler_params=pltpu.CompilerParams(vmem_limit_bytes=VMEM_BYTES),
        cost_estimate=pl.CostEstimate(flops=1_000_000, bytes_accessed=1_000_000, transcendentals=0),
        name="project_late",
    )(place, *sources, near, whole, part, xq, mid, outer)

    v = pl.pallas_call(
        value_kernel,
        out_shape=jax.ShapeDtypeStruct((groups, wide_rows * wide_cols, GROUP), jnp.bfloat16),
        in_specs=[scalars] + [vmem] * 4,
        out_specs=vmem,
        scratch_shapes=[pltpu.SemaphoreType.DMA((groups,))],
        compiler_params=pltpu.CompilerParams(vmem_limit_bytes=VMEM_BYTES),
        cost_estimate=pl.CostEstimate(flops=3_000_000_000, bytes_accessed=7_000_000, transcendentals=0),
        name="values",
    )(place, wt, whole, mid, outer)

    far_finals = [after(far_final, q)]
    for bit in rest:
        far_finals = far_finals + [swapped(p, "row", bit) for p in far_finals]
    finals, offsets = finals + far_finals, offsets + far_offsets
    carriers_here = carrier_tiles * TILE
    summary_result, wo, kce, vc = pl.pallas_call(
        functools.partial(carrier_kernel, offsets),
        out_shape=(
            jax.ShapeDtypeStruct(summary_vectors.shape, jnp.bfloat16),
            jax.ShapeDtypeStruct((channels, channels), jnp.bfloat16),
            jax.ShapeDtypeStruct((own_rows * groups, GROUP, GROUP), jnp.bfloat16),
            jax.ShapeDtypeStruct((carriers_here, channels), jnp.float32),
        ),
        in_specs=[scalars, vmem] + [anywhere] * len(finals),
        out_specs=(vmem,) * 4,
        scratch_shapes=[
            pltpu.VMEM((row * col * own_rows, channels), jnp.bfloat16),
            pltpu.SemaphoreType.DMA((2 * len(finals),)),
        ],
        compiler_params=pltpu.CompilerParams(vmem_limit_bytes=VMEM_BYTES),
        cost_estimate=pl.CostEstimate(flops=500_000_000, bytes_accessed=5_000_000, transcendentals=10_000),
        name="carriers",
    )(place, wt, *finals)

    scores = (groups, GROUP // HEAD_DIM * TILE * TILE, keys)
    mix = pl.pallas_call(
        functools.partial(attend_kernel, rows // TILE, cols // TILE),
        out_shape=jax.ShapeDtypeStruct((rows * cols, channels), jnp.bfloat16),
        in_specs=[vmem] * 6,
        out_specs=vmem,
        scratch_shapes=[
            pltpu.VMEM((rows * cols, channels), jnp.float32),
            pltpu.VMEM(scores, jnp.float32),
            pltpu.VMEM(scores, jnp.float32),
        ],
        compiler_params=pltpu.CompilerParams(vmem_limit_bytes=VMEM_BYTES),
        cost_estimate=pl.CostEstimate(flops=4_000_000_000, bytes_accessed=12_000_000, transcendentals=4_000_000),
        name="attend",
    )(q, k, v, hide, kce, vc)

    out = pl.pallas_call(
        out_kernel,
        out_shape=jax.ShapeDtypeStruct(grid_elements.shape, jnp.bfloat16),
        in_specs=[vmem] * 3,
        out_specs=anywhere,
        scratch_shapes=[
            pltpu.VMEM((cols // (2 * TILE), rows, 2 * TILE, channels), jnp.bfloat16),
            pltpu.SemaphoreType.DMA((cols // (2 * TILE),)),
        ],
        compiler_params=pltpu.CompilerParams(vmem_limit_bytes=VMEM_BYTES),
        cost_estimate=pl.CostEstimate(flops=1_200_000_000, bytes_accessed=6_000_000, transcendentals=0),
        name="out",
    )(x, mix, wo)
    return (out, summary_result)


def solution(mesh):
    placed = (
        P(("img", "row"), "col", None),
        P(("img", "row"), "col", None),
        P(None, "row"),
        P(None, "row"),
        P(("img", "row"), "col"),
    )
    return jax.shard_map(
        local,
        mesh=mesh,
        in_specs=placed,
        out_specs=(P(("img", "row"), "col", None), P(("img", "row"), "col", None)),
        check_vma=False,
    )
```

profile of v0, /device:TPU:0, one launch (start us, length us, event | category | flops | bytes accessed | tf_op | source)
XLA Modules:
  0.0 54.6 jit_solution(13845268864473274939)
XLA Ops:
  0.6 0.5 collective-permute-start.5
  1.1 0.1 stack.67.place_ref
  1.2 2.1 %edge_rows.1 = (bf16[32,32,128]{2,1,0:T(8,128)(2,1)S(1)}, bf16[4,32,768]{2,1,0:T(8,128)(2,1)S(1)}, bf16[4,32,768]{2,1,0:T(8,128)(2,1)S(1)}, bf16[32,32,768]{2,1,0:T(8,128)(2,1)S(1)}) custom-call(s32[11]{0:T(128)S(1)} %stack.67.place_ref, s32[32,32]{1,0:T(8,128)} %flags_hbm.1, bf16[32,32,768]{2,1,0:T(8,128)(2,1)} %x_hbm.1), custom_call_target="tpu_custom_call" | custom-call | flops 1000000 | bytes 1000000 | tf_op jit(solution)/shard_map/edge_rows/pallas_call | solution.py:639
  3.3 0.1 collective-permute-start.1
  3.5 0.7 %collective-permute-start.2 = (bf16[4,32,768]{2,1,0:T(8,128)(2,1)S(1)}, bf16[4,32,768]{2,1,0:T(8,128)(2,1)S(1)}, u32[]{:S(2)}, u32[]{:S(2)}) collective-permute-start(bf16[4,32,768]{2,1,0:T(8,128)(2,1)S(1)} %get-tuple-element.38), channel_id=1, source_target_pairs={{4,8},{8,4},{5,9},{9,5},{6,10},{10,6},{7,11},{11,7},{20,24},{24,20... | collective-permute-start | bytes 589832 | tf_op jit(solution)/shard_map/ppermute | solution.py:42
  4.1 1.6 %pieces.1 = (bf16[192,768]{1,0:T(8,128)(2,1)S(1)}, bf16[192,768]{1,0:T(8,128)(2,1)S(1)}) custom-call(s32[11]{0:T(128)S(1)} %stack.67.place_ref, bf16[576,768]{1,0:T(8,128)(2,1)} %bitcast.13), custom_call_target="tpu_custom_call" | custom-call | flops 1000000 | bytes 1000000 | tf_op jit(solution)/shard_map/pieces/pallas_call | solution.py:658
  5.8 4.3 %collective-permute-start = (bf16[192,768]{1,0:T(8,128)(2,1)S(1)}, bf16[192,768]{1,0:T(8,128)(2,1)S(1)}, u32[]{:S(2)}, u32[]{:S(2)}) collective-permute-start(bf16[192,768]{1,0:T(8,128)(2,1)S(1)} %get-tuple-element.35), channel_id=1, source_target_pairs={{0,8},{4,12},{8,0},{12,4},{1,9},{5,13},{9,1},{13,5},{2,10},{6,14},... | collective-permute-start | bytes 884744 | tf_op jit(solution)/shard_map/ppermute | solution.py:48
  10.0 1.8 %own_norm.1.xq_ref.refs_2_.refs_9_ = bf16[1024,768]{1,0:T(8,128)(2,1)S(1)} custom-call(bf16[32,32,768]{2,1,0:T(8,128)(2,1)S(1)} %get-tuple-element.32.x_ref), custom_call_target="tpu_custom_call" | custom-call | flops 1000000 | bytes 1000000 | tf_op jit(solution)/shard_map/own_norm/pallas_call | solution.py:671
  11.9 0.9 %edge_columns.1 = (bf16[21,8,768]{2,1,0:T(8,128)(2,1)S(1)}, bf16[20,8,768]{2,1,0:T(8,128)(2,1)S(1)}) custom-call(s32[11]{0:T(128)S(1)} %stack.67.place_ref, bf16[32,32,768]{2,1,0:T(8,128)(2,1)S(1)} %get-tuple-element.32.x_ref, bf16[32,32,128]{2,1,0:T(8,128)(2,1)S(1)} %get-tuple-element.37.mark_ref, ...), custom_call_target="tpu_custom_call" | custom-call | flops 1000000 | bytes 2000000 | tf_op jit(solution)/shard_map/edge_columns/pallas_call | solution.py:689
  12.7 1.8 %collective-permute-start.3 = (bf16[21,8,768]{2,1,0:T(8,128)(2,1)S(1)}, bf16[21,8,768]{2,1,0:T(8,128)(2,1)S(1)}, u32[]{:S(2)}, u32[]{:S(2)}) collective-permute-start(bf16[21,8,768]{2,1,0:T(8,128)(2,1)S(1)} %get-tuple-element.39), channel_id=1, source_target_pairs={{0,1},{2,3},{1,0},{3,2},{4,5},{6,7},{5,4},{7,6},{8,9},{10,11},{9,8... | collective-permute-start | bytes 774152 | tf_op jit(solution)/shard_map/ppermute | solution.py:42
  14.6 0.7 %collective-permute-start.4 = (bf16[20,8,768]{2,1,0:T(8,128)(2,1)S(1)}, bf16[20,8,768]{2,1,0:T(8,128)(2,1)S(1)}, u32[]{:S(2)}, u32[]{:S(2)}) collective-permute-start(bf16[20,8,768]{2,1,0:T(8,128)(2,1)S(1)} %get-tuple-element.40), channel_id=1, source_target_pairs={{1,2},{2,1},{5,6},{6,5},{9,10},{10,9},{13,14},{14,13},{17,18},{18,... | collective-permute-start | bytes 737288 | tf_op jit(solution)/shard_map/ppermute | solution.py:42
  15.2 1.4 %collective-permute-start.10 = (bf16[192,768]{1,0:T(8,128)(2,1)S(1)}, bf16[192,768]{1,0:T(8,128)(2,1)S(1)}, u32[]{:S(2)}, u32[]{:S(2)}) collective-permute-start(bf16[192,768]{1,0:T(8,128)(2,1)S(1)} %get-tuple-element.49), channel_id=1, source_target_pairs={{0,8},{4,12},{8,0},{12,4},{1,9},{5,13},{9,1},{13,5},{2,10},{6,14},... | collective-permute-start | bytes 884744 | tf_op jit(solution)/shard_map/ppermute | solution.py:48
  16.7 1.3 %middle_blocks.1.refs_3_.refs_10_.mid_ref = bf16[960,768]{1,0:T(8,128)(2,1)S(1)} custom-call(s32[11]{0:T(128)S(1)} %stack.67.place_ref, bf16[1024,768]{1,0:T(8,128)(2,1)S(1)} %own_norm.1.xq_ref.refs_2_.refs_9_, bf16[4,32,768]{2,1,0:T(8,128)(2,1)S(1)} %collective-permute-done.1.even_rows_ref, bf16[4,32,768]{2,1,0:T(8,128)(2,1)S(1)} %collective-permute-done.2.odd_rows_ref), custom_call_target="tpu_custom_call" | custom-call | flops 1000000 | bytes 1000000 | tf_op jit(solution)/shard_map/middle_blocks/pallas_call | solution.py:708
  18.0 3.1 %project_early.1 = (bf16[4,1024,256]{2,1,0:T(8,128)(2,1)S(1)}, bf16[960,128]{1,0:T(8,128)(2,1)S(1)}, bf16[1152,768]{1,0:T(8,128)(2,1)S(1)}) custom-call(s32[11]{0:T(128)S(1)} %stack.67.place_ref, bf16[576,768]{1,0:T(8,128)(2,1)S(1)} %bitcast.14, bf16[576,768]{1,0:T(8,128)(2,1)S(1)} %collective-permute-done.5.refs_1_, ...), custom_call_target="tpu_custom_call" | custom-call | flops 1000000 | bytes 1000000 | tf_op jit(solution)/shard_map/project_early/pallas_call | solution.py:718
  21.2 1.6 %collective-permute-start.8 = (bf16[192,768]{1,0:T(8,128)(2,1)S(1)}, bf16[192,768]{1,0:T(8,128)(2,1)S(1)}, u32[]{:S(2)}, u32[]{:S(2)}) collective-permute-start(bf16[192,768]{1,0:T(8,128)(2,1)S(1)} %collective-permute-done.refs_0_), channel_id=1, source_target_pairs={{0,16},{16,0},{1,17},{17,1},{2,18},{18,2},{3,19},{19,3},{4,20},{20... | collective-permute-start | bytes 884744 | tf_op jit(solution)/shard_map/ppermute | solution.py:754
  22.7 3.5 %collective-permute-start.6 = (bf16[8,768]{1,0:T(8,128)(2,1)S(1)}, bf16[8,768]{1,0:T(8,128)(2,1)S(1)}, u32[]{:S(2)}, u32[]{:S(2)}) collective-permute-start(bf16[8,768]{1,0:T(8,128)(2,1)S(1)} %carrier_pair.1.refs_0_), channel_id=1, source_target_pairs={{0,3},{1,2},{2,1},{3,0},{4,7},{5,6},{6,5},{7,4},{8,11},{9,10},{10,... | collective-permute-start | bytes 36872 | tf_op jit(solution)/shard_map/ppermute | solution.py:48
  26.3 2.0 %collective-permute-done.6.refs_1_ = bf16[8,768]{1,0:T(8,128)(2,1)S(1)} collective-permute-done((bf16[8,768]{1,0:T(8,128)(2,1)S(1)}, bf16[8,768]{1,0:T(8,128)(2,1)S(1)}, u32[]{:S(2)}, u32[]{:S(2)}) %collective-permute-start.6) | collective-permute-done | bytes 12320 | tf_op jit(solution)/shard_map/ppermute | solution.py:48
  28.3 1.7 %collective-permute-start.13 = (bf16[208,768]{1,0:T(8,128)(2,1)S(1)}, bf16[208,768]{1,0:T(8,128)(2,1)S(1)}, u32[]{:S(2)}, u32[]{:S(2)}) collective-permute-start(bf16[208,768]{1,0:T(8,128)(2,1)S(1)} %final_pack.1.refs_0_), channel_id=1, source_target_pairs={{0,8},{4,12},{8,0},{12,4},{1,9},{5,13},{9,1},{13,5},{2,10},{6,14},... | collective-permute-start | bytes 958472 | tf_op jit(solution)/shard_map/ppermute | solution.py:48
  30.0 1.8 %outer_blocks.1 = (bf16[640,768]{1,0:T(8,128)(2,1)S(1)}, f32[16,8,256]{2,1,0:T(8,128)S(1)}) custom-call(s32[11]{0:T(128)S(1)} %stack.67.place_ref, bf16[1024,768]{1,0:T(8,128)(2,1)S(1)} %own_norm.1.xq_ref.refs_2_.refs_9_, bf16[32,32,128]{2,1,0:T(8,128)(2,1)S(1)} %get-tuple-element.37.mark_ref, bf16[4,32,768]{2,1,0:T(8,128)(2,1)S(1)} %collective-permute-done.1.even_rows_ref, ...), custom_call_target="tpu_custom_call" | custom-call | flops 10000000 | bytes 6000000 | tf_op jit(solution)/shard_map/outer_blocks/pallas_call | solution.py:772
  31.7 0.1 collective-permute-start.7
  31.8 0.5 collective-permute-start.11
  32.3 0.1 collective-permute-start.9
  32.4 0.4 collective-permute-start.12
  32.8 0.6 %collective-permute-done.7.refs_1_ = bf16[192,768]{1,0:T(8,128)(2,1)S(1)} collective-permute-done((bf16[192,768]{1,0:T(8,128)(2,1)S(1)}, bf16[192,768]{1,0:T(8,128)(2,1)S(1)}, u32[]{:S(2)}, u32[]{:S(2)}) %collective-permute-start.7) | collective-permute-done | bytes 294944 | tf_op jit(solution)/shard_map/ppermute | solution.py:48
  33.4 0.4 collective-permute-done.11.refs_5_
  33.8 0.4 collective-permute-done.9.refs_3_
  34.2 4.1 %project_late.1 = (bf16[3,1024,256]{2,1,0:T(8,128)(2,1)S(1)}, bf16[3,1600,256]{2,1,0:T(8,128)(2,1)S(1)}, bf16[2304,768]{1,0:T(8,128)(2,1)S(1)}) custom-call(s32[11]{0:T(128)S(1)} %stack.67.place_ref, bf16[192,768]{1,0:T(8,128)(2,1)S(1)} %collective-permute-done.refs_0_, bf16[192,768]{1,0:T(8,128)(2,1)S(1)} %collective-permute-done.7.refs_1_, ...), custom_call_target="tpu_custom_call" | custom-call | flops 1000000 | bytes 1000000 | tf_op jit(solution)/shard_map/project_late/pallas_call | solution.py:801
  38.3 0.2 collective-permute-start.14
  38.5 2.9 %values.1.v_s = bf16[3,1600,256]{2,1,0:T(8,128)(2,1)S(1)} custom-call(s32[11]{0:T(128)S(1)} %stack.67.place_ref, bf16[2304,768]{1,0:T(8,128)(2,1)S(1)} %get-tuple-element.55.wt, bf16[4,1024,256]{2,1,0:T(8,128)(2,1)S(1)} %get-tuple-element.51.refs_7_.whole_ref, bf16[960,768]{1,0:T(8,128)(2,1)S(1)} %middle_blocks.1.refs_3_.refs_10_.mid_ref, ...), custom_call_target="tpu_custom_call" | custom-call | flops 3000000000 | bytes 7000000 | tf_op jit(solution)/shard_map/values/pallas_call | solution.py:820
  41.4 3.9 %carriers.1 = (bf16[2,2,768]{2,1,0:T(2,128)(2,1)}, bf16[768,768]{1,0:T(8,128)(2,1)S(1)}, bf16[12,256,256]{2,1,0:T(8,128)(2,1)S(1)}, f32[8,768]{1,0:T(8,128)S(1)}) custom-call(s32[11]{0:T(128)S(1)} %stack.67.place_ref, bf16[2304,768]{1,0:T(8,128)(2,1)S(1)} %get-tuple-element.55.wt, bf16[208,768]{1,0:T(8,128)(2,1)S(1)} %final_pack.1.refs_0_, ...), custom_call_target="tpu_custom_call" | custom-call | flops 500000000 | bytes 5000000 | tf_op jit(solution)/shard_map/carriers/pallas_call | solution.py:836
  45.3 6.8 %attend.1.mix_s = bf16[1024,768]{1,0:T(8,128)(2,1)S(1)} custom-call(bf16[3,1024,256]{2,1,0:T(8,128)(2,1)S(1)} %get-tuple-element.53.q_s, bf16[3,1600,256]{2,1,0:T(8,128)(2,1)S(1)} %get-tuple-element.54.k_s, bf16[3,1600,256]{2,1,0:T(8,128)(2,1)S(1)} %values.1.v_s, f32[16,8,256]{2,1,0:T(8,128)S(1)} %get-tuple-element.56.hide_ref, ...), custom_call_target="tpu_custom_call" | custom-call | flops 4000000000 | bytes 12000000 | tf_op jit(solution)/shard_map/attend/pallas_call | solution.py:856
  52.1 2.3 %out.1 = bf16[32,32,768]{2,1,0:T(8,128)(2,1)} custom-call(bf16[32,32,768]{2,1,0:T(8,128)(2,1)S(1)} %get-tuple-element.32.x_ref, bf16[1024,768]{1,0:T(8,128)(2,1)S(1)} %attend.1.mix_s, bf16[768,768]{1,0:T(8,128)(2,1)S(1)} %get-tuple-element.60.wo), custom_call_target="tpu_custom_call" | custom-call | flops 1200000000 | bytes 6000000 | tf_op jit(solution)/shard_map/out/pallas_call | solution.py:871
  (19 shorter events, 0.1 us)
Async XLA Ops:
  0.6 17.3 %collective-permute-start.5 = (bf16[576,768]{1,0:T(8,128)(2,1)}, bf16[576,768]{1,0:T(8,128)(2,1)S(1)}, u32[]{:S(2)}, u32[]{:S(2)}) collective-permute-start(bf16[576,768]{1,0:T(8,128)(2,1)} %bitcast.12), channel_id=1, source_target_pairs={{0,4},{4,0},{8,12},{12,8},{1,5},{5,1},{9,13},{13,9},{2,6},{6,2},{1... | collective-permute-start | bytes 2654216 | tf_op jit(solution)/shard_map/ppermute | solution.py:48
  3.3 8.5 %collective-permute-start.1 = (bf16[4,32,768]{2,1,0:T(8,128)(2,1)S(1)}, bf16[4,32,768]{2,1,0:T(8,128)(2,1)S(1)}, u32[]{:S(2)}, u32[]{:S(2)}) collective-permute-start(bf16[4,32,768]{2,1,0:T(8,128)(2,1)S(1)} %get-tuple-element.33), channel_id=1, source_target_pairs={{0,4},{8,12},{4,0},{12,8},{1,5},{9,13},{5,1},{13,9},{2,6},{10,14},... | collective-permute-start | bytes 589832 | tf_op jit(solution)/shard_map/ppermute | solution.py:42
  3.5 8.4 %collective-permute-start.2 = (bf16[4,32,768]{2,1,0:T(8,128)(2,1)S(1)}, bf16[4,32,768]{2,1,0:T(8,128)(2,1)S(1)}, u32[]{:S(2)}, u32[]{:S(2)}) collective-permute-start(bf16[4,32,768]{2,1,0:T(8,128)(2,1)S(1)} %get-tuple-element.38), channel_id=1, source_target_pairs={{4,8},{8,4},{5,9},{9,5},{6,10},{10,6},{7,11},{11,7},{20,24},{24,20... | collective-permute-start | bytes 589832 | tf_op jit(solution)/shard_map/ppermute | solution.py:42
  5.8 15.4 %collective-permute-start = (bf16[192,768]{1,0:T(8,128)(2,1)S(1)}, bf16[192,768]{1,0:T(8,128)(2,1)S(1)}, u32[]{:S(2)}, u32[]{:S(2)}) collective-permute-start(bf16[192,768]{1,0:T(8,128)(2,1)S(1)} %get-tuple-element.35), channel_id=1, source_target_pairs={{0,8},{4,12},{8,0},{12,4},{1,9},{5,13},{9,1},{13,5},{2,10},{6,14},... | collective-permute-start | bytes 884744 | tf_op jit(solution)/shard_map/ppermute | solution.py:48
  10.0 1.8 %copy-start.2 = (bf16[2,2,768]{2,1,0:T(2,128)(2,1)S(1)}, bf16[2,2,768]{2,1,0:T(2,128)(2,1)}, u32[]{:S(2)}) copy-start(bf16[2,2,768]{2,1,0:T(2,128)(2,1)} %own_ref.1) | copy-start | bytes 18436
  12.7 8.4 %collective-permute-start.3 = (bf16[21,8,768]{2,1,0:T(8,128)(2,1)S(1)}, bf16[21,8,768]{2,1,0:T(8,128)(2,1)S(1)}, u32[]{:S(2)}, u32[]{:S(2)}) collective-permute-start(bf16[21,8,768]{2,1,0:T(8,128)(2,1)S(1)} %get-tuple-element.39), channel_id=1, source_target_pairs={{0,1},{2,3},{1,0},{3,2},{4,5},{6,7},{5,4},{7,6},{8,9},{10,11},{9,8... | collective-permute-start | bytes 774152 | tf_op jit(solution)/shard_map/ppermute | solution.py:42
  14.6 6.6 %collective-permute-start.4 = (bf16[20,8,768]{2,1,0:T(8,128)(2,1)S(1)}, bf16[20,8,768]{2,1,0:T(8,128)(2,1)S(1)}, u32[]{:S(2)}, u32[]{:S(2)}) collective-permute-start(bf16[20,8,768]{2,1,0:T(8,128)(2,1)S(1)} %get-tuple-element.40), channel_id=1, source_target_pairs={{1,2},{2,1},{5,6},{6,5},{9,10},{10,9},{13,14},{14,13},{17,18},{18,... | collective-permute-start | bytes 737288 | tf_op jit(solution)/shard_map/ppermute | solution.py:42
  15.2 2.7 %copy-start = (bf16[768,576]{0,1:T(8,128)(2,1)S(1)}, bf16[768,576]{0,1:T(8,128)(2,1)}, u32[]{:S(2)}) copy-start(bf16[768,576]{0,1:T(8,128)(2,1)} %param.7) | copy-start | bytes 2654212
  15.2 16.6 %collective-permute-start.10 = (bf16[192,768]{1,0:T(8,128)(2,1)S(1)}, bf16[192,768]{1,0:T(8,128)(2,1)S(1)}, u32[]{:S(2)}, u32[]{:S(2)}) collective-permute-start(bf16[192,768]{1,0:T(8,128)(2,1)S(1)} %get-tuple-element.49), channel_id=1, source_target_pairs={{0,8},{4,12},{8,0},{12,4},{1,9},{5,13},{9,1},{13,5},{2,10},{6,14},... | collective-permute-start | bytes 884744 | tf_op jit(solution)/shard_map/ppermute | solution.py:48
  17.9 10.3 %copy-start.1 = (bf16[768,192]{0,1:T(8,128)(2,1)S(1)}, bf16[768,192]{0,1:T(8,128)(2,1)}, u32[]{:S(2)}) copy-start(bf16[768,192]{0,1:T(8,128)(2,1)} %param.8) | copy-start | bytes 884740
  21.2 11.1 %collective-permute-start.8 = (bf16[192,768]{1,0:T(8,128)(2,1)S(1)}, bf16[192,768]{1,0:T(8,128)(2,1)S(1)}, u32[]{:S(2)}, u32[]{:S(2)}) collective-permute-start(bf16[192,768]{1,0:T(8,128)(2,1)S(1)} %collective-permute-done.refs_0_), channel_id=1, source_target_pairs={{0,16},{16,0},{1,17},{17,1},{2,18},{18,2},{3,19},{19,3},{4,20},{20... | collective-permute-start | bytes 884744 | tf_op jit(solution)/shard_map/ppermute | solution.py:754
  22.7 5.5 %collective-permute-start.6 = (bf16[8,768]{1,0:T(8,128)(2,1)S(1)}, bf16[8,768]{1,0:T(8,128)(2,1)S(1)}, u32[]{:S(2)}, u32[]{:S(2)}) collective-permute-start(bf16[8,768]{1,0:T(8,128)(2,1)S(1)} %carrier_pair.1.refs_0_), channel_id=1, source_target_pairs={{0,3},{1,2},{2,1},{3,0},{4,7},{5,6},{6,5},{7,4},{8,11},{9,10},{10,... | collective-permute-start | bytes 36872 | tf_op jit(solution)/shard_map/ppermute | solution.py:48
  28.3 10.0 %collective-permute-start.13 = (bf16[208,768]{1,0:T(8,128)(2,1)S(1)}, bf16[208,768]{1,0:T(8,128)(2,1)S(1)}, u32[]{:S(2)}, u32[]{:S(2)}) collective-permute-start(bf16[208,768]{1,0:T(8,128)(2,1)S(1)} %final_pack.1.refs_0_), channel_id=1, source_target_pairs={{0,8},{4,12},{8,0},{12,4},{1,9},{5,13},{9,1},{13,5},{2,10},{6,14},... | collective-permute-start | bytes 958472 | tf_op jit(solution)/shard_map/ppermute | solution.py:48
  31.7 1.6 %collective-permute-start.7 = (bf16[192,768]{1,0:T(8,128)(2,1)S(1)}, bf16[192,768]{1,0:T(8,128)(2,1)S(1)}, u32[]{:S(2)}, u32[]{:S(2)}) collective-permute-start(bf16[192,768]{1,0:T(8,128)(2,1)S(1)} %collective-permute-done.refs_0_), channel_id=1, source_target_pairs={{0,4},{4,0},{8,12},{12,8},{1,5},{5,1},{9,13},{13,9},{2,6},{6,2},{1... | collective-permute-start | bytes 884744 | tf_op jit(solution)/shard_map/ppermute | solution.py:48
  31.8 2.0 %collective-permute-start.11 = (bf16[192,768]{1,0:T(8,128)(2,1)S(1)}, bf16[192,768]{1,0:T(8,128)(2,1)S(1)}, u32[]{:S(2)}, u32[]{:S(2)}) collective-permute-start(bf16[192,768]{1,0:T(8,128)(2,1)S(1)} %collective-permute-done.10.refs_4_), channel_id=1, source_target_pairs={{0,4},{4,0},{8,12},{12,8},{1,5},{5,1},{9,13},{13,9},{2,6},{6,2},{1... | collective-permute-start | bytes 884744 | tf_op jit(solution)/shard_map/ppermute | solution.py:48
  32.3 1.9 %collective-permute-start.9 = (bf16[192,768]{1,0:T(8,128)(2,1)S(1)}, bf16[192,768]{1,0:T(8,128)(2,1)S(1)}, u32[]{:S(2)}, u32[]{:S(2)}) collective-permute-start(bf16[192,768]{1,0:T(8,128)(2,1)S(1)} %collective-permute-done.8.refs_2_), channel_id=1, source_target_pairs={{0,4},{4,0},{8,12},{12,8},{1,5},{5,1},{9,13},{13,9},{2,6},{6,2},{1... | collective-permute-start | bytes 884744 | tf_op jit(solution)/shard_map/ppermute | solution.py:48
  32.4 9.0 %collective-permute-start.12 = (bf16[208,768]{1,0:T(8,128)(2,1)S(1)}, bf16[208,768]{1,0:T(8,128)(2,1)S(1)}, u32[]{:S(2)}, u32[]{:S(2)}) collective-permute-start(bf16[208,768]{1,0:T(8,128)(2,1)S(1)} %final_pack.1.refs_0_), channel_id=1, source_target_pairs={{0,4},{4,0},{8,12},{12,8},{1,5},{5,1},{9,13},{13,9},{2,6},{6,2},{1... | collective-permute-start | bytes 958472 | tf_op jit(solution)/shard_map/ppermute | solution.py:48
  38.3 3.1 %collective-permute-start.14 = (bf16[208,768]{1,0:T(8,128)(2,1)S(1)}, bf16[208,768]{1,0:T(8,128)(2,1)S(1)}, u32[]{:S(2)}, u32[]{:S(2)}) collective-permute-start(bf16[208,768]{1,0:T(8,128)(2,1)S(1)} %collective-permute-done.13.refs_2_), channel_id=1, source_target_pairs={{0,4},{4,0},{8,12},{12,8},{1,5},{5,1},{9,13},{13,9},{2,6},{6,2},{1... | collective-permute-start | bytes 958472 | tf_op jit(solution)/shard_map/ppermute | solution.py:48
where the time goes:
time: 55 us; the launch traced here: 54.6 us
  Pallas kernels  32.6 us (59%)
  starting transfers between devices  17.6 us (32%)
  waiting for transfers between devices  3.38 us (6%)
  between operations  1.02 us (2%)
    ppermute x10, starting transfers between devices, swapped(): return lax.ppermute(block, axis, [(i, i ^ bit) for i in range(count)])  12.7 us
    pallas_call x1, Pallas kernels, local(): pl.pallas_call(functools.partial(attend_kernel, rows // TILE, cols // TIL...  6.83 us
    pallas_call x1, Pallas kernels, local(): pl.pallas_call(functools.partial(late_kernel, numbered, triple_t.shape[0]...  4.07 us
    pallas_call x1, Pallas kernels, local(): pl.pallas_call(functools.partial(carrier_kernel, offsets), out_shape=(jax...  3.87 us
    ppermute x10, waiting for transfers between devices, swapped(): return lax.ppermute(block, axis, [(i, i ^ bit) for i in range(count)])  3.36 us
    ppermute x4, starting transfers between devices, pair_swapped(): got.append(lax.ppermute(block, axis, pairs + [(b, a) for a, b in pairs]))  3.29 us
    pallas_call x1, Pallas kernels, local(): pl.pallas_call(functools.partial(early_kernel, offsets), out_shape=(pltpu...  3.13 us
    pallas_call x1, Pallas kernels, local(): pl.pallas_call(value_kernel, out_shape=jax.ShapeDtypeStruct((groups, wide...  2.86 us
  transfers between devices with their start and end apart: 15, of which 4 were waited for; matrix products, arithmetic and copies ran while one was open for 0% of the time, Pallas kernels for 36%

commit v1 on v0

--- a/solution.py
+++ b/solution.py
@@ -337,16 +337,12 @@
 
 def early_kernel(offsets, place_ref, *refs):
     triples, refs = refs[: len(offsets)], refs[len(offsets) :]
-    xq_ref, mid_ref, whole_ref, part_ref, near, sems = refs
+    xq_ref, mid_ref, whole_ref, part_ref, near = refs
     channels = near.shape[1]
     triple_rows = near.shape[0] // len(offsets)
-    copies = []
     for j, off in enumerate(offsets):
         to = pl.multiple_of(((place_ref[ROW] ^ off) % len(offsets)) * triple_rows, 16)
-        copies.append(pltpu.make_async_copy(triples[j], near.at[pl.ds(to, triple_rows), :], sems.at[j]))
-        copies[-1].start()
-    for copy in copies:
-        copy.wait()
+        near[pl.ds(to, triple_rows), :] = triples[j][...]
 
     def run(half):
         for number, at, section, _, _, width in numbered_chunks(channels, half):
@@ -367,7 +363,7 @@
         pl.when(place_ref[HALF] == half)(functools.partial(run, half))
 
 
-def project_rest(half, sections, channels, near_at, far_at, sources, take, put):
+def project_rest(half, sections, channels, near_at, far_at, sources, put):
     xq_ref, mid_ref, outer_ref = sources
     edge, mid = outer_ref.shape[0] // 2, mid_ref.shape[0]
     for number, at, section, group, lane, width in numbered_chunks(channels, half):
@@ -375,7 +371,6 @@
             w = near_at(at, width)
             for first, to in ((0, 0), (edge, edge + mid)):
                 put(section, group, lane, width, slice(to, to + edge), nt(outer_ref[first : first + edge, :], w).astype(jnp.bfloat16))
-    take()
     for at, section, group, lane, width in column_chunks(channels, 1 - half):
         if section not in sections:
             continue
@@ -394,14 +389,12 @@
 
 def late_kernel(pieces, triple_rows, place_ref, *refs):
     sources, refs = refs[: len(pieces)], refs[len(pieces) :]
-    near, whole_ref, part_ref, xq_ref, mid_ref, outer_ref, q_s, k_s, wt, sems, early_sems, near_sem = refs
+    near, whole_ref, part_ref, xq_ref, mid_ref, outer_ref, q_s, k_s, wt, near_sem = refs
     channels = wt.shape[1]
     edge, mid = outer_ref.shape[0] // 2, mid_ref.shape[0]
-    coming = []
     for j, (off, start) in enumerate(pieces):
         to = pl.multiple_of((place_ref[ROW] ^ off) * triple_rows + place_ref[STARTS + start], 16)
-        coming.append(pltpu.make_async_copy(sources[j], wt.at[pl.ds(to, sources[j].shape[0]), :], sems.at[j]))
-        coming[-1].start()
+        wt[pl.ds(to, sources[j].shape[0]), :] = sources[j][...]
     to = pl.multiple_of(place_ref[HALF] * near.shape[0], 16)
     near_copy = pltpu.make_async_copy(near, wt.at[pl.ds(to, near.shape[0]), :], near_sem)
     near_copy.start()
@@ -412,37 +405,26 @@
         else:
             k_s[group, lines, lane : lane + width] = value
 
-    def take():
-        for copy in coming:
-            copy.wait()
-
     def run(half):
-        moves = []
         for number, at, section, group, lane, width in numbered_chunks(channels, half):
             if section == 0:
-                move = (whole_ref.at[number], q_s.at[group])
+                q_s[group] = whole_ref[number]
             elif section == 1 and width == GROUP:
-                move = (whole_ref.at[number, 0:mid, :], k_s.at[group, edge : edge + mid, :])
+                k_s[group, edge : edge + mid, :] = whole_ref[number, :mid, :]
             elif section == 1:
-                move = (part_ref, k_s.at[group, edge : edge + mid, lane : lane + width])
-            else:
-                continue
-            moves.append(pltpu.make_async_copy(*move, early_sems.at[len(moves)]))
-            moves[-1].start()
+                k_s[group, edge : edge + mid, lane : lane + width] = part_ref[...]
         base = half * near.shape[0]
         project_rest(
             half, (0, 1), channels, lambda at, width: near[at - base : at - base + width, :], lambda at, width: wt[at : at + width, :],
-            (xq_ref, mid_ref, outer_ref), take, put,
+            (xq_ref, mid_ref, outer_ref), put,
         )
-        for move in moves:
-            move.wait()
 
     for half in range(2):
         pl.when(place_ref[HALF] == half)(functools.partial(run, half))
     near_copy.wait()
 
 
-def value_kernel(place_ref, wt, whole_ref, mid_ref, outer_ref, v_s, early_sems):
+def value_kernel(place_ref, wt, whole_ref, mid_ref, outer_ref, v_s):
     channels = wt.shape[1]
     edge, mid = outer_ref.shape[0] // 2, mid_ref.shape[0]
 
@@ -450,16 +432,11 @@
         v_s[group, lines, lane : lane + width] = value
 
     def run(half):
-        moves = []
         for number, at, section, group, lane, width in numbered_chunks(channels, half):
             if section == 2:
-                target = v_s.at[group, edge : edge + mid, :]
-                moves.append(pltpu.make_async_copy(whole_ref.at[number, 0:mid, :], target, early_sems.at[len(moves)]))
-                moves[-1].start()
+                v_s[group, edge : edge + mid, :] = whole_ref[number, :mid, :]
         weights = lambda at, width: wt[at : at + width, :]
-        project_rest(half, (2,), channels, weights, weights, (None, mid_ref, outer_ref), lambda: None, put)
-        for move in moves:
-            move.wait()
+        project_rest(half, (2,), channels, weights, weights, (None, mid_ref, outer_ref), put)
 
     for half in range(2):
         pl.when(place_ref[HALF] == half)(functools.partial(run, half))
@@ -468,7 +445,7 @@
 def carrier_kernel(offsets, place_ref, wt, *refs):
     shards = len(offsets)
     finals, refs = refs[:shards], refs[shards:]
-    summary_ref, wo, kce, vc_s, carriers_s, sems = refs
+    summary_ref, wo, kce, vc_s = refs
     per_row = summary_ref.shape[1]
     channels = wt.shape[1]
     groups = channels // GROUP
@@ -476,22 +453,10 @@
     factor = HEAD_DIM ** (-0.5)
     carriers_here = vc_s.shape[0]
     final_rows = wo.shape[0] // shards
-    copies = []
     for j, off in enumerate(offsets):
         to = pl.multiple_of((place_ref[ROW] ^ off) * final_rows, 16)
-        copy = pltpu.make_async_copy(finals[j].at[0:final_rows, :], wo.at[pl.ds(to, final_rows), :], sems.at[j])
-        copy.start()
-        copies.append(copy)
-    coming = []
-    sent = carriers_s.shape[0] // shards
-    for j in range(shards):
-        source = finals[j].at[final_rows : final_rows + sent, :]
-        copy = pltpu.make_async_copy(source, carriers_s.at[j * sent : (j + 1) * sent, :], sems.at[shards + j])
-        copy.start()
-        coming.append(copy)
-    for copy in coming:
-        copy.wait()
-    carriers = carriers_s[...].astype(jnp.float32)
+        wo[pl.ds(to, final_rows), :] = finals[j][:final_rows, :]
+    carriers = jnp.concatenate([final[final_rows:, :].astype(jnp.float32) for final in finals], axis=0)
     own = carriers[:carriers_here]
     carriers = layer_normalise(carriers).astype(jnp.bfloat16)
     own_norm = layer_normalise(own).astype(jnp.bfloat16)
@@ -506,8 +471,6 @@
     mix = jnp.zeros((carriers_here, channels), jnp.float32)
     for h in range(heads):
         mix = jnp.where(head_of == h, o[h * carriers_here : (h + 1) * carriers_here, :], mix)
-    for copy in copies:
-        copy.wait()
     renewed = own + nt(mix.astype(jnp.bfloat16), wo[...])
     for i in range(summary_ref.shape[0]):
         summary_ref[i] = renewed[i * per_row : (i + 1) * per_row, :].astype(jnp.bfloat16)
@@ -630,7 +593,7 @@
     row_at, col_at, img_at = lax.axis_index("row"), lax.axis_index("col"), lax.axis_index("img")
     row_bits = bits_of(row)
     far, rest = row_bits[0], row_bits[1:]
-    piece_rows = triple_t.shape[0] // (1 + img) // 16 * 16
+    piece_rows = triple_t.shape[0] * 5 // (8 * img) // 16 * 16
     relays = img if piece_rows else 0
     starts = [(img_at - k) % img for k in range(relays)] + [jnp.int32(relays)]
     place = [row_at == 0, row_at == row - 1, col_at == 0, col_at == col - 1, row_at % 2 == 0, col_at % 2 == 0, row_at, row_at // far]
@@ -722,9 +685,8 @@
             pltpu.VMEM((mid.shape[0], GROUP // 2), jnp.bfloat16),
             pltpu.VMEM((3 * channels // 2, channels), jnp.bfloat16),
         ),
-        in_specs=[scalars] + [anywhere] * len(triples) + [vmem] * 2,
+        in_specs=[scalars] + [vmem] * (len(triples) + 2),
         out_specs=(vmem,) * 3,
-        scratch_shapes=[pltpu.SemaphoreType.DMA((len(triples),))],
         compiler_params=pltpu.CompilerParams(vmem_limit_bytes=16 * 1024 * 1024),
         cost_estimate=pl.CostEstimate(flops=1_000_000, bytes_accessed=1_000_000, transcendentals=0),
         name="project_early",
@@ -755,18 +717,6 @@
         far_pieces = [first] + others
     far_pieces.append(far_last)
 
-    final_pack = pl.pallas_call(
-        pack_kernel,
-        out_shape=pltpu.VMEM((final_t.shape[0] + col * own_rows, channels), jnp.bfloat16),
-        in_specs=[vmem] * (1 + len(parts)),
-        out_specs=vmem,
-        compiler_params=small,
-        cost_estimate=pl.CostEstimate(flops=1_000, bytes_accessed=1_000, transcendentals=0),
-        name="final_pack",
-    )(final_t, *parts)
-    finals = [final_pack]
-    for bit in rest:
-        finals = finals + [swapped(p, "row", bit) for p in finals]
     tiles = (rows // TILE) * (cols // TILE)
     keys = 4 * TILE * TILE
     outer, hide = pl.pallas_call(
@@ -786,12 +736,25 @@
         compiler_params=pltpu.CompilerParams(vmem_limit_bytes=12 * 1024 * 1024),
         cost_estimate=pl.CostEstimate(flops=10_000_000, bytes_accessed=6_000_000, transcendentals=1000),
         name="outer_blocks",
-    )(place, after(xq, got), mark, even_rows, odd_rows, even_cols, odd_cols)
+    )(place, xq, mark, even_rows, odd_rows, even_cols, odd_cols)
+
+    final_pack = pl.pallas_call(
+        pack_kernel,
+        out_shape=pltpu.VMEM((final_t.shape[0] + col * own_rows, channels), jnp.bfloat16),
+        in_specs=[vmem] * (1 + len(parts)),
+        out_specs=vmem,
+        compiler_params=small,
+        cost_estimate=pl.CostEstimate(flops=1_000, bytes_accessed=1_000, transcendentals=0),
+        name="final_pack",
+    )(final_t, *parts[:-1], after(parts[-1], outer))
+    finals = [final_pack]
+    for bit in rest:
+        finals = finals + [swapped(p, "row", bit) for p in finals]
 
     far_final = swapped(final_pack, "row", far)
 
     far_offsets = [far]
-    far_pieces = [[after(piece, outer)] for piece in far_pieces]
+    far_pieces = [[after(piece, outer, got)] for piece in far_pieces]
     for bit in rest:
         far_pieces = [same + [swapped(p, "row", bit) for p in same] for same in far_pieces]
         far_offsets = far_offsets + [o ^ bit for o in far_offsets]
@@ -805,13 +768,9 @@
             jax.ShapeDtypeStruct((groups, wide_rows * wide_cols, GROUP), jnp.bfloat16),
             jax.ShapeDtypeStruct((3 * channels, channels), jnp.bfloat16),
         ),
-        in_specs=[scalars] + [anywhere] * len(sources) + [vmem] * 6,
+        in_specs=[scalars] + [vmem] * (len(sources) + 6),
         out_specs=(vmem,) * 3,
-        scratch_shapes=[
-            pltpu.SemaphoreType.DMA((len(sources),)),
-            pltpu.SemaphoreType.DMA((3 * groups,)),
-            pltpu.SemaphoreType.DMA,
-        ],
+        scratch_shapes=[pltpu.SemaphoreType.DMA],
         compiler_params=pltpu.CompilerParams(vmem_limit_bytes=VMEM_BYTES),
         cost_estimate=pl.CostEstimate(flops=1_000_000, bytes_accessed=1_000_000, transcendentals=0),
         name="project_late",
@@ -822,7 +781,6 @@
         out_shape=jax.ShapeDtypeStruct((groups, wide_rows * wide_cols, GROUP), jnp.bfloat16),
         in_specs=[scalars] + [vmem] * 4,
         out_specs=vmem,
-        scratch_shapes=[pltpu.SemaphoreType.DMA((groups,))],
         compiler_params=pltpu.CompilerParams(vmem_limit_bytes=VMEM_BYTES),
         cost_estimate=pl.CostEstimate(flops=3_000_000_000, bytes_accessed=7_000_000, transcendentals=0),
         name="values",
@@ -841,12 +799,8 @@
             jax.ShapeDtypeStruct((own_rows * groups, GROUP, GROUP), jnp.bfloat16),
             jax.ShapeDtypeStruct((carriers_here, channels), jnp.float32),
         ),
-        in_specs=[scalars, vmem] + [anywhere] * len(finals),
+        in_specs=[scalars] + [vmem] * (1 + len(finals)),
         out_specs=(vmem,) * 4,
-        scratch_shapes=[
-            pltpu.VMEM((row * col * own_rows, channels), jnp.bfloat16),
-            pltpu.SemaphoreType.DMA((2 * len(finals),)),
-        ],
         compiler_params=pltpu.CompilerParams(vmem_limit_bytes=VMEM_BYTES),
         cost_estimate=pl.CostEstimate(flops=500_000_000, bytes_accessed=5_000_000, transcendentals=10_000),
         name="carriers",

time: 55 us -> 54.2 us (0.985)
  Pallas kernels: 32.6 us -> 30.8 us
  waiting for transfers between devices: 3.38 us -> 4.7 us
    ppermute x10, waiting for transfers between devices: 3.36 us -> 4.45 us  [swapped(): return lax.ppermute(block, axis, [(i, i ^ bit) for i in range(count)])]
    pallas_call x1, Pallas kernels: 4.07 us -> 3.18 us  [local(): pl.pallas_call(functools.partial(late_kernel, numbered, triple_t.shape[0]...]
    pallas_call x1, Pallas kernels: 3.87 us -> 3.23 us  [local(): pl.pallas_call(functools.partial(carrier_kernel, offsets), out_shape=(jax...]
  transfers between devices with their start and end apart: 15 -> 15, of which waited for: 4 -> 5; matrix products, arithmetic and copies ran while one was open for 0% -> 0% of each run, Pallas kernels for 36% -> 34%
where the time goes in v1:
time: 54.2 us; the launch traced here: 53.7 us
  Pallas kernels  30.8 us (57%)
  starting transfers between devices  17.1 us (32%)
  waiting for transfers between devices  4.7 us (9%)
  between operations  0.99 us (2%)
    ppermute x10, starting transfers between devices, swapped(): return lax.ppermute(block, axis, [(i, i ^ bit) for i in range(count)])  12.3 us
    pallas_call x1, Pallas kernels, local(): pl.pallas_call(functools.partial(attend_kernel, rows // TILE, cols // TIL...  6.85 us
    ppermute x10, waiting for transfers between devices, swapped(): return lax.ppermute(block, axis, [(i, i ^ bit) for i in range(count)])  4.45 us
    ppermute x4, starting transfers between devices, pair_swapped(): got.append(lax.ppermute(block, axis, pairs + [(b, a) for a, b in pairs]))  3.29 us
    pallas_call x1, Pallas kernels, local(): pl.pallas_call(functools.partial(carrier_kernel, offsets), out_shape=(jax...  3.23 us
    pallas_call x1, Pallas kernels, local(): pl.pallas_call(functools.partial(late_kernel, numbered, triple_t.shape[0]...  3.18 us
    pallas_call x1, Pallas kernels, local(): pl.pallas_call(functools.partial(early_kernel, offsets), out_shape=(pltpu...  2.85 us
    pallas_call x1, Pallas kernels, local(): pl.pallas_call(value_kernel, out_shape=jax.ShapeDtypeStruct((groups, wide...  2.84 us
  transfers between devices with their start and end apart: 15, of which 5 were waited for; matrix products, arithmetic and copies ran while one was open for 0% of the time, Pallas kernels for 34%

profile of v1, /device:TPU:0, one launch (start us, length us, event | category | flops | bytes accessed | tf_op | source)
XLA Modules:
  0.0 53.7 jit_solution(16399168194675725913)
XLA Ops:
  0.6 0.5 collective-permute-start.5
  1.1 0.1 stack.67.place_ref
  1.2 2.1 %edge_rows.1 = (bf16[32,32,128]{2,1,0:T(8,128)(2,1)S(1)}, bf16[4,32,768]{2,1,0:T(8,128)(2,1)S(1)}, bf16[4,32,768]{2,1,0:T(8,128)(2,1)S(1)}, bf16[32,32,768]{2,1,0:T(8,128)(2,1)S(1)}) custom-call(s32[11]{0:T(128)S(1)} %stack.67.place_ref, s32[32,32]{1,0:T(8,128)} %flags_hbm.1, bf16[32,32,768]{2,1,0:T(8,128)(2,1)} %x_hbm.1), custom_call_target="tpu_custom_call" | custom-call | flops 1000000 | bytes 1000000 | tf_op jit(solution)/shard_map/edge_rows/pallas_call | solution.py:602
  3.3 0.1 collective-permute-start.1
  3.5 0.7 %collective-permute-start.2 = (bf16[4,32,768]{2,1,0:T(8,128)(2,1)S(1)}, bf16[4,32,768]{2,1,0:T(8,128)(2,1)S(1)}, u32[]{:S(2)}, u32[]{:S(2)}) collective-permute-start(bf16[4,32,768]{2,1,0:T(8,128)(2,1)S(1)} %get-tuple-element.38), channel_id=1, source_target_pairs={{4,8},{8,4},{5,9},{9,5},{6,10},{10,6},{7,11},{11,7},{20,24},{24,20... | collective-permute-start | bytes 589832 | tf_op jit(solution)/shard_map/ppermute | solution.py:42
  4.1 1.6 %pieces.1 = (bf16[176,768]{1,0:T(8,128)(2,1)S(1)}, bf16[224,768]{1,0:T(8,128)(2,1)S(1)}) custom-call(s32[11]{0:T(128)S(1)} %stack.67.place_ref, bf16[576,768]{1,0:T(8,128)(2,1)} %bitcast.13), custom_call_target="tpu_custom_call" | custom-call | flops 1000000 | bytes 1000000 | tf_op jit(solution)/shard_map/pieces/pallas_call | solution.py:621
  5.8 4.3 %collective-permute-start = (bf16[176,768]{1,0:T(8,128)(2,1)S(1)}, bf16[176,768]{1,0:T(8,128)(2,1)S(1)}, u32[]{:S(2)}, u32[]{:S(2)}) collective-permute-start(bf16[176,768]{1,0:T(8,128)(2,1)S(1)} %get-tuple-element.35), channel_id=1, source_target_pairs={{0,8},{4,12},{8,0},{12,4},{1,9},{5,13},{9,1},{13,5},{2,10},{6,14},... | collective-permute-start | bytes 811016 | tf_op jit(solution)/shard_map/ppermute | solution.py:48
  10.0 1.8 %own_norm.1.xq_ref.refs_2_.refs_9_ = bf16[1024,768]{1,0:T(8,128)(2,1)S(1)} custom-call(bf16[32,32,768]{2,1,0:T(8,128)(2,1)S(1)} %get-tuple-element.32.x_ref), custom_call_target="tpu_custom_call" | custom-call | flops 1000000 | bytes 1000000 | tf_op jit(solution)/shard_map/own_norm/pallas_call | solution.py:634
  11.9 0.9 %edge_columns.1 = (bf16[21,8,768]{2,1,0:T(8,128)(2,1)S(1)}, bf16[20,8,768]{2,1,0:T(8,128)(2,1)S(1)}) custom-call(s32[11]{0:T(128)S(1)} %stack.67.place_ref, bf16[32,32,768]{2,1,0:T(8,128)(2,1)S(1)} %get-tuple-element.32.x_ref, bf16[32,32,128]{2,1,0:T(8,128)(2,1)S(1)} %get-tuple-element.37.mark_ref, ...), custom_call_target="tpu_custom_call" | custom-call | flops 1000000 | bytes 2000000 | tf_op jit(solution)/shard_map/edge_columns/pallas_call | solution.py:652
  12.8 1.8 %collective-permute-start.3 = (bf16[21,8,768]{2,1,0:T(8,128)(2,1)S(1)}, bf16[21,8,768]{2,1,0:T(8,128)(2,1)S(1)}, u32[]{:S(2)}, u32[]{:S(2)}) collective-permute-start(bf16[21,8,768]{2,1,0:T(8,128)(2,1)S(1)} %get-tuple-element.39), channel_id=1, source_target_pairs={{0,1},{2,3},{1,0},{3,2},{4,5},{6,7},{5,4},{7,6},{8,9},{10,11},{9,8... | collective-permute-start | bytes 774152 | tf_op jit(solution)/shard_map/ppermute | solution.py:42
  14.6 0.7 %collective-permute-start.4 = (bf16[20,8,768]{2,1,0:T(8,128)(2,1)S(1)}, bf16[20,8,768]{2,1,0:T(8,128)(2,1)S(1)}, u32[]{:S(2)}, u32[]{:S(2)}) collective-permute-start(bf16[20,8,768]{2,1,0:T(8,128)(2,1)S(1)} %get-tuple-element.40), channel_id=1, source_target_pairs={{1,2},{2,1},{5,6},{6,5},{9,10},{10,9},{13,14},{14,13},{17,18},{18,... | collective-permute-start | bytes 737288 | tf_op jit(solution)/shard_map/ppermute | solution.py:42
  15.2 0.0 copy-start
  15.3 1.4 %collective-permute-start.10 = (bf16[224,768]{1,0:T(8,128)(2,1)S(1)}, bf16[224,768]{1,0:T(8,128)(2,1)S(1)}, u32[]{:S(2)}, u32[]{:S(2)}) collective-permute-start(bf16[224,768]{1,0:T(8,128)(2,1)S(1)} %get-tuple-element.48), channel_id=1, source_target_pairs={{0,8},{4,12},{8,0},{12,4},{1,9},{5,13},{9,1},{13,5},{2,10},{6,14},... | collective-permute-start | bytes 1032200 | tf_op jit(solution)/shard_map/ppermute | solution.py:48
  16.7 1.3 %middle_blocks.1.refs_3_.refs_10_.mid_ref = bf16[960,768]{1,0:T(8,128)(2,1)S(1)} custom-call(s32[11]{0:T(128)S(1)} %stack.67.place_ref, bf16[1024,768]{1,0:T(8,128)(2,1)S(1)} %own_norm.1.xq_ref.refs_2_.refs_9_, bf16[4,32,768]{2,1,0:T(8,128)(2,1)S(1)} %collective-permute-done.1.even_rows_ref, bf16[4,32,768]{2,1,0:T(8,128)(2,1)S(1)} %collective-permute-done.2.odd_rows_ref), custom_call_target="tpu_custom_call" | custom-call | flops 1000000 | bytes 1000000 | tf_op jit(solution)/shard_map/middle_blocks/pallas_call | solution.py:671
  18.0 2.9 %project_early.1 = (bf16[4,1024,256]{2,1,0:T(8,128)(2,1)S(1)}, bf16[960,128]{1,0:T(8,128)(2,1)S(1)}, bf16[1152,768]{1,0:T(8,128)(2,1)S(1)}) custom-call(s32[11]{0:T(128)S(1)} %stack.67.place_ref, bf16[576,768]{1,0:T(8,128)(2,1)S(1)} %bitcast.14, bf16[576,768]{1,0:T(8,128)(2,1)S(1)} %collective-permute-done.5.refs_1_, ...), custom_call_target="tpu_custom_call" | custom-call | flops 1000000 | bytes 1000000 | tf_op jit(solution)/shard_map/project_early/pallas_call | solution.py:681
  20.8 0.2 collective-permute-done.3.got_hbm.even_cols_ref
  21.1 1.6 %collective-permute-start.8 = (bf16[176,768]{1,0:T(8,128)(2,1)S(1)}, bf16[176,768]{1,0:T(8,128)(2,1)S(1)}, u32[]{:S(2)}, u32[]{:S(2)}) collective-permute-start(bf16[176,768]{1,0:T(8,128)(2,1)S(1)} %collective-permute-done.refs_0_), channel_id=1, source_target_pairs={{0,16},{16,0},{1,17},{17,1},{2,18},{18,2},{3,19},{19,3},{4,20},{20... | collective-permute-start | bytes 811016 | tf_op jit(solution)/shard_map/ppermute | solution.py:716
  22.7 3.6 %collective-permute-start.6 = (bf16[8,768]{1,0:T(8,128)(2,1)S(1)}, bf16[8,768]{1,0:T(8,128)(2,1)S(1)}, u32[]{:S(2)}, u32[]{:S(2)}) collective-permute-start(bf16[8,768]{1,0:T(8,128)(2,1)S(1)} %carrier_pair.1.refs_0_), channel_id=1, source_target_pairs={{0,3},{1,2},{2,1},{3,0},{4,7},{5,6},{6,5},{7,4},{8,11},{9,10},{10,... | collective-permute-start | bytes 36872 | tf_op jit(solution)/shard_map/ppermute | solution.py:48
  26.3 1.8 %outer_blocks.1 = (bf16[640,768]{1,0:T(8,128)(2,1)S(1)}, f32[16,8,256]{2,1,0:T(8,128)S(1)}) custom-call(s32[11]{0:T(128)S(1)} %stack.67.place_ref, bf16[1024,768]{1,0:T(8,128)(2,1)S(1)} %own_norm.1.xq_ref.refs_2_.refs_9_, bf16[32,32,128]{2,1,0:T(8,128)(2,1)S(1)} %get-tuple-element.37.mark_ref, bf16[4,32,768]{2,1,0:T(8,128)(2,1)S(1)} %collective-permute-done.1.even_rows_ref, ...), custom_call_target="tpu_custom_call" | custom-call | flops 10000000 | bytes 6000000 | tf_op jit(solution)/shard_map/outer_blocks/pallas_call | solution.py:722
  28.1 0.1 collective-permute-done.6.refs_1_
  28.2 1.8 %collective-permute-start.13 = (bf16[208,768]{1,0:T(8,128)(2,1)S(1)}, bf16[208,768]{1,0:T(8,128)(2,1)S(1)}, u32[]{:S(2)}, u32[]{:S(2)}) collective-permute-start(bf16[208,768]{1,0:T(8,128)(2,1)S(1)} %final_pack.1.refs_0_), channel_id=1, source_target_pairs={{0,8},{4,12},{8,0},{12,4},{1,9},{5,13},{9,1},{13,5},{2,10},{6,14},... | collective-permute-start | bytes 958472 | tf_op jit(solution)/shard_map/ppermute | solution.py:48
  30.0 0.2 collective-permute-start.7
  30.2 0.3 collective-permute-start.9
  30.5 0.2 collective-permute-start.12
  30.7 0.8 %collective-permute-done.7.refs_1_ = bf16[176,768]{1,0:T(8,128)(2,1)S(1)} collective-permute-done((bf16[176,768]{1,0:T(8,128)(2,1)S(1)}, bf16[176,768]{1,0:T(8,128)(2,1)S(1)}, u32[]{:S(2)}, u32[]{:S(2)}) %collective-permute-start.7) | collective-permute-done | bytes 270368 | tf_op jit(solution)/shard_map/ppermute | solution.py:48
  31.6 0.4 collective-permute-done.9.refs_3_
  31.9 3.2 %project_late.1 = (bf16[3,1024,256]{2,1,0:T(8,128)(2,1)S(1)}, bf16[3,1600,256]{2,1,0:T(8,128)(2,1)S(1)}, bf16[2304,768]{1,0:T(8,128)(2,1)S(1)}) custom-call(s32[11]{0:T(128)S(1)} %stack.67.place_ref, bf16[176,768]{1,0:T(8,128)(2,1)S(1)} %collective-permute-done.refs_0_, bf16[176,768]{1,0:T(8,128)(2,1)S(1)} %collective-permute-done.7.refs_1_, ...), custom_call_target="tpu_custom_call" | custom-call | flops 1000000 | bytes 1000000 | tf_op jit(solution)/shard_map/project_late/pallas_call | solution.py:764
  35.1 3.1 %collective-permute-done.13.refs_2_ = bf16[208,768]{1,0:T(8,128)(2,1)S(1)} collective-permute-done((bf16[208,768]{1,0:T(8,128)(2,1)S(1)}, bf16[208,768]{1,0:T(8,128)(2,1)S(1)}, u32[]{:S(2)}, u32[]{:S(2)}) %collective-permute-start.13) | collective-permute-done | bytes 319520 | tf_op jit(solution)/shard_map/ppermute | solution.py:48
  38.2 2.8 %values.1.v_s = bf16[3,1600,256]{2,1,0:T(8,128)(2,1)S(1)} custom-call(s32[11]{0:T(128)S(1)} %stack.67.place_ref, bf16[2304,768]{1,0:T(8,128)(2,1)S(1)} %get-tuple-element.54.wt, bf16[4,1024,256]{2,1,0:T(8,128)(2,1)S(1)} %get-tuple-element.50.refs_7_.whole_ref, bf16[960,768]{1,0:T(8,128)(2,1)S(1)} %middle_blocks.1.refs_3_.refs_10_.mid_ref, ...), custom_call_target="tpu_custom_call" | custom-call | flops 3000000000 | bytes 7000000 | tf_op jit(solution)/shard_map/values/pallas_call | solution.py:779
  41.1 3.2 %carriers.1 = (bf16[2,2,768]{2,1,0:T(2,128)(2,1)}, bf16[768,768]{1,0:T(8,128)(2,1)S(1)}, bf16[12,256,256]{2,1,0:T(8,128)(2,1)S(1)}, f32[8,768]{1,0:T(8,128)S(1)}) custom-call(s32[11]{0:T(128)S(1)} %stack.67.place_ref, bf16[2304,768]{1,0:T(8,128)(2,1)S(1)} %get-tuple-element.54.wt, bf16[208,768]{1,0:T(8,128)(2,1)S(1)} %final_pack.1.refs_0_, ...), custom_call_target="tpu_custom_call" | custom-call | flops 500000000 | bytes 5000000 | tf_op jit(solution)/shard_map/carriers/pallas_call | solution.py:794
  44.3 6.9 %attend.1.mix_s = bf16[1024,768]{1,0:T(8,128)(2,1)S(1)} custom-call(bf16[3,1024,256]{2,1,0:T(8,128)(2,1)S(1)} %get-tuple-element.52.q_s, bf16[3,1600,256]{2,1,0:T(8,128)(2,1)S(1)} %get-tuple-element.53.k_s, bf16[3,1600,256]{2,1,0:T(8,128)(2,1)S(1)} %values.1.v_s, f32[16,8,256]{2,1,0:T(8,128)S(1)} %get-tuple-element.55.hide_ref, ...), custom_call_target="tpu_custom_call" | custom-call | flops 4000000000 | bytes 12000000 | tf_op jit(solution)/shard_map/attend/pallas_call | solution.py:810
  51.2 2.3 %out.1 = bf16[32,32,768]{2,1,0:T(8,128)(2,1)} custom-call(bf16[32,32,768]{2,1,0:T(8,128)(2,1)S(1)} %get-tuple-element.32.x_ref, bf16[1024,768]{1,0:T(8,128)(2,1)S(1)} %attend.1.mix_s, bf16[768,768]{1,0:T(8,128)(2,1)S(1)} %get-tuple-element.60.wo), custom_call_target="tpu_custom_call" | custom-call | flops 1200000000 | bytes 6000000 | tf_op jit(solution)/shard_map/out/pallas_call | solution.py:825
  (19 shorter events, 0.1 us)
Async XLA Ops:
  0.6 17.3 %collective-permute-start.5 = (bf16[576,768]{1,0:T(8,128)(2,1)}, bf16[576,768]{1,0:T(8,128)(2,1)S(1)}, u32[]{:S(2)}, u32[]{:S(2)}) collective-permute-start(bf16[576,768]{1,0:T(8,128)(2,1)} %bitcast.12), channel_id=1, source_target_pairs={{0,4},{4,0},{8,12},{12,8},{1,5},{5,1},{9,13},{13,9},{2,6},{6,2},{1... | collective-permute-start | bytes 2654216 | tf_op jit(solution)/shard_map/ppermute | solution.py:48
  3.3 8.5 %collective-permute-start.1 = (bf16[4,32,768]{2,1,0:T(8,128)(2,1)S(1)}, bf16[4,32,768]{2,1,0:T(8,128)(2,1)S(1)}, u32[]{:S(2)}, u32[]{:S(2)}) collective-permute-start(bf16[4,32,768]{2,1,0:T(8,128)(2,1)S(1)} %get-tuple-element.33), channel_id=1, source_target_pairs={{0,4},{8,12},{4,0},{12,8},{1,5},{9,13},{5,1},{13,9},{2,6},{10,14},... | collective-permute-start | bytes 589832 | tf_op jit(solution)/shard_map/ppermute | solution.py:42
  3.5 8.4 %collective-permute-start.2 = (bf16[4,32,768]{2,1,0:T(8,128)(2,1)S(1)}, bf16[4,32,768]{2,1,0:T(8,128)(2,1)S(1)}, u32[]{:S(2)}, u32[]{:S(2)}) collective-permute-start(bf16[4,32,768]{2,1,0:T(8,128)(2,1)S(1)} %get-tuple-element.38), channel_id=1, source_target_pairs={{4,8},{8,4},{5,9},{9,5},{6,10},{10,6},{7,11},{11,7},{20,24},{24,20... | collective-permute-start | bytes 589832 | tf_op jit(solution)/shard_map/ppermute | solution.py:42
  5.8 15.3 %collective-permute-start = (bf16[176,768]{1,0:T(8,128)(2,1)S(1)}, bf16[176,768]{1,0:T(8,128)(2,1)S(1)}, u32[]{:S(2)}, u32[]{:S(2)}) collective-permute-start(bf16[176,768]{1,0:T(8,128)(2,1)S(1)} %get-tuple-element.35), channel_id=1, source_target_pairs={{0,8},{4,12},{8,0},{12,4},{1,9},{5,13},{9,1},{13,5},{2,10},{6,14},... | collective-permute-start | bytes 811016 | tf_op jit(solution)/shard_map/ppermute | solution.py:48
  10.0 1.8 %copy-start.2 = (bf16[2,2,768]{2,1,0:T(2,128)(2,1)S(1)}, bf16[2,2,768]{2,1,0:T(2,128)(2,1)}, u32[]{:S(2)}) copy-start(bf16[2,2,768]{2,1,0:T(2,128)(2,1)} %own_ref.1) | copy-start | bytes 18436
  12.8 8.3 %collective-permute-start.3 = (bf16[21,8,768]{2,1,0:T(8,128)(2,1)S(1)}, bf16[21,8,768]{2,1,0:T(8,128)(2,1)S(1)}, u32[]{:S(2)}, u32[]{:S(2)}) collective-permute-start(bf16[21,8,768]{2,1,0:T(8,128)(2,1)S(1)} %get-tuple-element.39), channel_id=1, source_target_pairs={{0,1},{2,3},{1,0},{3,2},{4,5},{6,7},{5,4},{7,6},{8,9},{10,11},{9,8... | collective-permute-start | bytes 774152 | tf_op jit(solution)/shard_map/ppermute | solution.py:42
  14.6 6.5 %collective-permute-start.4 = (bf16[20,8,768]{2,1,0:T(8,128)(2,1)S(1)}, bf16[20,8,768]{2,1,0:T(8,128)(2,1)S(1)}, u32[]{:S(2)}, u32[]{:S(2)}) collective-permute-start(bf16[20,8,768]{2,1,0:T(8,128)(2,1)S(1)} %get-tuple-element.40), channel_id=1, source_target_pairs={{1,2},{2,1},{5,6},{6,5},{9,10},{10,9},{13,14},{14,13},{17,18},{18,... | collective-permute-start | bytes 737288 | tf_op jit(solution)/shard_map/ppermute | solution.py:42
  15.2 2.7 %copy-start = (bf16[768,576]{0,1:T(8,128)(2,1)S(1)}, bf16[768,576]{0,1:T(8,128)(2,1)}, u32[]{:S(2)}) copy-start(bf16[768,576]{0,1:T(8,128)(2,1)} %param.7) | copy-start | bytes 2654212
  15.3 12.8 %collective-permute-start.10 = (bf16[224,768]{1,0:T(8,128)(2,1)S(1)}, bf16[224,768]{1,0:T(8,128)(2,1)S(1)}, u32[]{:S(2)}, u32[]{:S(2)}) collective-permute-start(bf16[224,768]{1,0:T(8,128)(2,1)S(1)} %get-tuple-element.48), channel_id=1, source_target_pairs={{0,8},{4,12},{8,0},{12,4},{1,9},{5,13},{9,1},{13,5},{2,10},{6,14},... | collective-permute-start | bytes 1032200 | tf_op jit(solution)/shard_map/ppermute | solution.py:48
  20.8 7.4 %copy-start.1 = (bf16[768,192]{0,1:T(8,128)(2,1)S(1)}, bf16[768,192]{0,1:T(8,128)(2,1)}, u32[]{:S(2)}) copy-start(bf16[768,192]{0,1:T(8,128)(2,1)} %param.8) | copy-start | bytes 884740
  21.1 9.1 %collective-permute-start.8 = (bf16[176,768]{1,0:T(8,128)(2,1)S(1)}, bf16[176,768]{1,0:T(8,128)(2,1)S(1)}, u32[]{:S(2)}, u32[]{:S(2)}) collective-permute-start(bf16[176,768]{1,0:T(8,128)(2,1)S(1)} %collective-permute-done.refs_0_), channel_id=1, source_target_pairs={{0,16},{16,0},{1,17},{17,1},{2,18},{18,2},{3,19},{19,3},{4,20},{20... | collective-permute-start | bytes 811016 | tf_op jit(solution)/shard_map/ppermute | solution.py:716
  22.7 5.5 %collective-permute-start.6 = (bf16[8,768]{1,0:T(8,128)(2,1)S(1)}, bf16[8,768]{1,0:T(8,128)(2,1)S(1)}, u32[]{:S(2)}, u32[]{:S(2)}) collective-permute-start(bf16[8,768]{1,0:T(8,128)(2,1)S(1)} %carrier_pair.1.refs_0_), channel_id=1, source_target_pairs={{0,3},{1,2},{2,1},{3,0},{4,7},{5,6},{6,5},{7,4},{8,11},{9,10},{10,... | collective-permute-start | bytes 36872 | tf_op jit(solution)/shard_map/ppermute | solution.py:48
  28.2 3.4 %collective-permute-start.11 = (bf16[224,768]{1,0:T(8,128)(2,1)S(1)}, bf16[224,768]{1,0:T(8,128)(2,1)S(1)}, u32[]{:S(2)}, u32[]{:S(2)}) collective-permute-start(bf16[224,768]{1,0:T(8,128)(2,1)S(1)} %collective-permute-done.10.refs_4_), channel_id=1, source_target_pairs={{0,4},{4,0},{8,12},{12,8},{1,5},{5,1},{9,13},{13,9},{2,6},{6,2},{1... | collective-permute-start | bytes 1032200 | tf_op jit(solution)/shard_map/ppermute | solution.py:48
  28.2 10.0 %collective-permute-start.13 = (bf16[208,768]{1,0:T(8,128)(2,1)S(1)}, bf16[208,768]{1,0:T(8,128)(2,1)S(1)}, u32[]{:S(2)}, u32[]{:S(2)}) collective-permute-start(bf16[208,768]{1,0:T(8,128)(2,1)S(1)} %final_pack.1.refs_0_), channel_id=1, source_target_pairs={{0,8},{4,12},{8,0},{12,4},{1,9},{5,13},{9,1},{13,5},{2,10},{6,14},... | collective-permute-start | bytes 958472 | tf_op jit(solution)/shard_map/ppermute | solution.py:48
  30.0 1.5 %collective-permute-start.7 = (bf16[176,768]{1,0:T(8,128)(2,1)S(1)}, bf16[176,768]{1,0:T(8,128)(2,1)S(1)}, u32[]{:S(2)}, u32[]{:S(2)}) collective-permute-start(bf16[176,768]{1,0:T(8,128)(2,1)S(1)} %collective-permute-done.refs_0_), channel_id=1, source_target_pairs={{0,4},{4,0},{8,12},{12,8},{1,5},{5,1},{9,13},{13,9},{2,6},{6,2},{1... | collective-permute-start | bytes 811016 | tf_op jit(solution)/shard_map/ppermute | solution.py:48
  30.2 1.7 %collective-permute-start.9 = (bf16[176,768]{1,0:T(8,128)(2,1)S(1)}, bf16[176,768]{1,0:T(8,128)(2,1)S(1)}, u32[]{:S(2)}, u32[]{:S(2)}) collective-permute-start(bf16[176,768]{1,0:T(8,128)(2,1)S(1)} %collective-permute-done.8.refs_2_), channel_id=1, source_target_pairs={{0,4},{4,0},{8,12},{12,8},{1,5},{5,1},{9,13},{13,9},{2,6},{6,2},{1... | collective-permute-start | bytes 811016 | tf_op jit(solution)/shard_map/ppermute | solution.py:48
  30.5 10.6 %collective-permute-start.12 = (bf16[208,768]{1,0:T(8,128)(2,1)S(1)}, bf16[208,768]{1,0:T(8,128)(2,1)S(1)}, u32[]{:S(2)}, u32[]{:S(2)}) collective-permute-start(bf16[208,768]{1,0:T(8,128)(2,1)S(1)} %final_pack.1.refs_0_), channel_id=1, source_target_pairs={{0,4},{4,0},{8,12},{12,8},{1,5},{5,1},{9,13},{13,9},{2,6},{6,2},{1... | collective-permute-start | bytes 958472 | tf_op jit(solution)/shard_map/ppermute | solution.py:48
  38.2 2.9 %collective-permute-start.14 = (bf16[208,768]{1,0:T(8,128)(2,1)S(1)}, bf16[208,768]{1,0:T(8,128)(2,1)S(1)}, u32[]{:S(2)}, u32[]{:S(2)}) collective-permute-start(bf16[208,768]{1,0:T(8,128)(2,1)S(1)} %collective-permute-done.13.refs_2_), channel_id=1, source_target_pairs={{0,4},{4,0},{8,12},{12,8},{1,5},{5,1},{9,13},{13,9},{2,6},{6,2},{1... | collective-permute-start | bytes 958472 | tf_op jit(solution)/shard_map/ppermute | solution.py:48

commit v2 on v1

--- a/solution.py
+++ b/solution.py
@@ -152,12 +152,9 @@
     out_ref[...] = pair_s[...].astype(jnp.bfloat16)
 
 
-def pack_kernel(final_ref, *refs):
+def join_kernel(*refs):
     parts, out_ref = refs[:-1], refs[-1]
-    rows = final_ref.shape[0]
-    out_ref[:rows, :] = final_ref[...]
-    carriers = jnp.concatenate([part[...].astype(jnp.float32) for part in parts], axis=0)
-    out_ref[rows:, :] = carriers.astype(jnp.bfloat16)
+    out_ref[...] = jnp.concatenate([part[...].astype(jnp.float32) for part in parts], axis=0).astype(jnp.bfloat16)
 
 
 def own_kernel(x_ref, xq_ref):
@@ -444,7 +441,7 @@
 
 def carrier_kernel(offsets, place_ref, wt, *refs):
     shards = len(offsets)
-    finals, refs = refs[:shards], refs[shards:]
+    parts, finals, refs = refs[:shards], refs[shards : 2 * shards], refs[2 * shards :]
     summary_ref, wo, kce, vc_s = refs
     per_row = summary_ref.shape[1]
     channels = wt.shape[1]
@@ -455,8 +452,8 @@
     final_rows = wo.shape[0] // shards
     for j, off in enumerate(offsets):
         to = pl.multiple_of((place_ref[ROW] ^ off) * final_rows, 16)
-        wo[pl.ds(to, final_rows), :] = finals[j][:final_rows, :]
-    carriers = jnp.concatenate([final[final_rows:, :].astype(jnp.float32) for final in finals], axis=0)
+        wo[pl.ds(to, final_rows), :] = finals[j][...]
+    carriers = jnp.concatenate([part[...].astype(jnp.float32) for part in parts], axis=0)
     own = carriers[:carriers_here]
     carriers = layer_normalise(carriers).astype(jnp.bfloat16)
     own_norm = layer_normalise(own).astype(jnp.bfloat16)
@@ -738,20 +735,22 @@
         name="outer_blocks",
     )(place, xq, mark, even_rows, odd_rows, even_cols, odd_cols)
 
-    final_pack = pl.pallas_call(
-        pack_kernel,
-        out_shape=pltpu.VMEM((final_t.shape[0] + col * own_rows, channels), jnp.bfloat16),
-        in_specs=[vmem] * (1 + len(parts)),
+    row_carriers = pl.pallas_call(
+        join_kernel,
+        out_shape=pltpu.VMEM((col * own_rows, channels), jnp.bfloat16),
+        in_specs=[vmem] * len(parts),
         out_specs=vmem,
         compiler_params=small,
         cost_estimate=pl.CostEstimate(flops=1_000, bytes_accessed=1_000, transcendentals=0),
-        name="final_pack",
-    )(final_t, *parts[:-1], after(parts[-1], outer))
-    finals = [final_pack]
+        name="join_carriers",
+    )(*parts[:-1], after(parts[-1], outer))
+    finals, carriers = [final_t], [row_carriers]
     for bit in rest:
         finals = finals + [swapped(p, "row", bit) for p in finals]
-
-    far_final = swapped(final_pack, "row", far)
+    for bit in row_bits:
+        carriers = carriers + [swapped(p, "row", bit) for p in carriers]
+
+    far_final = swapped(after(final_t, even_cols, odd_cols), "row", far)
 
     far_offsets = [far]
     far_pieces = [[after(piece, outer, got)] for piece in far_pieces]
@@ -799,12 +798,12 @@
             jax.ShapeDtypeStruct((own_rows * groups, GROUP, GROUP), jnp.bfloat16),
             jax.ShapeDtypeStruct((carriers_here, channels), jnp.float32),
         ),
-        in_specs=[scalars] + [vmem] * (1 + len(finals)),
+        in_specs=[scalars] + [vmem] * (1 + len(carriers) + len(finals)),
         out_specs=(vmem,) * 4,
         compiler_params=pltpu.CompilerParams(vmem_limit_bytes=VMEM_BYTES),
         cost_estimate=pl.CostEstimate(flops=500_000_000, bytes_accessed=5_000_000, transcendentals=10_000),
         name="carriers",
-    )(place, wt, *finals)
+    )(place, wt, *carriers, *finals)
 
     scores = (groups, GROUP // HEAD_DIM * TILE * TILE, keys)
     mix = pl.pallas_call(

time: 54.2 us -> 54.4 us (level)
  starting transfers between devices: 17.1 us -> 18 us
  waiting for transfers between devices: 4.7 us -> 4.08 us
    ppermute x10 -> x13, starting transfers between devices: 12.3 us -> 13.1 us  [swapped(): return lax.ppermute(block, axis, [(i, i ^ bit) for i in range(count)])]
    ppermute x10 -> x13, waiting for transfers between devices: 4.45 us -> 3.82 us  [swapped(): return lax.ppermute(block, axis, [(i, i ^ bit) for i in range(count)])]
  transfers between devices with their start and end apart: 15 -> 18, of which waited for: 5 -> 5; matrix products, arithmetic and copies ran while one was open for 0% -> 0% of each run, Pallas kernels for 34% -> 34%
where the time goes in v2:
time: 54.4 us; the launch traced here: 54 us
  Pallas kernels  30.8 us (57%)
  starting transfers between devices  18 us (33%)
  waiting for transfers between devices  4.08 us (8%)
  between operations  1 us (2%)
    ppermute x13, starting transfers between devices, swapped(): return lax.ppermute(block, axis, [(i, i ^ bit) for i in range(count)])  13.1 us
    pallas_call x1, Pallas kernels, local(): pl.pallas_call(functools.partial(attend_kernel, rows // TILE, cols // TIL...  6.94 us
    ppermute x13, waiting for transfers between devices, swapped(): return lax.ppermute(block, axis, [(i, i ^ bit) for i in range(count)])  3.82 us
    ppermute x4, starting transfers between devices, pair_swapped(): got.append(lax.ppermute(block, axis, pairs + [(b, a) for a, b in pairs]))  3.29 us
    pallas_call x1, Pallas kernels, local(): pl.pallas_call(functools.partial(carrier_kernel, offsets), out_shape=(jax...  3.23 us
    pallas_call x1, Pallas kernels, local(): pl.pallas_call(functools.partial(late_kernel, numbered, triple_t.shape[0]...  3.18 us
    pallas_call x1, Pallas kernels, local(): pl.pallas_call(functools.partial(early_kernel, offsets), out_shape=(pltpu...  2.85 us
    pallas_call x1, Pallas kernels, local(): pl.pallas_call(value_kernel, out_shape=jax.ShapeDtypeStruct((groups, wide...  2.83 us
  transfers between devices with their start and end apart: 18, of which 5 were waited for; matrix products, arithmetic and copies ran while one was open for 0% of the time, Pallas kernels for 34%

profile of v2, /device:TPU:0, one launch (start us, length us, event | category | flops | bytes accessed | tf_op | source)
XLA Modules:
  0.0 54.0 jit_solution(17721829716246496505)
XLA Ops:
  0.6 0.5 collective-permute-start.5
  1.2 2.1 %edge_rows.1 = (bf16[32,32,128]{2,1,0:T(8,128)(2,1)S(1)}, bf16[4,32,768]{2,1,0:T(8,128)(2,1)S(1)}, bf16[4,32,768]{2,1,0:T(8,128)(2,1)S(1)}, bf16[32,32,768]{2,1,0:T(8,128)(2,1)S(1)}) custom-call(s32[11]{0:T(128)S(1)} %stack.67.place_ref, s32[32,32]{1,0:T(8,128)} %flags_hbm.1, bf16[32,32,768]{2,1,0:T(8,128)(2,1)} %x_hbm.1), custom_call_target="tpu_custom_call" | custom-call | flops 1000000 | bytes 1000000 | tf_op jit(solution)/shard_map/edge_rows/pallas_call | solution.py:599
  3.3 0.1 collective-permute-start.1
  3.5 0.7 %collective-permute-start.2 = (bf16[4,32,768]{2,1,0:T(8,128)(2,1)S(1)}, bf16[4,32,768]{2,1,0:T(8,128)(2,1)S(1)}, u32[]{:S(2)}, u32[]{:S(2)}) collective-permute-start(bf16[4,32,768]{2,1,0:T(8,128)(2,1)S(1)} %get-tuple-element.39), channel_id=1, source_target_pairs={{4,8},{8,4},{5,9},{9,5},{6,10},{10,6},{7,11},{11,7},{20,24},{24,20... | collective-permute-start | bytes 589832 | tf_op jit(solution)/shard_map/ppermute | solution.py:42
  4.1 1.6 %pieces.1 = (bf16[176,768]{1,0:T(8,128)(2,1)S(1)}, bf16[224,768]{1,0:T(8,128)(2,1)S(1)}) custom-call(s32[11]{0:T(128)S(1)} %stack.67.place_ref, bf16[576,768]{1,0:T(8,128)(2,1)} %bitcast.13), custom_call_target="tpu_custom_call" | custom-call | flops 1000000 | bytes 1000000 | tf_op jit(solution)/shard_map/pieces/pallas_call | solution.py:618
  5.8 4.3 %collective-permute-start = (bf16[176,768]{1,0:T(8,128)(2,1)S(1)}, bf16[176,768]{1,0:T(8,128)(2,1)S(1)}, u32[]{:S(2)}, u32[]{:S(2)}) collective-permute-start(bf16[176,768]{1,0:T(8,128)(2,1)S(1)} %get-tuple-element.36), channel_id=1, source_target_pairs={{0,8},{4,12},{8,0},{12,4},{1,9},{5,13},{9,1},{13,5},{2,10},{6,14},... | collective-permute-start | bytes 811016 | tf_op jit(solution)/shard_map/ppermute | solution.py:48
  10.0 1.8 %own_norm.1.xq_ref.refs_2_.refs_9_ = bf16[1024,768]{1,0:T(8,128)(2,1)S(1)} custom-call(bf16[32,32,768]{2,1,0:T(8,128)(2,1)S(1)} %get-tuple-element.33.x_ref), custom_call_target="tpu_custom_call" | custom-call | flops 1000000 | bytes 1000000 | tf_op jit(solution)/shard_map/own_norm/pallas_call | solution.py:631
  11.9 0.9 %edge_columns.1 = (bf16[21,8,768]{2,1,0:T(8,128)(2,1)S(1)}, bf16[20,8,768]{2,1,0:T(8,128)(2,1)S(1)}) custom-call(s32[11]{0:T(128)S(1)} %stack.67.place_ref, bf16[32,32,768]{2,1,0:T(8,128)(2,1)S(1)} %get-tuple-element.33.x_ref, bf16[32,32,128]{2,1,0:T(8,128)(2,1)S(1)} %get-tuple-element.38.mark_ref, ...), custom_call_target="tpu_custom_call" | custom-call | flops 1000000 | bytes 2000000 | tf_op jit(solution)/shard_map/edge_columns/pallas_call | solution.py:649
  12.8 1.8 %collective-permute-start.3 = (bf16[21,8,768]{2,1,0:T(8,128)(2,1)S(1)}, bf16[21,8,768]{2,1,0:T(8,128)(2,1)S(1)}, u32[]{:S(2)}, u32[]{:S(2)}) collective-permute-start(bf16[21,8,768]{2,1,0:T(8,128)(2,1)S(1)} %get-tuple-element.40), channel_id=1, source_target_pairs={{0,1},{2,3},{1,0},{3,2},{4,5},{6,7},{5,4},{7,6},{8,9},{10,11},{9,8... | collective-permute-start | bytes 774152 | tf_op jit(solution)/shard_map/ppermute | solution.py:42
  14.6 0.7 %collective-permute-start.4 = (bf16[20,8,768]{2,1,0:T(8,128)(2,1)S(1)}, bf16[20,8,768]{2,1,0:T(8,128)(2,1)S(1)}, u32[]{:S(2)}, u32[]{:S(2)}) collective-permute-start(bf16[20,8,768]{2,1,0:T(8,128)(2,1)S(1)} %get-tuple-element.41), channel_id=1, source_target_pairs={{1,2},{2,1},{5,6},{6,5},{9,10},{10,9},{13,14},{14,13},{17,18},{18,... | collective-permute-start | bytes 737288 | tf_op jit(solution)/shard_map/ppermute | solution.py:42
  15.3 1.4 %collective-permute-start.10 = (bf16[224,768]{1,0:T(8,128)(2,1)S(1)}, bf16[224,768]{1,0:T(8,128)(2,1)S(1)}, u32[]{:S(2)}, u32[]{:S(2)}) collective-permute-start(bf16[224,768]{1,0:T(8,128)(2,1)S(1)} %get-tuple-element.49), channel_id=1, source_target_pairs={{0,8},{4,12},{8,0},{12,4},{1,9},{5,13},{9,1},{13,5},{2,10},{6,14},... | collective-permute-start | bytes 1032200 | tf_op jit(solution)/shard_map/ppermute | solution.py:48
  16.7 1.3 %middle_blocks.1.refs_3_.refs_10_.mid_ref = bf16[960,768]{1,0:T(8,128)(2,1)S(1)} custom-call(s32[11]{0:T(128)S(1)} %stack.67.place_ref, bf16[1024,768]{1,0:T(8,128)(2,1)S(1)} %own_norm.1.xq_ref.refs_2_.refs_9_, bf16[4,32,768]{2,1,0:T(8,128)(2,1)S(1)} %collective-permute-done.1.even_rows_ref, bf16[4,32,768]{2,1,0:T(8,128)(2,1)S(1)} %collective-permute-done.2.odd_rows_ref), custom_call_target="tpu_custom_call" | custom-call | flops 1000000 | bytes 1000000 | tf_op jit(solution)/shard_map/middle_blocks/pallas_call | solution.py:668
  18.0 2.9 %project_early.1 = (bf16[4,1024,256]{2,1,0:T(8,128)(2,1)S(1)}, bf16[960,128]{1,0:T(8,128)(2,1)S(1)}, bf16[1152,768]{1,0:T(8,128)(2,1)S(1)}) custom-call(s32[11]{0:T(128)S(1)} %stack.67.place_ref, bf16[576,768]{1,0:T(8,128)(2,1)S(1)} %bitcast.14, bf16[576,768]{1,0:T(8,128)(2,1)S(1)} %collective-permute-done.5.refs_1_, ...), custom_call_target="tpu_custom_call" | custom-call | flops 1000000 | bytes 1000000 | tf_op jit(solution)/shard_map/project_early/pallas_call | solution.py:678
  20.8 0.2 collective-permute-done.3.got_hbm.even_cols_ref
  21.1 1.6 %collective-permute-start.8 = (bf16[176,768]{1,0:T(8,128)(2,1)S(1)}, bf16[176,768]{1,0:T(8,128)(2,1)S(1)}, u32[]{:S(2)}, u32[]{:S(2)}) collective-permute-start(bf16[176,768]{1,0:T(8,128)(2,1)S(1)} %collective-permute-done.refs_0_), channel_id=1, source_target_pairs={{0,16},{16,0},{1,17},{17,1},{2,18},{18,2},{3,19},{19,3},{4,20},{20... | collective-permute-start | bytes 811016 | tf_op jit(solution)/shard_map/ppermute | solution.py:713
  22.7 3.6 %collective-permute-start.6 = (bf16[8,768]{1,0:T(8,128)(2,1)S(1)}, bf16[8,768]{1,0:T(8,128)(2,1)S(1)}, u32[]{:S(2)}, u32[]{:S(2)}) collective-permute-start(bf16[8,768]{1,0:T(8,128)(2,1)S(1)} %carrier_pair.1.refs_0_), channel_id=1, source_target_pairs={{0,3},{1,2},{2,1},{3,0},{4,7},{5,6},{6,5},{7,4},{8,11},{9,10},{10,... | collective-permute-start | bytes 36872 | tf_op jit(solution)/shard_map/ppermute | solution.py:48
  26.3 1.8 %outer_blocks.1 = (bf16[640,768]{1,0:T(8,128)(2,1)S(1)}, f32[16,8,256]{2,1,0:T(8,128)S(1)}) custom-call(s32[11]{0:T(128)S(1)} %stack.67.place_ref, bf16[1024,768]{1,0:T(8,128)(2,1)S(1)} %own_norm.1.xq_ref.refs_2_.refs_9_, bf16[32,32,128]{2,1,0:T(8,128)(2,1)S(1)} %get-tuple-element.38.mark_ref, bf16[4,32,768]{2,1,0:T(8,128)(2,1)S(1)} %collective-permute-done.1.even_rows_ref, ...), custom_call_target="tpu_custom_call" | custom-call | flops 10000000 | bytes 6000000 | tf_op jit(solution)/shard_map/outer_blocks/pallas_call | solution.py:719
  28.1 0.1 collective-permute-done.6.refs_1_
  28.2 1.8 %collective-permute-start.16 = (bf16[192,768]{1,0:T(8,128)(2,1)S(1)}, bf16[192,768]{1,0:T(8,128)(2,1)S(1)}, u32[]{:S(2)}, u32[]{:S(2)}) collective-permute-start(bf16[192,768]{1,0:T(8,128)(2,1)S(1)} %bitcast.15), channel_id=1, source_target_pairs={{0,8},{4,12},{8,0},{12,4},{1,9},{5,13},{9,1},{13,5},{2,10},{6,14},... | collective-permute-start | bytes 884744 | tf_op jit(solution)/shard_map/ppermute | solution.py:48
  30.0 0.2 collective-permute-start.7
  30.1 0.3 collective-permute-start.9
  30.5 0.4 collective-permute-start.12
  30.8 0.7 %collective-permute-done.7.refs_1_ = bf16[176,768]{1,0:T(8,128)(2,1)S(1)} collective-permute-done((bf16[176,768]{1,0:T(8,128)(2,1)S(1)}, bf16[176,768]{1,0:T(8,128)(2,1)S(1)}, u32[]{:S(2)}, u32[]{:S(2)}) %collective-permute-start.7) | collective-permute-done | bytes 270368 | tf_op jit(solution)/shard_map/ppermute | solution.py:48
  31.5 0.2 collective-permute-start.15
  31.7 0.2 collective-permute-done.9.refs_3_
  31.9 3.2 %project_late.1 = (bf16[3,1024,256]{2,1,0:T(8,128)(2,1)S(1)}, bf16[3,1600,256]{2,1,0:T(8,128)(2,1)S(1)}, bf16[2304,768]{1,0:T(8,128)(2,1)S(1)}) custom-call(s32[11]{0:T(128)S(1)} %stack.67.place_ref, bf16[176,768]{1,0:T(8,128)(2,1)S(1)} %collective-permute-done.refs_0_, bf16[176,768]{1,0:T(8,128)(2,1)S(1)} %collective-permute-done.7.refs_1_, ...), custom_call_target="tpu_custom_call" | custom-call | flops 1000000 | bytes 1000000 | tf_op jit(solution)/shard_map/project_late/pallas_call | solution.py:763
  35.1 2.8 %collective-permute-done.16.refs_6_ = bf16[192,768]{1,0:T(8,128)(2,1)S(1)} collective-permute-done((bf16[192,768]{1,0:T(8,128)(2,1)S(1)}, bf16[192,768]{1,0:T(8,128)(2,1)S(1)}, u32[]{:S(2)}, u32[]{:S(2)}) %collective-permute-start.16) | collective-permute-done | bytes 294944 | tf_op jit(solution)/shard_map/ppermute | solution.py:48
  37.9 0.5 collective-permute-start.13
  38.4 2.8 %values.1.v_s = bf16[3,1600,256]{2,1,0:T(8,128)(2,1)S(1)} custom-call(s32[11]{0:T(128)S(1)} %stack.67.place_ref, bf16[2304,768]{1,0:T(8,128)(2,1)S(1)} %get-tuple-element.55.wt, bf16[4,1024,256]{2,1,0:T(8,128)(2,1)S(1)} %get-tuple-element.51.refs_7_.whole_ref, bf16[960,768]{1,0:T(8,128)(2,1)S(1)} %middle_blocks.1.refs_3_.refs_10_.mid_ref, ...), custom_call_target="tpu_custom_call" | custom-call | flops 3000000000 | bytes 7000000 | tf_op jit(solution)/shard_map/values/pallas_call | solution.py:778
  41.3 3.2 %carriers.1 = (bf16[2,2,768]{2,1,0:T(2,128)(2,1)}, bf16[768,768]{1,0:T(8,128)(2,1)S(1)}, bf16[12,256,256]{2,1,0:T(8,128)(2,1)S(1)}, f32[8,768]{1,0:T(8,128)S(1)}) custom-call(s32[11]{0:T(128)S(1)} %stack.67.place_ref, bf16[2304,768]{1,0:T(8,128)(2,1)S(1)} %get-tuple-element.55.wt, bf16[16,768]{1,0:T(8,128)(2,1)S(1)} %join_carriers.1.refs_0_, ...), custom_call_target="tpu_custom_call" | custom-call | flops 500000000 | bytes 5000000 | tf_op jit(solution)/shard_map/carriers/pallas_call | solution.py:793
  44.5 6.9 %attend.1.mix_s = bf16[1024,768]{1,0:T(8,128)(2,1)S(1)} custom-call(bf16[3,1024,256]{2,1,0:T(8,128)(2,1)S(1)} %get-tuple-element.53.q_s, bf16[3,1600,256]{2,1,0:T(8,128)(2,1)S(1)} %get-tuple-element.54.k_s, bf16[3,1600,256]{2,1,0:T(8,128)(2,1)S(1)} %values.1.v_s, f32[16,8,256]{2,1,0:T(8,128)S(1)} %get-tuple-element.56.hide_ref, ...), custom_call_target="tpu_custom_call" | custom-call | flops 4000000000 | bytes 12000000 | tf_op jit(solution)/shard_map/attend/pallas_call | solution.py:809
  51.5 2.3 %out.1 = bf16[32,32,768]{2,1,0:T(8,128)(2,1)} custom-call(bf16[32,32,768]{2,1,0:T(8,128)(2,1)S(1)} %get-tuple-element.33.x_ref, bf16[1024,768]{1,0:T(8,128)(2,1)S(1)} %attend.1.mix_s, bf16[768,768]{1,0:T(8,128)(2,1)S(1)} %get-tuple-element.62.wo), custom_call_target="tpu_custom_call" | custom-call | flops 1200000000 | bytes 6000000 | tf_op jit(solution)/shard_map/out/pallas_call | solution.py:824
  (25 shorter events, 0.2 us)
Async XLA Ops:
  0.6 17.3 %collective-permute-start.5 = (bf16[576,768]{1,0:T(8,128)(2,1)}, bf16[576,768]{1,0:T(8,128)(2,1)S(1)}, u32[]{:S(2)}, u32[]{:S(2)}) collective-permute-start(bf16[576,768]{1,0:T(8,128)(2,1)} %bitcast.12), channel_id=1, source_target_pairs={{0,4},{4,0},{8,12},{12,8},{1,5},{5,1},{9,13},{13,9},{2,6},{6,2},{1... | collective-permute-start | bytes 2654216 | tf_op jit(solution)/shard_map/ppermute | solution.py:48
  3.3 8.5 %collective-permute-start.1 = (bf16[4,32,768]{2,1,0:T(8,128)(2,1)S(1)}, bf16[4,32,768]{2,1,0:T(8,128)(2,1)S(1)}, u32[]{:S(2)}, u32[]{:S(2)}) collective-permute-start(bf16[4,32,768]{2,1,0:T(8,128)(2,1)S(1)} %get-tuple-element.34), channel_id=1, source_target_pairs={{0,4},{8,12},{4,0},{12,8},{1,5},{9,13},{5,1},{13,9},{2,6},{10,14},... | collective-permute-start | bytes 589832 | tf_op jit(solution)/shard_map/ppermute | solution.py:42
  3.5 8.4 %collective-permute-start.2 = (bf16[4,32,768]{2,1,0:T(8,128)(2,1)S(1)}, bf16[4,32,768]{2,1,0:T(8,128)(2,1)S(1)}, u32[]{:S(2)}, u32[]{:S(2)}) collective-permute-start(bf16[4,32,768]{2,1,0:T(8,128)(2,1)S(1)} %get-tuple-element.39), channel_id=1, source_target_pairs={{4,8},{8,4},{5,9},{9,5},{6,10},{10,6},{7,11},{11,7},{20,24},{24,20... | collective-permute-start | bytes 589832 | tf_op jit(solution)/shard_map/ppermute | solution.py:42
  5.8 15.3 %collective-permute-start = (bf16[176,768]{1,0:T(8,128)(2,1)S(1)}, bf16[176,768]{1,0:T(8,128)(2,1)S(1)}, u32[]{:S(2)}, u32[]{:S(2)}) collective-permute-start(bf16[176,768]{1,0:T(8,128)(2,1)S(1)} %get-tuple-element.36), channel_id=1, source_target_pairs={{0,8},{4,12},{8,0},{12,4},{1,9},{5,13},{9,1},{13,5},{2,10},{6,14},... | collective-permute-start | bytes 811016 | tf_op jit(solution)/shard_map/ppermute | solution.py:48
  10.0 1.8 %copy-start.2 = (bf16[2,2,768]{2,1,0:T(2,128)(2,1)S(1)}, bf16[2,2,768]{2,1,0:T(2,128)(2,1)}, u32[]{:S(2)}) copy-start(bf16[2,2,768]{2,1,0:T(2,128)(2,1)} %own_ref.1) | copy-start | bytes 18436
  12.8 8.3 %collective-permute-start.3 = (bf16[21,8,768]{2,1,0:T(8,128)(2,1)S(1)}, bf16[21,8,768]{2,1,0:T(8,128)(2,1)S(1)}, u32[]{:S(2)}, u32[]{:S(2)}) collective-permute-start(bf16[21,8,768]{2,1,0:T(8,128)(2,1)S(1)} %get-tuple-element.40), channel_id=1, source_target_pairs={{0,1},{2,3},{1,0},{3,2},{4,5},{6,7},{5,4},{7,6},{8,9},{10,11},{9,8... | collective-permute-start | bytes 774152 | tf_op jit(solution)/shard_map/ppermute | solution.py:42
  14.6 6.6 %collective-permute-start.4 = (bf16[20,8,768]{2,1,0:T(8,128)(2,1)S(1)}, bf16[20,8,768]{2,1,0:T(8,128)(2,1)S(1)}, u32[]{:S(2)}, u32[]{:S(2)}) collective-permute-start(bf16[20,8,768]{2,1,0:T(8,128)(2,1)S(1)} %get-tuple-element.41), channel_id=1, source_target_pairs={{1,2},{2,1},{5,6},{6,5},{9,10},{10,9},{13,14},{14,13},{17,18},{18,... | collective-permute-start | bytes 737288 | tf_op jit(solution)/shard_map/ppermute | solution.py:42
  15.2 2.7 %copy-start = (bf16[768,576]{0,1:T(8,128)(2,1)S(1)}, bf16[768,576]{0,1:T(8,128)(2,1)}, u32[]{:S(2)}) copy-start(bf16[768,576]{0,1:T(8,128)(2,1)} %param.7) | copy-start | bytes 2654212
  15.3 12.8 %collective-permute-start.10 = (bf16[224,768]{1,0:T(8,128)(2,1)S(1)}, bf16[224,768]{1,0:T(8,128)(2,1)S(1)}, u32[]{:S(2)}, u32[]{:S(2)}) collective-permute-start(bf16[224,768]{1,0:T(8,128)(2,1)S(1)} %get-tuple-element.49), channel_id=1, source_target_pairs={{0,8},{4,12},{8,0},{12,4},{1,9},{5,13},{9,1},{13,5},{2,10},{6,14},... | collective-permute-start | bytes 1032200 | tf_op jit(solution)/shard_map/ppermute | solution.py:48
  20.8 7.4 %copy-start.1 = (bf16[768,192]{0,1:T(8,128)(2,1)S(1)}, bf16[768,192]{0,1:T(8,128)(2,1)}, u32[]{:S(2)}) copy-start(bf16[768,192]{0,1:T(8,128)(2,1)} %param.8) | copy-start | bytes 884740
  21.1 9.0 %collective-permute-start.8 = (bf16[176,768]{1,0:T(8,128)(2,1)S(1)}, bf16[176,768]{1,0:T(8,128)(2,1)S(1)}, u32[]{:S(2)}, u32[]{:S(2)}) collective-permute-start(bf16[176,768]{1,0:T(8,128)(2,1)S(1)} %collective-permute-done.refs_0_), channel_id=1, source_target_pairs={{0,16},{16,0},{1,17},{17,1},{2,18},{18,2},{3,19},{19,3},{4,20},{20... | collective-permute-start | bytes 811016 | tf_op jit(solution)/shard_map/ppermute | solution.py:713
  22.7 5.5 %collective-permute-start.6 = (bf16[8,768]{1,0:T(8,128)(2,1)S(1)}, bf16[8,768]{1,0:T(8,128)(2,1)S(1)}, u32[]{:S(2)}, u32[]{:S(2)}) collective-permute-start(bf16[8,768]{1,0:T(8,128)(2,1)S(1)} %carrier_pair.1.refs_0_), channel_id=1, source_target_pairs={{0,3},{1,2},{2,1},{3,0},{4,7},{5,6},{6,5},{7,4},{8,11},{9,10},{10,... | collective-permute-start | bytes 36872 | tf_op jit(solution)/shard_map/ppermute | solution.py:48
  28.2 3.5 %collective-permute-start.11 = (bf16[224,768]{1,0:T(8,128)(2,1)S(1)}, bf16[224,768]{1,0:T(8,128)(2,1)S(1)}, u32[]{:S(2)}, u32[]{:S(2)}) collective-permute-start(bf16[224,768]{1,0:T(8,128)(2,1)S(1)} %collective-permute-done.10.refs_4_), channel_id=1, source_target_pairs={{0,4},{4,0},{8,12},{12,8},{1,5},{5,1},{9,13},{13,9},{2,6},{6,2},{1... | collective-permute-start | bytes 1032200 | tf_op jit(solution)/shard_map/ppermute | solution.py:48
  28.2 9.7 %collective-permute-start.16 = (bf16[192,768]{1,0:T(8,128)(2,1)S(1)}, bf16[192,768]{1,0:T(8,128)(2,1)S(1)}, u32[]{:S(2)}, u32[]{:S(2)}) collective-permute-start(bf16[192,768]{1,0:T(8,128)(2,1)S(1)} %bitcast.15), channel_id=1, source_target_pairs={{0,8},{4,12},{8,0},{12,4},{1,9},{5,13},{9,1},{13,5},{2,10},{6,14},... | collective-permute-start | bytes 884744 | tf_op jit(solution)/shard_map/ppermute | solution.py:48
  30.0 1.5 %collective-permute-start.7 = (bf16[176,768]{1,0:T(8,128)(2,1)S(1)}, bf16[176,768]{1,0:T(8,128)(2,1)S(1)}, u32[]{:S(2)}, u32[]{:S(2)}) collective-permute-start(bf16[176,768]{1,0:T(8,128)(2,1)S(1)} %collective-permute-done.refs_0_), channel_id=1, source_target_pairs={{0,4},{4,0},{8,12},{12,8},{1,5},{5,1},{9,13},{13,9},{2,6},{6,2},{1... | collective-permute-start | bytes 811016 | tf_op jit(solution)/shard_map/ppermute | solution.py:48
  30.1 1.8 %collective-permute-start.9 = (bf16[176,768]{1,0:T(8,128)(2,1)S(1)}, bf16[176,768]{1,0:T(8,128)(2,1)S(1)}, u32[]{:S(2)}, u32[]{:S(2)}) collective-permute-start(bf16[176,768]{1,0:T(8,128)(2,1)S(1)} %collective-permute-done.8.refs_2_), channel_id=1, source_target_pairs={{0,4},{4,0},{8,12},{12,8},{1,5},{5,1},{9,13},{13,9},{2,6},{6,2},{1... | collective-permute-start | bytes 811016 | tf_op jit(solution)/shard_map/ppermute | solution.py:48
  30.5 7.9 %collective-permute-start.12 = (bf16[16,768]{1,0:T(8,128)(2,1)S(1)}, bf16[16,768]{1,0:T(8,128)(2,1)S(1)}, u32[]{:S(2)}, u32[]{:S(2)}) collective-permute-start(bf16[16,768]{1,0:T(8,128)(2,1)S(1)} %join_carriers.1.refs_0_), channel_id=1, source_target_pairs={{0,8},{4,12},{8,0},{12,4},{1,9},{5,13},{9,1},{13,5},{2,10},{6,14},... | collective-permute-start | bytes 73736 | tf_op jit(solution)/shard_map/ppermute | solution.py:48
  31.5 9.7 %collective-permute-start.15 = (bf16[192,768]{1,0:T(8,128)(2,1)S(1)}, bf16[192,768]{1,0:T(8,128)(2,1)S(1)}, u32[]{:S(2)}, u32[]{:S(2)}) collective-permute-start(bf16[192,768]{1,0:T(8,128)(2,1)S(1)} %bitcast.16), channel_id=1, source_target_pairs={{0,4},{4,0},{8,12},{12,8},{1,5},{5,1},{9,13},{13,9},{2,6},{6,2},{1... | collective-permute-start | bytes 884744 | tf_op jit(solution)/shard_map/ppermute | solution.py:48
  37.9 3.4 %collective-permute-start.17 = (bf16[192,768]{1,0:T(8,128)(2,1)S(1)}, bf16[192,768]{1,0:T(8,128)(2,1)S(1)}, u32[]{:S(2)}, u32[]{:S(2)}) collective-permute-start(bf16[192,768]{1,0:T(8,128)(2,1)S(1)} %collective-permute-done.16.refs_6_), channel_id=1, source_target_pairs={{0,4},{4,0},{8,12},{12,8},{1,5},{5,1},{9,13},{13,9},{2,6},{6,2},{1... | collective-permute-start | bytes 884744 | tf_op jit(solution)/shard_map/ppermute | solution.py:48
  37.9 3.4 %collective-permute-start.13 = (bf16[16,768]{1,0:T(8,128)(2,1)S(1)}, bf16[16,768]{1,0:T(8,128)(2,1)S(1)}, u32[]{:S(2)}, u32[]{:S(2)}) collective-permute-start(bf16[16,768]{1,0:T(8,128)(2,1)S(1)} %join_carriers.1.refs_0_), channel_id=1, source_target_pairs={{0,4},{4,0},{8,12},{12,8},{1,5},{5,1},{9,13},{13,9},{2,6},{6,2},{1... | collective-permute-start | bytes 73736 | tf_op jit(solution)/shard_map/ppermute | solution.py:48
  38.4 2.9 %collective-permute-start.14 = (bf16[16,768]{1,0:T(8,128)(2,1)S(1)}, bf16[16,768]{1,0:T(8,128)(2,1)S(1)}, u32[]{:S(2)}, u32[]{:S(2)}) collective-permute-start(bf16[16,768]{1,0:T(8,128)(2,1)S(1)} %collective-permute-done.12.refs_1_), channel_id=1, source_target_pairs={{0,4},{4,0},{8,12},{12,8},{1,5},{5,1},{9,13},{13,9},{2,6},{6,2},{1... | collective-permute-start | bytes 73736 | tf_op jit(solution)/shard_map/ppermute | solution.py:48

commit v3 on v1

--- a/solution.py
+++ b/solution.py
@@ -363,16 +363,16 @@
         pl.when(place_ref[HALF] == half)(functools.partial(run, half))
 
 
-def project_rest(half, sections, channels, near_at, far_at, sources, put):
+def project_rest(half, sections, channels, near_at, far_at, sources, put, groups=None):
     xq_ref, mid_ref, outer_ref = sources
     edge, mid = outer_ref.shape[0] // 2, mid_ref.shape[0]
     for number, at, section, group, lane, width in numbered_chunks(channels, half):
-        if section in sections and section > 0:
+        if section in sections and section > 0 and (groups is None or group in groups):
             w = near_at(at, width)
             for first, to in ((0, 0), (edge, edge + mid)):
                 put(section, group, lane, width, slice(to, to + edge), nt(outer_ref[first : first + edge, :], w).astype(jnp.bfloat16))
     for at, section, group, lane, width in column_chunks(channels, 1 - half):
-        if section not in sections:
+        if section not in sections or (groups is not None and group not in groups):
             continue
         w = far_at(at, width)
         if section == 0:
@@ -424,19 +424,20 @@
     near_copy.wait()
 
 
-def value_kernel(place_ref, wt, whole_ref, mid_ref, outer_ref, v_s):
+def value_kernel(first, place_ref, wt, whole_ref, mid_ref, outer_ref, v_s):
+    here = range(first, first + v_s.shape[0])
     channels = wt.shape[1]
     edge, mid = outer_ref.shape[0] // 2, mid_ref.shape[0]
 
     def put(section, group, lane, width, lines, value):
-        v_s[group, lines, lane : lane + width] = value
+        v_s[group - first, lines, lane : lane + width] = value
 
     def run(half):
         for number, at, section, group, lane, width in numbered_chunks(channels, half):
-            if section == 2:
-                v_s[group, edge : edge + mid, :] = whole_ref[number, :mid, :]
+            if section == 2 and group in here:
+                v_s[group - first, edge : edge + mid, :] = whole_ref[number, :mid, :]
         weights = lambda at, width: wt[at : at + width, :]
-        project_rest(half, (2,), channels, weights, weights, (None, mid_ref, outer_ref), put)
+        project_rest(half, (2,), channels, weights, weights, (None, mid_ref, outer_ref), put, here)
 
     for half in range(2):
         pl.when(place_ref[HALF] == half)(functools.partial(run, half))
@@ -486,7 +487,7 @@
             kce[w * groups + g] = jnp.where(same, fresh[w : w + 1, g * GROUP : (g + 1) * GROUP], 0.0).astype(jnp.bfloat16)
 
 
-def attend_kernel(tall, broad, q_s, k_s, v_s, hide_ref, kce, vc_s, mix_s, pc_s, even_s, odd_s):
+def attend_kernel(tall, broad, q_s, k_s, v_low, v_high, hide_ref, kce, vc_s, mix_s, pc_s, even_s, odd_s):
     groups, tiles = q_s.shape[0], hide_ref.shape[0]
     heads_in = GROUP // HEAD_DIM
     queries, span = TILE * TILE, 2 * TILE * TILE
@@ -531,7 +532,8 @@
         for g in range(groups):
             p = jnp.exp2(ref[g].reshape(heads_in, queries, 2 * span) + bias[None])
             total = jnp.sum(p, axis=-1, keepdims=True)
-            v = jnp.concatenate([v_s[g, pl.ds(k0, span), :], v_s[g, pl.ds(k1, span), :]], axis=0)
+            v_ref, at = (v_low, g) if g < v_low.shape[0] else (v_high, g - v_low.shape[0])
+            v = jnp.concatenate([v_ref[at, pl.ds(k0, span), :], v_ref[at, pl.ds(k1, span), :]], axis=0)
             o = nn(p.reshape(heads_in * queries, 2 * span).astype(jnp.bfloat16), v).reshape(heads_in, queries, GROUP)
             v_new = vc_s[pl.ds(window, 1), g * GROUP : (g + 1) * GROUP]
             for j in range(GROUP // LANES):
@@ -776,17 +778,22 @@
         name="project_late",
     )(place, *sources, near, whole, part, xq, mid, outer)
 
-    v = pl.pallas_call(
-        value_kernel,
-        out_shape=jax.ShapeDtypeStruct((groups, wide_rows * wide_cols, GROUP), jnp.bfloat16),
-        in_specs=[scalars] + [vmem] * 4,
-        out_specs=vmem,
-        compiler_params=pltpu.CompilerParams(vmem_limit_bytes=VMEM_BYTES),
-        cost_estimate=pl.CostEstimate(flops=3_000_000_000, bytes_accessed=7_000_000, transcendentals=0),
-        name="values",
-    )(place, wt, whole, mid, outer)
-
-    far_finals = [after(far_final, q)]
+    def values(first, count, wt):
+        return pl.pallas_call(
+            functools.partial(value_kernel, first),
+            out_shape=jax.ShapeDtypeStruct((count, wide_rows * wide_cols, GROUP), jnp.bfloat16),
+            in_specs=[scalars] + [vmem] * 4,
+            out_specs=vmem,
+            compiler_params=pltpu.CompilerParams(vmem_limit_bytes=VMEM_BYTES),
+            cost_estimate=pl.CostEstimate(flops=3_000_000_000, bytes_accessed=7_000_000, transcendentals=0),
+            name="values",
+        )(place, wt, whole, mid, outer)
+
+    split = groups // 2 + groups % 2
+    v_low = values(0, split, wt)
+    v_high = values(split, groups - split, after(wt, v_low))
+
+    far_finals = [after(far_final, v_low)]
     for bit in rest:
         far_finals = far_finals + [swapped(p, "row", bit) for p in far_finals]
     finals, offsets = finals + far_finals, offsets + far_offsets
@@ -810,7 +817,7 @@
     mix = pl.pallas_call(
         functools.partial(attend_kernel, rows // TILE, cols // TILE),
         out_shape=jax.ShapeDtypeStruct((rows * cols, channels), jnp.bfloat16),
-        in_specs=[vmem] * 6,
+        in_specs=[vmem] * 7,
         out_specs=vmem,
         scratch_shapes=[
             pltpu.VMEM((rows * cols, channels), jnp.float32),
@@ -820,7 +827,7 @@
         compiler_params=pltpu.CompilerParams(vmem_limit_bytes=VMEM_BYTES),
         cost_estimate=pl.CostEstimate(flops=4_000_000_000, bytes_accessed=12_000_000, transcendentals=4_000_000),
         name="attend",
-    )(q, k, v, hide, kce, vc)
+    )(q, k, v_low, v_high, hide, kce, vc)
 
     out = pl.pallas_call(
         out_kernel,

time: 54.2 us -> 55.5 us (1.024)
  the two profiles are of different devices: /device:TPU:0 before, /device:TPU:9 now
where the time goes in v3:
time: 55.5 us; the launch traced here: 55.2 us
  Pallas kernels  31.6 us (57%)
  starting transfers between devices  19.2 us (35%)
  waiting for transfers between devices  3.35 us (6%)
  between operations  1.02 us (2%)
    ppermute x10, starting transfers between devices, swapped(): return lax.ppermute(block, axis, [(i, i ^ bit) for i in range(count)])  9.78 us
    ppermute x4, starting transfers between devices, pair_swapped(): got.append(lax.ppermute(block, axis, pairs + [(b, a) for a, b in pairs]))  8.15 us
    pallas_call x1, Pallas kernels, local(): pl.pallas_call(functools.partial(attend_kernel, rows // TILE, cols // TIL...  6.87 us
    pallas_call x2, Pallas kernels, values(): pl.pallas_call(functools.partial(value_kernel, first), out_shape=jax.Shap...  3.58 us
    pallas_call x1, Pallas kernels, local(): pl.pallas_call(functools.partial(carrier_kernel, offsets), out_shape=(jax...  3.23 us
    pallas_call x1, Pallas kernels, local(): pl.pallas_call(functools.partial(late_kernel, numbered, triple_t.shape[0]...  3.19 us
    pallas_call x1, Pallas kernels, local(): pl.pallas_call(functools.partial(early_kernel, offsets), out_shape=(pltpu...  2.85 us
    ppermute x10, waiting for transfers between devices, swapped(): return lax.ppermute(block, axis, [(i, i ^ bit) for i in range(count)])  2.67 us
  transfers between devices with their start and end apart: 15, of which 3 were waited for; matrix products, arithmetic and copies ran while one was open for 0% of the time, Pallas kernels for 35%

profile of v3, /device:TPU:9, one launch (start us, length us, event | category | flops | bytes accessed | tf_op | source)
XLA Modules:
  0.0 55.2 jit_solution(2028264903729637000)
XLA Ops:
  0.6 0.7 %collective-permute-start.5 = (bf16[576,768]{1,0:T(8,128)(2,1)}, bf16[576,768]{1,0:T(8,128)(2,1)S(1)}, u32[]{:S(2)}, u32[]{:S(2)}) collective-permute-start(bf16[576,768]{1,0:T(8,128)(2,1)} %bitcast.12), channel_id=1, source_target_pairs={{0,4},{4,0},{8,12},{12,8},{1,5},{5,1},{9,13},{13,9},{2,6},{6,2},{1... | collective-permute-start | bytes 2654216 | tf_op jit(solution)/shard_map/ppermute | solution.py:48
  1.4 0.1 stack.67.place_ref
  1.5 2.1 %edge_rows.1 = (bf16[32,32,128]{2,1,0:T(8,128)(2,1)S(1)}, bf16[4,32,768]{2,1,0:T(8,128)(2,1)S(1)}, bf16[4,32,768]{2,1,0:T(8,128)(2,1)S(1)}, bf16[32,32,768]{2,1,0:T(8,128)(2,1)S(1)}) custom-call(s32[11]{0:T(128)S(1)} %stack.67.place_ref, s32[32,32]{1,0:T(8,128)} %flags_hbm.1, bf16[32,32,768]{2,1,0:T(8,128)(2,1)} %x_hbm.1), custom_call_target="tpu_custom_call" | custom-call | flops 1000000 | bytes 1000000 | tf_op jit(solution)/shard_map/edge_rows/pallas_call | solution.py:604
  3.6 0.1 collective-permute-start.1
  3.7 3.5 %collective-permute-start.2 = (bf16[4,32,768]{2,1,0:T(8,128)(2,1)S(1)}, bf16[4,32,768]{2,1,0:T(8,128)(2,1)S(1)}, u32[]{:S(2)}, u32[]{:S(2)}) collective-permute-start(bf16[4,32,768]{2,1,0:T(8,128)(2,1)S(1)} %get-tuple-element.39), channel_id=1, source_target_pairs={{4,8},{8,4},{5,9},{9,5},{6,10},{10,6},{7,11},{11,7},{20,24},{24,20... | collective-permute-start | bytes 589832 | tf_op jit(solution)/shard_map/ppermute | solution.py:42
  7.2 1.6 %pieces.1 = (bf16[176,768]{1,0:T(8,128)(2,1)S(1)}, bf16[224,768]{1,0:T(8,128)(2,1)S(1)}) custom-call(s32[11]{0:T(128)S(1)} %stack.67.place_ref, bf16[576,768]{1,0:T(8,128)(2,1)} %bitcast.13), custom_call_target="tpu_custom_call" | custom-call | flops 1000000 | bytes 1000000 | tf_op jit(solution)/shard_map/pieces/pallas_call | solution.py:623
  8.8 0.1 collective-permute-start
  8.9 0.0 copy-start.2
  8.9 1.8 %own_norm.1.xq_ref.refs_2_.refs_9_ = bf16[1024,768]{1,0:T(8,128)(2,1)S(1)} custom-call(bf16[32,32,768]{2,1,0:T(8,128)(2,1)S(1)} %get-tuple-element.33.x_ref), custom_call_target="tpu_custom_call" | custom-call | flops 1000000 | bytes 1000000 | tf_op jit(solution)/shard_map/own_norm/pallas_call | solution.py:636
  10.7 0.9 %edge_columns.1 = (bf16[21,8,768]{2,1,0:T(8,128)(2,1)S(1)}, bf16[20,8,768]{2,1,0:T(8,128)(2,1)S(1)}) custom-call(s32[11]{0:T(128)S(1)} %stack.67.place_ref, bf16[32,32,768]{2,1,0:T(8,128)(2,1)S(1)} %get-tuple-element.33.x_ref, bf16[32,32,128]{2,1,0:T(8,128)(2,1)S(1)} %get-tuple-element.38.mark_ref, ...), custom_call_target="tpu_custom_call" | custom-call | flops 1000000 | bytes 2000000 | tf_op jit(solution)/shard_map/edge_columns/pallas_call | solution.py:654
  11.6 0.2 collective-permute-start.3
  11.8 4.3 %collective-permute-start.4 = (bf16[20,8,768]{2,1,0:T(8,128)(2,1)S(1)}, bf16[20,8,768]{2,1,0:T(8,128)(2,1)S(1)}, u32[]{:S(2)}, u32[]{:S(2)}) collective-permute-start(bf16[20,8,768]{2,1,0:T(8,128)(2,1)S(1)} %get-tuple-element.41), channel_id=1, source_target_pairs={{1,2},{2,1},{5,6},{6,5},{9,10},{10,9},{13,14},{14,13},{17,18},{18,... | collective-permute-start | bytes 737288 | tf_op jit(solution)/shard_map/ppermute | solution.py:42
  16.2 1.5 %collective-permute-start.10 = (bf16[224,768]{1,0:T(8,128)(2,1)S(1)}, bf16[224,768]{1,0:T(8,128)(2,1)S(1)}, u32[]{:S(2)}, u32[]{:S(2)}) collective-permute-start(bf16[224,768]{1,0:T(8,128)(2,1)S(1)} %get-tuple-element.49), channel_id=1, source_target_pairs={{0,8},{4,12},{8,0},{12,4},{1,9},{5,13},{9,1},{13,5},{2,10},{6,14},... | collective-permute-start | bytes 1032200 | tf_op jit(solution)/shard_map/ppermute | solution.py:48
  17.7 1.3 %middle_blocks.1.refs_3_.refs_10_.mid_ref = bf16[960,768]{1,0:T(8,128)(2,1)S(1)} custom-call(s32[11]{0:T(128)S(1)} %stack.67.place_ref, bf16[1024,768]{1,0:T(8,128)(2,1)S(1)} %own_norm.1.xq_ref.refs_2_.refs_9_, bf16[4,32,768]{2,1,0:T(8,128)(2,1)S(1)} %collective-permute-done.1.even_rows_ref, bf16[4,32,768]{2,1,0:T(8,128)(2,1)S(1)} %collective-permute-done.2.odd_rows_ref), custom_call_target="tpu_custom_call" | custom-call | flops 1000000 | bytes 1000000 | tf_op jit(solution)/shard_map/middle_blocks/pallas_call | solution.py:673
  19.0 2.9 %project_early.1 = (bf16[4,1024,256]{2,1,0:T(8,128)(2,1)S(1)}, bf16[960,128]{1,0:T(8,128)(2,1)S(1)}, bf16[1152,768]{1,0:T(8,128)(2,1)S(1)}) custom-call(s32[11]{0:T(128)S(1)} %stack.67.place_ref, bf16[576,768]{1,0:T(8,128)(2,1)S(1)} %bitcast.14, bf16[576,768]{1,0:T(8,128)(2,1)S(1)} %collective-permute-done.5.refs_1_, ...), custom_call_target="tpu_custom_call" | custom-call | flops 1000000 | bytes 1000000 | tf_op jit(solution)/shard_map/project_early/pallas_call | solution.py:683
  21.9 1.3 %collective-permute-start.8 = (bf16[176,768]{1,0:T(8,128)(2,1)S(1)}, bf16[176,768]{1,0:T(8,128)(2,1)S(1)}, u32[]{:S(2)}, u32[]{:S(2)}) collective-permute-start(bf16[176,768]{1,0:T(8,128)(2,1)S(1)} %collective-permute-done.refs_0_), channel_id=1, source_target_pairs={{0,16},{16,0},{1,17},{17,1},{2,18},{18,2},{3,19},{19,3},{4,20},{20... | collective-permute-start | bytes 811016 | tf_op jit(solution)/shard_map/ppermute | solution.py:718
  23.2 0.8 %collective-permute-start.6 = (bf16[8,768]{1,0:T(8,128)(2,1)S(1)}, bf16[8,768]{1,0:T(8,128)(2,1)S(1)}, u32[]{:S(2)}, u32[]{:S(2)}) collective-permute-start(bf16[8,768]{1,0:T(8,128)(2,1)S(1)} %carrier_pair.1.refs_0_), channel_id=1, source_target_pairs={{0,3},{1,2},{2,1},{3,0},{4,7},{5,6},{6,5},{7,4},{8,11},{9,10},{10,... | collective-permute-start | bytes 36872 | tf_op jit(solution)/shard_map/ppermute | solution.py:48
  24.0 1.8 %outer_blocks.1 = (bf16[640,768]{1,0:T(8,128)(2,1)S(1)}, f32[16,8,256]{2,1,0:T(8,128)S(1)}) custom-call(s32[11]{0:T(128)S(1)} %stack.67.place_ref, bf16[1024,768]{1,0:T(8,128)(2,1)S(1)} %own_norm.1.xq_ref.refs_2_.refs_9_, bf16[32,32,128]{2,1,0:T(8,128)(2,1)S(1)} %get-tuple-element.38.mark_ref, bf16[4,32,768]{2,1,0:T(8,128)(2,1)S(1)} %collective-permute-done.1.even_rows_ref, ...), custom_call_target="tpu_custom_call" | custom-call | flops 10000000 | bytes 6000000 | tf_op jit(solution)/shard_map/outer_blocks/pallas_call | solution.py:724
  25.7 0.4 collective-permute-done.6.refs_1_
  26.1 2.1 %collective-permute-start.11 = (bf16[224,768]{1,0:T(8,128)(2,1)S(1)}, bf16[224,768]{1,0:T(8,128)(2,1)S(1)}, u32[]{:S(2)}, u32[]{:S(2)}) collective-permute-start(bf16[224,768]{1,0:T(8,128)(2,1)S(1)} %collective-permute-done.10.refs_4_), channel_id=1, source_target_pairs={{0,4},{4,0},{8,12},{12,8},{1,5},{5,1},{9,13},{13,9},{2,6},{6,2},{1... | collective-permute-start | bytes 1032200 | tf_op jit(solution)/shard_map/ppermute | solution.py:48
  28.2 0.7 %collective-permute-done.8.refs_2_ = bf16[176,768]{1,0:T(8,128)(2,1)S(1)} collective-permute-done((bf16[176,768]{1,0:T(8,128)(2,1)S(1)}, bf16[176,768]{1,0:T(8,128)(2,1)S(1)}, u32[]{:S(2)}, u32[]{:S(2)}) %collective-permute-start.8) | collective-permute-done | bytes 270368 | tf_op jit(solution)/shard_map/ppermute | solution.py:718
  28.9 2.0 %collective-permute-start.9 = (bf16[176,768]{1,0:T(8,128)(2,1)S(1)}, bf16[176,768]{1,0:T(8,128)(2,1)S(1)}, u32[]{:S(2)}, u32[]{:S(2)}) collective-permute-start(bf16[176,768]{1,0:T(8,128)(2,1)S(1)} %collective-permute-done.8.refs_2_), channel_id=1, source_target_pairs={{0,4},{4,0},{8,12},{12,8},{1,5},{5,1},{9,13},{13,9},{2,6},{6,2},{1... | collective-permute-start | bytes 811016 | tf_op jit(solution)/shard_map/ppermute | solution.py:48
  30.9 1.6 %collective-permute-start.13 = (bf16[208,768]{1,0:T(8,128)(2,1)S(1)}, bf16[208,768]{1,0:T(8,128)(2,1)S(1)}, u32[]{:S(2)}, u32[]{:S(2)}) collective-permute-start(bf16[208,768]{1,0:T(8,128)(2,1)S(1)} %final_pack.1.refs_0_), channel_id=1, source_target_pairs={{0,8},{4,12},{8,0},{12,4},{1,9},{5,13},{9,1},{13,5},{2,10},{6,14},... | collective-permute-start | bytes 958472 | tf_op jit(solution)/shard_map/ppermute | solution.py:48
  32.5 0.3 collective-permute-start.12
  32.8 3.2 %project_late.1 = (bf16[3,1024,256]{2,1,0:T(8,128)(2,1)S(1)}, bf16[3,1600,256]{2,1,0:T(8,128)(2,1)S(1)}, bf16[2304,768]{1,0:T(8,128)(2,1)S(1)}) custom-call(s32[11]{0:T(128)S(1)} %stack.67.place_ref, bf16[176,768]{1,0:T(8,128)(2,1)S(1)} %collective-permute-done.refs_0_, bf16[176,768]{1,0:T(8,128)(2,1)S(1)} %collective-permute-done.7.refs_1_, ...), custom_call_target="tpu_custom_call" | custom-call | flops 1000000 | bytes 1000000 | tf_op jit(solution)/shard_map/project_late/pallas_call | solution.py:766
  36.0 2.0 %values.2.v_low = bf16[2,1600,256]{2,1,0:T(8,128)(2,1)S(1)} custom-call(s32[11]{0:T(128)S(1)} %stack.67.place_ref, bf16[2304,768]{1,0:T(8,128)(2,1)S(1)} %get-tuple-element.56.wt, bf16[4,1024,256]{2,1,0:T(8,128)(2,1)S(1)} %get-tuple-element.51.refs_7_.whole_ref, bf16[960,768]{1,0:T(8,128)(2,1)S(1)} %middle_blocks.1.refs_3_.refs_10_.mid_ref, ...), custom_call_target="tpu_custom_call" | custom-call | flops 3000000000 | bytes 7000000 | tf_op jit(solution)/shard_map/values/pallas_call | solution.py:782
  38.0 2.3 %collective-permute-done.13.refs_2_ = bf16[208,768]{1,0:T(8,128)(2,1)S(1)} collective-permute-done((bf16[208,768]{1,0:T(8,128)(2,1)S(1)}, bf16[208,768]{1,0:T(8,128)(2,1)S(1)}, u32[]{:S(2)}, u32[]{:S(2)}) %collective-permute-start.13) | collective-permute-done | bytes 319520 | tf_op jit(solution)/shard_map/ppermute | solution.py:48
  40.3 0.7 %collective-permute-start.14 = (bf16[208,768]{1,0:T(8,128)(2,1)S(1)}, bf16[208,768]{1,0:T(8,128)(2,1)S(1)}, u32[]{:S(2)}, u32[]{:S(2)}) collective-permute-start(bf16[208,768]{1,0:T(8,128)(2,1)S(1)} %collective-permute-done.13.refs_2_), channel_id=1, source_target_pairs={{0,4},{4,0},{8,12},{12,8},{1,5},{5,1},{9,13},{13,9},{2,6},{6,2},{1... | collective-permute-start | bytes 958472 | tf_op jit(solution)/shard_map/ppermute | solution.py:48
  41.0 1.6 %values.3.v_high = bf16[1,1600,256]{2,1,0:T(8,128)(2,1)S(1)} custom-call(s32[11]{0:T(128)S(1)} %stack.67.place_ref, bf16[2304,768]{1,0:T(8,128)(2,1)S(1)} %get-tuple-element.56.wt, bf16[4,1024,256]{2,1,0:T(8,128)(2,1)S(1)} %get-tuple-element.51.refs_7_.whole_ref, bf16[960,768]{1,0:T(8,128)(2,1)S(1)} %middle_blocks.1.refs_3_.refs_10_.mid_ref, ...), custom_call_target="tpu_custom_call" | custom-call | flops 3000000000 | bytes 7000000 | tf_op jit(solution)/shard_map/values/pallas_call | solution.py:782
  42.6 3.2 %carriers.1 = (bf16[2,2,768]{2,1,0:T(2,128)(2,1)}, bf16[768,768]{1,0:T(8,128)(2,1)S(1)}, bf16[12,256,256]{2,1,0:T(8,128)(2,1)S(1)}, f32[8,768]{1,0:T(8,128)S(1)}) custom-call(s32[11]{0:T(128)S(1)} %stack.67.place_ref, bf16[2304,768]{1,0:T(8,128)(2,1)S(1)} %get-tuple-element.56.wt, bf16[208,768]{1,0:T(8,128)(2,1)S(1)} %final_pack.1.refs_0_, ...), custom_call_target="tpu_custom_call" | custom-call | flops 500000000 | bytes 5000000 | tf_op jit(solution)/shard_map/carriers/pallas_call | solution.py:801
  45.8 6.9 %attend.1.mix_s = bf16[1024,768]{1,0:T(8,128)(2,1)S(1)} custom-call(bf16[3,1024,256]{2,1,0:T(8,128)(2,1)S(1)} %get-tuple-element.53.q_s, bf16[3,1600,256]{2,1,0:T(8,128)(2,1)S(1)} %get-tuple-element.54.k_s, bf16[2,1600,256]{2,1,0:T(8,128)(2,1)S(1)} %values.2.v_low, bf16[1,1600,256]{2,1,0:T(8,128)(2,1)S(1)} %values.3.v_high, ...), custom_call_target="tpu_custom_call" | custom-call | flops 4000000000 | bytes 12000000 | tf_op jit(solution)/shard_map/attend/pallas_call | solution.py:817
  52.7 2.3 %out.1 = bf16[32,32,768]{2,1,0:T(8,128)(2,1)} custom-call(bf16[32,32,768]{2,1,0:T(8,128)(2,1)S(1)} %get-tuple-element.33.x_ref, bf16[1024,768]{1,0:T(8,128)(2,1)S(1)} %attend.1.mix_s, bf16[768,768]{1,0:T(8,128)(2,1)S(1)} %get-tuple-element.62.wo), custom_call_target="tpu_custom_call" | custom-call | flops 1200000000 | bytes 6000000 | tf_op jit(solution)/shard_map/out/pallas_call | solution.py:832
  (20 shorter events, 0.1 us)
Async XLA Ops:
  0.6 18.3 %collective-permute-start.5 = (bf16[576,768]{1,0:T(8,128)(2,1)}, bf16[576,768]{1,0:T(8,128)(2,1)S(1)}, u32[]{:S(2)}, u32[]{:S(2)}) collective-permute-start(bf16[576,768]{1,0:T(8,128)(2,1)} %bitcast.12), channel_id=1, source_target_pairs={{0,4},{4,0},{8,12},{12,8},{1,5},{5,1},{9,13},{13,9},{2,6},{6,2},{1... | collective-permute-start | bytes 2654216 | tf_op jit(solution)/shard_map/ppermute | solution.py:48
  3.6 7.2 %collective-permute-start.1 = (bf16[4,32,768]{2,1,0:T(8,128)(2,1)S(1)}, bf16[4,32,768]{2,1,0:T(8,128)(2,1)S(1)}, u32[]{:S(2)}, u32[]{:S(2)}) collective-permute-start(bf16[4,32,768]{2,1,0:T(8,128)(2,1)S(1)} %get-tuple-element.34), channel_id=1, source_target_pairs={{0,4},{8,12},{4,0},{12,8},{1,5},{9,13},{5,1},{13,9},{2,6},{10,14},... | collective-permute-start | bytes 589832 | tf_op jit(solution)/shard_map/ppermute | solution.py:42
  3.7 7.0 %collective-permute-start.2 = (bf16[4,32,768]{2,1,0:T(8,128)(2,1)S(1)}, bf16[4,32,768]{2,1,0:T(8,128)(2,1)S(1)}, u32[]{:S(2)}, u32[]{:S(2)}) collective-permute-start(bf16[4,32,768]{2,1,0:T(8,128)(2,1)S(1)} %get-tuple-element.39), channel_id=1, source_target_pairs={{4,8},{8,4},{5,9},{9,5},{6,10},{10,6},{7,11},{11,7},{20,24},{24,20... | collective-permute-start | bytes 589832 | tf_op jit(solution)/shard_map/ppermute | solution.py:42
  8.8 13.1 %collective-permute-start = (bf16[176,768]{1,0:T(8,128)(2,1)S(1)}, bf16[176,768]{1,0:T(8,128)(2,1)S(1)}, u32[]{:S(2)}, u32[]{:S(2)}) collective-permute-start(bf16[176,768]{1,0:T(8,128)(2,1)S(1)} %get-tuple-element.36), channel_id=1, source_target_pairs={{0,8},{4,12},{8,0},{12,4},{1,9},{5,13},{9,1},{13,5},{2,10},{6,14},... | collective-permute-start | bytes 811016 | tf_op jit(solution)/shard_map/ppermute | solution.py:48
  8.9 1.9 %copy-start.2 = (bf16[2,2,768]{2,1,0:T(2,128)(2,1)S(1)}, bf16[2,2,768]{2,1,0:T(2,128)(2,1)}, u32[]{:S(2)}) copy-start(bf16[2,2,768]{2,1,0:T(2,128)(2,1)} %own_ref.1) | copy-start | bytes 18436
  11.6 10.3 %collective-permute-start.3 = (bf16[21,8,768]{2,1,0:T(8,128)(2,1)S(1)}, bf16[21,8,768]{2,1,0:T(8,128)(2,1)S(1)}, u32[]{:S(2)}, u32[]{:S(2)}) collective-permute-start(bf16[21,8,768]{2,1,0:T(8,128)(2,1)S(1)} %get-tuple-element.40), channel_id=1, source_target_pairs={{0,1},{2,3},{1,0},{3,2},{4,5},{6,7},{5,4},{7,6},{8,9},{10,11},{9,8... | collective-permute-start | bytes 774152 | tf_op jit(solution)/shard_map/ppermute | solution.py:42
  11.8 10.1 %collective-permute-start.4 = (bf16[20,8,768]{2,1,0:T(8,128)(2,1)S(1)}, bf16[20,8,768]{2,1,0:T(8,128)(2,1)S(1)}, u32[]{:S(2)}, u32[]{:S(2)}) collective-permute-start(bf16[20,8,768]{2,1,0:T(8,128)(2,1)S(1)} %get-tuple-element.41), channel_id=1, source_target_pairs={{1,2},{2,1},{5,6},{6,5},{9,10},{10,9},{13,14},{14,13},{17,18},{18,... | collective-permute-start | bytes 737288 | tf_op jit(solution)/shard_map/ppermute | solution.py:42
  16.2 2.8 %copy-start = (bf16[768,576]{0,1:T(8,128)(2,1)S(1)}, bf16[768,576]{0,1:T(8,128)(2,1)}, u32[]{:S(2)}) copy-start(bf16[768,576]{0,1:T(8,128)(2,1)} %param.7) | copy-start | bytes 2654212
  16.2 9.6 %collective-permute-start.10 = (bf16[224,768]{1,0:T(8,128)(2,1)S(1)}, bf16[224,768]{1,0:T(8,128)(2,1)S(1)}, u32[]{:S(2)}, u32[]{:S(2)}) collective-permute-start(bf16[224,768]{1,0:T(8,128)(2,1)S(1)} %get-tuple-element.49), channel_id=1, source_target_pairs={{0,8},{4,12},{8,0},{12,4},{1,9},{5,13},{9,1},{13,5},{2,10},{6,14},... | collective-permute-start | bytes 1032200 | tf_op jit(solution)/shard_map/ppermute | solution.py:48
  21.8 9.1 %copy-start.1 = (bf16[768,192]{0,1:T(8,128)(2,1)S(1)}, bf16[768,192]{0,1:T(8,128)(2,1)}, u32[]{:S(2)}) copy-start(bf16[768,192]{0,1:T(8,128)(2,1)} %param.8) | copy-start | bytes 884740
  21.9 7.0 %collective-permute-start.8 = (bf16[176,768]{1,0:T(8,128)(2,1)S(1)}, bf16[176,768]{1,0:T(8,128)(2,1)S(1)}, u32[]{:S(2)}, u32[]{:S(2)}) collective-permute-start(bf16[176,768]{1,0:T(8,128)(2,1)S(1)} %collective-permute-done.refs_0_), channel_id=1, source_target_pairs={{0,16},{16,0},{1,17},{17,1},{2,18},{18,2},{3,19},{19,3},{4,20},{20... | collective-permute-start | bytes 811016 | tf_op jit(solution)/shard_map/ppermute | solution.py:718
  23.2 2.9 %collective-permute-start.6 = (bf16[8,768]{1,0:T(8,128)(2,1)S(1)}, bf16[8,768]{1,0:T(8,128)(2,1)S(1)}, u32[]{:S(2)}, u32[]{:S(2)}) collective-permute-start(bf16[8,768]{1,0:T(8,128)(2,1)S(1)} %carrier_pair.1.refs_0_), channel_id=1, source_target_pairs={{0,3},{1,2},{2,1},{3,0},{4,7},{5,6},{6,5},{7,4},{8,11},{9,10},{10,... | collective-permute-start | bytes 36872 | tf_op jit(solution)/shard_map/ppermute | solution.py:48
  26.1 6.7 %collective-permute-start.11 = (bf16[224,768]{1,0:T(8,128)(2,1)S(1)}, bf16[224,768]{1,0:T(8,128)(2,1)S(1)}, u32[]{:S(2)}, u32[]{:S(2)}) collective-permute-start(bf16[224,768]{1,0:T(8,128)(2,1)S(1)} %collective-permute-done.10.refs_4_), channel_id=1, source_target_pairs={{0,4},{4,0},{8,12},{12,8},{1,5},{5,1},{9,13},{13,9},{2,6},{6,2},{1... | collective-permute-start | bytes 1032200 | tf_op jit(solution)/shard_map/ppermute | solution.py:48
  28.2 4.6 %collective-permute-start.7 = (bf16[176,768]{1,0:T(8,128)(2,1)S(1)}, bf16[176,768]{1,0:T(8,128)(2,1)S(1)}, u32[]{:S(2)}, u32[]{:S(2)}) collective-permute-start(bf16[176,768]{1,0:T(8,128)(2,1)S(1)} %collective-permute-done.refs_0_), channel_id=1, source_target_pairs={{0,4},{4,0},{8,12},{12,8},{1,5},{5,1},{9,13},{13,9},{2,6},{6,2},{1... | collective-permute-start | bytes 811016 | tf_op jit(solution)/shard_map/ppermute | solution.py:48
  28.9 3.9 %collective-permute-start.9 = (bf16[176,768]{1,0:T(8,128)(2,1)S(1)}, bf16[176,768]{1,0:T(8,128)(2,1)S(1)}, u32[]{:S(2)}, u32[]{:S(2)}) collective-permute-start(bf16[176,768]{1,0:T(8,128)(2,1)S(1)} %collective-permute-done.8.refs_2_), channel_id=1, source_target_pairs={{0,4},{4,0},{8,12},{12,8},{1,5},{5,1},{9,13},{13,9},{2,6},{6,2},{1... | collective-permute-start | bytes 811016 | tf_op jit(solution)/shard_map/ppermute | solution.py:48
  30.9 9.4 %collective-permute-start.13 = (bf16[208,768]{1,0:T(8,128)(2,1)S(1)}, bf16[208,768]{1,0:T(8,128)(2,1)S(1)}, u32[]{:S(2)}, u32[]{:S(2)}) collective-permute-start(bf16[208,768]{1,0:T(8,128)(2,1)S(1)} %final_pack.1.refs_0_), channel_id=1, source_target_pairs={{0,8},{4,12},{8,0},{12,4},{1,9},{5,13},{9,1},{13,5},{2,10},{6,14},... | collective-permute-start | bytes 958472 | tf_op jit(solution)/shard_map/ppermute | solution.py:48
  32.5 10.1 %collective-permute-start.12 = (bf16[208,768]{1,0:T(8,128)(2,1)S(1)}, bf16[208,768]{1,0:T(8,128)(2,1)S(1)}, u32[]{:S(2)}, u32[]{:S(2)}) collective-permute-start(bf16[208,768]{1,0:T(8,128)(2,1)S(1)} %final_pack.1.refs_0_), channel_id=1, source_target_pairs={{0,4},{4,0},{8,12},{12,8},{1,5},{5,1},{9,13},{13,9},{2,6},{6,2},{1... | collective-permute-start | bytes 958472 | tf_op jit(solution)/shard_map/ppermute | solution.py:48
  40.3 2.3 %collective-permute-start.14 = (bf16[208,768]{1,0:T(8,128)(2,1)S(1)}, bf16[208,768]{1,0:T(8,128)(2,1)S(1)}, u32[]{:S(2)}, u32[]{:S(2)}) collective-permute-start(bf16[208,768]{1,0:T(8,128)(2,1)S(1)} %collective-permute-done.13.refs_2_), channel_id=1, source_target_pairs={{0,4},{4,0},{8,12},{12,8},{1,5},{5,1},{9,13},{13,9},{2,6},{6,2},{1... | collective-permute-start | bytes 958472 | tf_op jit(solution)/shard_map/ppermute | solution.py:48

commit v4 on v3

--- a/solution.py
+++ b/solution.py
@@ -785,7 +785,7 @@
             in_specs=[scalars] + [vmem] * 4,
             out_specs=vmem,
             compiler_params=pltpu.CompilerParams(vmem_limit_bytes=VMEM_BYTES),
-            cost_estimate=pl.CostEstimate(flops=3_000_000_000, bytes_accessed=7_000_000, transcendentals=0),
+            cost_estimate=pl.CostEstimate(flops=1_000, bytes_accessed=1_000, transcendentals=0),
             name="values",
         )(place, wt, whole, mid, outer)
 

time: 55.5 us -> 52.9 us (0.953)
  the two profiles are of different devices: /device:TPU:9 before, /device:TPU:0 now
where the time goes in v4:
time: 52.9 us; the launch traced here: 52.5 us
  Pallas kernels  31.5 us (60%)
  starting transfers between devices  17.1 us (32%)
  waiting for transfers between devices  2.71 us (5%)
  between operations  0.99 us (2%)
    ppermute x10, starting transfers between devices, swapped(): return lax.ppermute(block, axis, [(i, i ^ bit) for i in range(count)])  12.3 us
    pallas_call x1, Pallas kernels, local(): pl.pallas_call(functools.partial(attend_kernel, rows // TILE, cols // TIL...  6.87 us
    pallas_call x2, Pallas kernels, values(): pl.pallas_call(functools.partial(value_kernel, first), out_shape=jax.Shap...  3.57 us
    ppermute x4, starting transfers between devices, pair_swapped(): got.append(lax.ppermute(block, axis, pairs + [(b, a) for a, b in pairs]))  3.29 us
    pallas_call x1, Pallas kernels, local(): pl.pallas_call(functools.partial(carrier_kernel, offsets), out_shape=(jax...  3.23 us
    pallas_call x1, Pallas kernels, local(): pl.pallas_call(functools.partial(late_kernel, numbered, triple_t.shape[0]...  3.19 us
    pallas_call x1, Pallas kernels, local(): pl.pallas_call(functools.partial(early_kernel, offsets), out_shape=(pltpu...  2.85 us
    ppermute x10, waiting for transfers between devices, swapped(): return lax.ppermute(block, axis, [(i, i ^ bit) for i in range(count)])  2.45 us
  transfers between devices with their start and end apart: 15, of which 5 were waited for; matrix products, arithmetic and copies ran while one was open for 0% of the time, Pallas kernels for 36%

profile of v4, /device:TPU:0, one launch (start us, length us, event | category | flops | bytes accessed | tf_op | source)
XLA Modules:
  0.0 52.5 jit_solution(16121397283254543706)
XLA Ops:
  0.6 0.5 collective-permute-start.5
  1.1 0.1 stack.67.place_ref
  1.2 2.1 %edge_rows.1 = (bf16[32,32,128]{2,1,0:T(8,128)(2,1)S(1)}, bf16[4,32,768]{2,1,0:T(8,128)(2,1)S(1)}, bf16[4,32,768]{2,1,0:T(8,128)(2,1)S(1)}, bf16[32,32,768]{2,1,0:T(8,128)(2,1)S(1)}) custom-call(s32[11]{0:T(128)S(1)} %stack.67.place_ref, s32[32,32]{1,0:T(8,128)} %flags_hbm.1, bf16[32,32,768]{2,1,0:T(8,128)(2,1)} %x_hbm.1), custom_call_target="tpu_custom_call" | custom-call | flops 1000000 | bytes 1000000 | tf_op jit(solution)/shard_map/edge_rows/pallas_call | solution.py:604
  3.3 0.1 collective-permute-start.1
  3.5 0.7 %collective-permute-start.2 = (bf16[4,32,768]{2,1,0:T(8,128)(2,1)S(1)}, bf16[4,32,768]{2,1,0:T(8,128)(2,1)S(1)}, u32[]{:S(2)}, u32[]{:S(2)}) collective-permute-start(bf16[4,32,768]{2,1,0:T(8,128)(2,1)S(1)} %get-tuple-element.39), channel_id=1, source_target_pairs={{4,8},{8,4},{5,9},{9,5},{6,10},{10,6},{7,11},{11,7},{20,24},{24,20... | collective-permute-start | bytes 589832 | tf_op jit(solution)/shard_map/ppermute | solution.py:42
  4.1 1.6 %pieces.1 = (bf16[176,768]{1,0:T(8,128)(2,1)S(1)}, bf16[224,768]{1,0:T(8,128)(2,1)S(1)}) custom-call(s32[11]{0:T(128)S(1)} %stack.67.place_ref, bf16[576,768]{1,0:T(8,128)(2,1)} %bitcast.13), custom_call_target="tpu_custom_call" | custom-call | flops 1000000 | bytes 1000000 | tf_op jit(solution)/shard_map/pieces/pallas_call | solution.py:623
  5.8 4.3 %collective-permute-start = (bf16[176,768]{1,0:T(8,128)(2,1)S(1)}, bf16[176,768]{1,0:T(8,128)(2,1)S(1)}, u32[]{:S(2)}, u32[]{:S(2)}) collective-permute-start(bf16[176,768]{1,0:T(8,128)(2,1)S(1)} %get-tuple-element.36), channel_id=1, source_target_pairs={{0,8},{4,12},{8,0},{12,4},{1,9},{5,13},{9,1},{13,5},{2,10},{6,14},... | collective-permute-start | bytes 811016 | tf_op jit(solution)/shard_map/ppermute | solution.py:48
  10.0 1.8 %own_norm.1.xq_ref.refs_2_.refs_9_ = bf16[1024,768]{1,0:T(8,128)(2,1)S(1)} custom-call(bf16[32,32,768]{2,1,0:T(8,128)(2,1)S(1)} %get-tuple-element.33.x_ref), custom_call_target="tpu_custom_call" | custom-call | flops 1000000 | bytes 1000000 | tf_op jit(solution)/shard_map/own_norm/pallas_call | solution.py:636
  11.9 0.9 %edge_columns.1 = (bf16[21,8,768]{2,1,0:T(8,128)(2,1)S(1)}, bf16[20,8,768]{2,1,0:T(8,128)(2,1)S(1)}) custom-call(s32[11]{0:T(128)S(1)} %stack.67.place_ref, bf16[32,32,768]{2,1,0:T(8,128)(2,1)S(1)} %get-tuple-element.33.x_ref, bf16[32,32,128]{2,1,0:T(8,128)(2,1)S(1)} %get-tuple-element.38.mark_ref, ...), custom_call_target="tpu_custom_call" | custom-call | flops 1000000 | bytes 2000000 | tf_op jit(solution)/shard_map/edge_columns/pallas_call | solution.py:654
  12.8 1.8 %collective-permute-start.3 = (bf16[21,8,768]{2,1,0:T(8,128)(2,1)S(1)}, bf16[21,8,768]{2,1,0:T(8,128)(2,1)S(1)}, u32[]{:S(2)}, u32[]{:S(2)}) collective-permute-start(bf16[21,8,768]{2,1,0:T(8,128)(2,1)S(1)} %get-tuple-element.40), channel_id=1, source_target_pairs={{0,1},{2,3},{1,0},{3,2},{4,5},{6,7},{5,4},{7,6},{8,9},{10,11},{9,8... | collective-permute-start | bytes 774152 | tf_op jit(solution)/shard_map/ppermute | solution.py:42
  14.6 0.7 %collective-permute-start.4 = (bf16[20,8,768]{2,1,0:T(8,128)(2,1)S(1)}, bf16[20,8,768]{2,1,0:T(8,128)(2,1)S(1)}, u32[]{:S(2)}, u32[]{:S(2)}) collective-permute-start(bf16[20,8,768]{2,1,0:T(8,128)(2,1)S(1)} %get-tuple-element.41), channel_id=1, source_target_pairs={{1,2},{2,1},{5,6},{6,5},{9,10},{10,9},{13,14},{14,13},{17,18},{18,... | collective-permute-start | bytes 737288 | tf_op jit(solution)/shard_map/ppermute | solution.py:42
  15.3 1.4 %collective-permute-start.10 = (bf16[224,768]{1,0:T(8,128)(2,1)S(1)}, bf16[224,768]{1,0:T(8,128)(2,1)S(1)}, u32[]{:S(2)}, u32[]{:S(2)}) collective-permute-start(bf16[224,768]{1,0:T(8,128)(2,1)S(1)} %get-tuple-element.49), channel_id=1, source_target_pairs={{0,8},{4,12},{8,0},{12,4},{1,9},{5,13},{9,1},{13,5},{2,10},{6,14},... | collective-permute-start | bytes 1032200 | tf_op jit(solution)/shard_map/ppermute | solution.py:48
  16.7 1.3 %middle_blocks.1.refs_3_.refs_10_.mid_ref = bf16[960,768]{1,0:T(8,128)(2,1)S(1)} custom-call(s32[11]{0:T(128)S(1)} %stack.67.place_ref, bf16[1024,768]{1,0:T(8,128)(2,1)S(1)} %own_norm.1.xq_ref.refs_2_.refs_9_, bf16[4,32,768]{2,1,0:T(8,128)(2,1)S(1)} %collective-permute-done.1.even_rows_ref, bf16[4,32,768]{2,1,0:T(8,128)(2,1)S(1)} %collective-permute-done.2.odd_rows_ref), custom_call_target="tpu_custom_call" | custom-call | flops 1000000 | bytes 1000000 | tf_op jit(solution)/shard_map/middle_blocks/pallas_call | solution.py:673
  18.0 2.9 %project_early.1 = (bf16[4,1024,256]{2,1,0:T(8,128)(2,1)S(1)}, bf16[960,128]{1,0:T(8,128)(2,1)S(1)}, bf16[1152,768]{1,0:T(8,128)(2,1)S(1)}) custom-call(s32[11]{0:T(128)S(1)} %stack.67.place_ref, bf16[576,768]{1,0:T(8,128)(2,1)S(1)} %bitcast.14, bf16[576,768]{1,0:T(8,128)(2,1)S(1)} %collective-permute-done.5.refs_1_, ...), custom_call_target="tpu_custom_call" | custom-call | flops 1000000 | bytes 1000000 | tf_op jit(solution)/shard_map/project_early/pallas_call | solution.py:683
  20.8 0.2 collective-permute-done.3.got_hbm.even_cols_ref
  21.1 1.6 %collective-permute-start.8 = (bf16[176,768]{1,0:T(8,128)(2,1)S(1)}, bf16[176,768]{1,0:T(8,128)(2,1)S(1)}, u32[]{:S(2)}, u32[]{:S(2)}) collective-permute-start(bf16[176,768]{1,0:T(8,128)(2,1)S(1)} %collective-permute-done.refs_0_), channel_id=1, source_target_pairs={{0,16},{16,0},{1,17},{17,1},{2,18},{18,2},{3,19},{19,3},{4,20},{20... | collective-permute-start | bytes 811016 | tf_op jit(solution)/shard_map/ppermute | solution.py:718
  22.7 3.6 %collective-permute-start.6 = (bf16[8,768]{1,0:T(8,128)(2,1)S(1)}, bf16[8,768]{1,0:T(8,128)(2,1)S(1)}, u32[]{:S(2)}, u32[]{:S(2)}) collective-permute-start(bf16[8,768]{1,0:T(8,128)(2,1)S(1)} %carrier_pair.1.refs_0_), channel_id=1, source_target_pairs={{0,3},{1,2},{2,1},{3,0},{4,7},{5,6},{6,5},{7,4},{8,11},{9,10},{10,... | collective-permute-start | bytes 36872 | tf_op jit(solution)/shard_map/ppermute | solution.py:48
  26.3 1.8 %outer_blocks.1 = (bf16[640,768]{1,0:T(8,128)(2,1)S(1)}, f32[16,8,256]{2,1,0:T(8,128)S(1)}) custom-call(s32[11]{0:T(128)S(1)} %stack.67.place_ref, bf16[1024,768]{1,0:T(8,128)(2,1)S(1)} %own_norm.1.xq_ref.refs_2_.refs_9_, bf16[32,32,128]{2,1,0:T(8,128)(2,1)S(1)} %get-tuple-element.38.mark_ref, bf16[4,32,768]{2,1,0:T(8,128)(2,1)S(1)} %collective-permute-done.1.even_rows_ref, ...), custom_call_target="tpu_custom_call" | custom-call | flops 10000000 | bytes 6000000 | tf_op jit(solution)/shard_map/outer_blocks/pallas_call | solution.py:724
  28.1 0.1 collective-permute-done.6.refs_1_
  28.2 1.8 %collective-permute-start.13 = (bf16[208,768]{1,0:T(8,128)(2,1)S(1)}, bf16[208,768]{1,0:T(8,128)(2,1)S(1)}, u32[]{:S(2)}, u32[]{:S(2)}) collective-permute-start(bf16[208,768]{1,0:T(8,128)(2,1)S(1)} %final_pack.1.refs_0_), channel_id=1, source_target_pairs={{0,8},{4,12},{8,0},{12,4},{1,9},{5,13},{9,1},{13,5},{2,10},{6,14},... | collective-permute-start | bytes 958472 | tf_op jit(solution)/shard_map/ppermute | solution.py:48
  30.0 0.2 collective-permute-start.7
  30.2 0.3 collective-permute-start.9
  30.5 0.2 collective-permute-start.12
  30.7 0.8 %collective-permute-done.7.refs_1_ = bf16[176,768]{1,0:T(8,128)(2,1)S(1)} collective-permute-done((bf16[176,768]{1,0:T(8,128)(2,1)S(1)}, bf16[176,768]{1,0:T(8,128)(2,1)S(1)}, u32[]{:S(2)}, u32[]{:S(2)}) %collective-permute-start.7) | collective-permute-done | bytes 270368 | tf_op jit(solution)/shard_map/ppermute | solution.py:48
  31.6 0.4 collective-permute-done.9.refs_3_
  31.9 3.2 %project_late.1 = (bf16[3,1024,256]{2,1,0:T(8,128)(2,1)S(1)}, bf16[3,1600,256]{2,1,0:T(8,128)(2,1)S(1)}, bf16[2304,768]{1,0:T(8,128)(2,1)S(1)}) custom-call(s32[11]{0:T(128)S(1)} %stack.67.place_ref, bf16[176,768]{1,0:T(8,128)(2,1)S(1)} %collective-permute-done.refs_0_, bf16[176,768]{1,0:T(8,128)(2,1)S(1)} %collective-permute-done.7.refs_1_, ...), custom_call_target="tpu_custom_call" | custom-call | flops 1000000 | bytes 1000000 | tf_op jit(solution)/shard_map/project_late/pallas_call | solution.py:766
  35.1 2.0 %values.2.v_low = bf16[2,1600,256]{2,1,0:T(8,128)(2,1)S(1)} custom-call(s32[11]{0:T(128)S(1)} %stack.67.place_ref, bf16[2304,768]{1,0:T(8,128)(2,1)S(1)} %get-tuple-element.56.wt, bf16[4,1024,256]{2,1,0:T(8,128)(2,1)S(1)} %get-tuple-element.51.refs_7_.whole_ref, bf16[960,768]{1,0:T(8,128)(2,1)S(1)} %middle_blocks.1.refs_3_.refs_10_.mid_ref, ...), custom_call_target="tpu_custom_call" | custom-call | flops 1000 | bytes 1000 | tf_op jit(solution)/shard_map/values/pallas_call | solution.py:782
  37.2 1.1 %collective-permute-done.13.refs_2_ = bf16[208,768]{1,0:T(8,128)(2,1)S(1)} collective-permute-done((bf16[208,768]{1,0:T(8,128)(2,1)S(1)}, bf16[208,768]{1,0:T(8,128)(2,1)S(1)}, u32[]{:S(2)}, u32[]{:S(2)}) %collective-permute-start.13) | collective-permute-done | bytes 319520 | tf_op jit(solution)/shard_map/ppermute | solution.py:48
  38.2 1.6 %values.3.v_high = bf16[1,1600,256]{2,1,0:T(8,128)(2,1)S(1)} custom-call(s32[11]{0:T(128)S(1)} %stack.67.place_ref, bf16[2304,768]{1,0:T(8,128)(2,1)S(1)} %get-tuple-element.56.wt, bf16[4,1024,256]{2,1,0:T(8,128)(2,1)S(1)} %get-tuple-element.51.refs_7_.whole_ref, bf16[960,768]{1,0:T(8,128)(2,1)S(1)} %middle_blocks.1.refs_3_.refs_10_.mid_ref, ...), custom_call_target="tpu_custom_call" | custom-call | flops 1000 | bytes 1000 | tf_op jit(solution)/shard_map/values/pallas_call | solution.py:782
  39.9 3.2 %carriers.1 = (bf16[2,2,768]{2,1,0:T(2,128)(2,1)}, bf16[768,768]{1,0:T(8,128)(2,1)S(1)}, bf16[12,256,256]{2,1,0:T(8,128)(2,1)S(1)}, f32[8,768]{1,0:T(8,128)S(1)}) custom-call(s32[11]{0:T(128)S(1)} %stack.67.place_ref, bf16[2304,768]{1,0:T(8,128)(2,1)S(1)} %get-tuple-element.56.wt, bf16[208,768]{1,0:T(8,128)(2,1)S(1)} %final_pack.1.refs_0_, ...), custom_call_target="tpu_custom_call" | custom-call | flops 500000000 | bytes 5000000 | tf_op jit(solution)/shard_map/carriers/pallas_call | solution.py:801
  43.1 6.9 %attend.1.mix_s = bf16[1024,768]{1,0:T(8,128)(2,1)S(1)} custom-call(bf16[3,1024,256]{2,1,0:T(8,128)(2,1)S(1)} %get-tuple-element.53.q_s, bf16[3,1600,256]{2,1,0:T(8,128)(2,1)S(1)} %get-tuple-element.54.k_s, bf16[2,1600,256]{2,1,0:T(8,128)(2,1)S(1)} %values.2.v_low, bf16[1,1600,256]{2,1,0:T(8,128)(2,1)S(1)} %values.3.v_high, ...), custom_call_target="tpu_custom_call" | custom-call | flops 4000000000 | bytes 12000000 | tf_op jit(solution)/shard_map/attend/pallas_call | solution.py:817
  50.0 2.4 %out.1 = bf16[32,32,768]{2,1,0:T(8,128)(2,1)} custom-call(bf16[32,32,768]{2,1,0:T(8,128)(2,1)S(1)} %get-tuple-element.33.x_ref, bf16[1024,768]{1,0:T(8,128)(2,1)S(1)} %attend.1.mix_s, bf16[768,768]{1,0:T(8,128)(2,1)S(1)} %get-tuple-element.62.wo), custom_call_target="tpu_custom_call" | custom-call | flops 1200000000 | bytes 6000000 | tf_op jit(solution)/shard_map/out/pallas_call | solution.py:832
  (20 shorter events, 0.1 us)
Async XLA Ops:
  0.6 17.3 %collective-permute-start.5 = (bf16[576,768]{1,0:T(8,128)(2,1)}, bf16[576,768]{1,0:T(8,128)(2,1)S(1)}, u32[]{:S(2)}, u32[]{:S(2)}) collective-permute-start(bf16[576,768]{1,0:T(8,128)(2,1)} %bitcast.12), channel_id=1, source_target_pairs={{0,4},{4,0},{8,12},{12,8},{1,5},{5,1},{9,13},{13,9},{2,6},{6,2},{1... | collective-permute-start | bytes 2654216 | tf_op jit(solution)/shard_map/ppermute | solution.py:48
  3.3 8.5 %collective-permute-start.1 = (bf16[4,32,768]{2,1,0:T(8,128)(2,1)S(1)}, bf16[4,32,768]{2,1,0:T(8,128)(2,1)S(1)}, u32[]{:S(2)}, u32[]{:S(2)}) collective-permute-start(bf16[4,32,768]{2,1,0:T(8,128)(2,1)S(1)} %get-tuple-element.34), channel_id=1, source_target_pairs={{0,4},{8,12},{4,0},{12,8},{1,5},{9,13},{5,1},{13,9},{2,6},{10,14},... | collective-permute-start | bytes 589832 | tf_op jit(solution)/shard_map/ppermute | solution.py:42
  3.5 8.4 %collective-permute-start.2 = (bf16[4,32,768]{2,1,0:T(8,128)(2,1)S(1)}, bf16[4,32,768]{2,1,0:T(8,128)(2,1)S(1)}, u32[]{:S(2)}, u32[]{:S(2)}) collective-permute-start(bf16[4,32,768]{2,1,0:T(8,128)(2,1)S(1)} %get-tuple-element.39), channel_id=1, source_target_pairs={{4,8},{8,4},{5,9},{9,5},{6,10},{10,6},{7,11},{11,7},{20,24},{24,20... | collective-permute-start | bytes 589832 | tf_op jit(solution)/shard_map/ppermute | solution.py:42
  5.8 15.3 %collective-permute-start = (bf16[176,768]{1,0:T(8,128)(2,1)S(1)}, bf16[176,768]{1,0:T(8,128)(2,1)S(1)}, u32[]{:S(2)}, u32[]{:S(2)}) collective-permute-start(bf16[176,768]{1,0:T(8,128)(2,1)S(1)} %get-tuple-element.36), channel_id=1, source_target_pairs={{0,8},{4,12},{8,0},{12,4},{1,9},{5,13},{9,1},{13,5},{2,10},{6,14},... | collective-permute-start | bytes 811016 | tf_op jit(solution)/shard_map/ppermute | solution.py:48
  10.0 1.8 %copy-start.2 = (bf16[2,2,768]{2,1,0:T(2,128)(2,1)S(1)}, bf16[2,2,768]{2,1,0:T(2,128)(2,1)}, u32[]{:S(2)}) copy-start(bf16[2,2,768]{2,1,0:T(2,128)(2,1)} %own_ref.1) | copy-start | bytes 18436
  12.8 8.3 %collective-permute-start.3 = (bf16[21,8,768]{2,1,0:T(8,128)(2,1)S(1)}, bf16[21,8,768]{2,1,0:T(8,128)(2,1)S(1)}, u32[]{:S(2)}, u32[]{:S(2)}) collective-permute-start(bf16[21,8,768]{2,1,0:T(8,128)(2,1)S(1)} %get-tuple-element.40), channel_id=1, source_target_pairs={{0,1},{2,3},{1,0},{3,2},{4,5},{6,7},{5,4},{7,6},{8,9},{10,11},{9,8... | collective-permute-start | bytes 774152 | tf_op jit(solution)/shard_map/ppermute | solution.py:42
  14.6 6.6 %collective-permute-start.4 = (bf16[20,8,768]{2,1,0:T(8,128)(2,1)S(1)}, bf16[20,8,768]{2,1,0:T(8,128)(2,1)S(1)}, u32[]{:S(2)}, u32[]{:S(2)}) collective-permute-start(bf16[20,8,768]{2,1,0:T(8,128)(2,1)S(1)} %get-tuple-element.41), channel_id=1, source_target_pairs={{1,2},{2,1},{5,6},{6,5},{9,10},{10,9},{13,14},{14,13},{17,18},{18,... | collective-permute-start | bytes 737288 | tf_op jit(solution)/shard_map/ppermute | solution.py:42
  15.2 2.7 %copy-start = (bf16[768,576]{0,1:T(8,128)(2,1)S(1)}, bf16[768,576]{0,1:T(8,128)(2,1)}, u32[]{:S(2)}) copy-start(bf16[768,576]{0,1:T(8,128)(2,1)} %param.7) | copy-start | bytes 2654212
  15.3 12.8 %collective-permute-start.10 = (bf16[224,768]{1,0:T(8,128)(2,1)S(1)}, bf16[224,768]{1,0:T(8,128)(2,1)S(1)}, u32[]{:S(2)}, u32[]{:S(2)}) collective-permute-start(bf16[224,768]{1,0:T(8,128)(2,1)S(1)} %get-tuple-element.49), channel_id=1, source_target_pairs={{0,8},{4,12},{8,0},{12,4},{1,9},{5,13},{9,1},{13,5},{2,10},{6,14},... | collective-permute-start | bytes 1032200 | tf_op jit(solution)/shard_map/ppermute | solution.py:48
  20.8 7.4 %copy-start.1 = (bf16[768,192]{0,1:T(8,128)(2,1)S(1)}, bf16[768,192]{0,1:T(8,128)(2,1)}, u32[]{:S(2)}) copy-start(bf16[768,192]{0,1:T(8,128)(2,1)} %param.8) | copy-start | bytes 884740
  21.1 9.1 %collective-permute-start.8 = (bf16[176,768]{1,0:T(8,128)(2,1)S(1)}, bf16[176,768]{1,0:T(8,128)(2,1)S(1)}, u32[]{:S(2)}, u32[]{:S(2)}) collective-permute-start(bf16[176,768]{1,0:T(8,128)(2,1)S(1)} %collective-permute-done.refs_0_), channel_id=1, source_target_pairs={{0,16},{16,0},{1,17},{17,1},{2,18},{18,2},{3,19},{19,3},{4,20},{20... | collective-permute-start | bytes 811016 | tf_op jit(solution)/shard_map/ppermute | solution.py:718
  22.7 5.5 %collective-permute-start.6 = (bf16[8,768]{1,0:T(8,128)(2,1)S(1)}, bf16[8,768]{1,0:T(8,128)(2,1)S(1)}, u32[]{:S(2)}, u32[]{:S(2)}) collective-permute-start(bf16[8,768]{1,0:T(8,128)(2,1)S(1)} %carrier_pair.1.refs_0_), channel_id=1, source_target_pairs={{0,3},{1,2},{2,1},{3,0},{4,7},{5,6},{6,5},{7,4},{8,11},{9,10},{10,... | collective-permute-start | bytes 36872 | tf_op jit(solution)/shard_map/ppermute | solution.py:48
  28.2 3.4 %collective-permute-start.11 = (bf16[224,768]{1,0:T(8,128)(2,1)S(1)}, bf16[224,768]{1,0:T(8,128)(2,1)S(1)}, u32[]{:S(2)}, u32[]{:S(2)}) collective-permute-start(bf16[224,768]{1,0:T(8,128)(2,1)S(1)} %collective-permute-done.10.refs_4_), channel_id=1, source_target_pairs={{0,4},{4,0},{8,12},{12,8},{1,5},{5,1},{9,13},{13,9},{2,6},{6,2},{1... | collective-permute-start | bytes 1032200 | tf_op jit(solution)/shard_map/ppermute | solution.py:48
  28.2 10.0 %collective-permute-start.13 = (bf16[208,768]{1,0:T(8,128)(2,1)S(1)}, bf16[208,768]{1,0:T(8,128)(2,1)S(1)}, u32[]{:S(2)}, u32[]{:S(2)}) collective-permute-start(bf16[208,768]{1,0:T(8,128)(2,1)S(1)} %final_pack.1.refs_0_), channel_id=1, source_target_pairs={{0,8},{4,12},{8,0},{12,4},{1,9},{5,13},{9,1},{13,5},{2,10},{6,14},... | collective-permute-start | bytes 958472 | tf_op jit(solution)/shard_map/ppermute | solution.py:48
  30.0 1.5 %collective-permute-start.7 = (bf16[176,768]{1,0:T(8,128)(2,1)S(1)}, bf16[176,768]{1,0:T(8,128)(2,1)S(1)}, u32[]{:S(2)}, u32[]{:S(2)}) collective-permute-start(bf16[176,768]{1,0:T(8,128)(2,1)S(1)} %collective-permute-done.refs_0_), channel_id=1, source_target_pairs={{0,4},{4,0},{8,12},{12,8},{1,5},{5,1},{9,13},{13,9},{2,6},{6,2},{1... | collective-permute-start | bytes 811016 | tf_op jit(solution)/shard_map/ppermute | solution.py:48
  30.2 1.7 %collective-permute-start.9 = (bf16[176,768]{1,0:T(8,128)(2,1)S(1)}, bf16[176,768]{1,0:T(8,128)(2,1)S(1)}, u32[]{:S(2)}, u32[]{:S(2)}) collective-permute-start(bf16[176,768]{1,0:T(8,128)(2,1)S(1)} %collective-permute-done.8.refs_2_), channel_id=1, source_target_pairs={{0,4},{4,0},{8,12},{12,8},{1,5},{5,1},{9,13},{13,9},{2,6},{6,2},{1... | collective-permute-start | bytes 811016 | tf_op jit(solution)/shard_map/ppermute | solution.py:48
  30.5 9.3 %collective-permute-start.12 = (bf16[208,768]{1,0:T(8,128)(2,1)S(1)}, bf16[208,768]{1,0:T(8,128)(2,1)S(1)}, u32[]{:S(2)}, u32[]{:S(2)}) collective-permute-start(bf16[208,768]{1,0:T(8,128)(2,1)S(1)} %final_pack.1.refs_0_), channel_id=1, source_target_pairs={{0,4},{4,0},{8,12},{12,8},{1,5},{5,1},{9,13},{13,9},{2,6},{6,2},{1... | collective-permute-start | bytes 958472 | tf_op jit(solution)/shard_map/ppermute | solution.py:48
  38.2 1.6 %collective-permute-start.14 = (bf16[208,768]{1,0:T(8,128)(2,1)S(1)}, bf16[208,768]{1,0:T(8,128)(2,1)S(1)}, u32[]{:S(2)}, u32[]{:S(2)}) collective-permute-start(bf16[208,768]{1,0:T(8,128)(2,1)S(1)} %collective-permute-done.13.refs_2_), channel_id=1, source_target_pairs={{0,4},{4,0},{8,12},{12,8},{1,5},{5,1},{9,13},{13,9},{2,6},{6,2},{1... | collective-permute-start | bytes 958472 | tf_op jit(solution)/shard_map/ppermute | solution.py:48

commit v5 on v4

--- a/solution.py
+++ b/solution.py
@@ -557,7 +557,7 @@
         finish(t + 1, odd_s)
         return 0
 
-    lax.fori_loop(0, tiles // 2, two, 0)
+    lax.fori_loop(0, tiles // 2, two, 0, unroll=2)
 
 
 def out_kernel(x_ref, mix_s, wo, out_hbm, out_ref, out_sems):

time: 52.9 us -> 52 us (0.983)
  Pallas kernels: 31.5 us -> 30.6 us
    pallas_call x1, Pallas kernels: 6.87 us -> 5.98 us  [local(): pl.pallas_call(functools.partial(attend_kernel, rows // TILE, cols // TIL...]
  transfers between devices with their start and end apart: 15 -> 15, of which waited for: 5 -> 5; matrix products, arithmetic and copies ran while one was open for 0% -> 0% of each run, Pallas kernels for 36% -> 37%
where the time goes in v5:
time: 52 us; the launch traced here: 51.6 us
  Pallas kernels  30.6 us (59%)
  starting transfers between devices  17.1 us (33%)
  waiting for transfers between devices  2.71 us (5%)
  between operations  0.99 us (2%)
    ppermute x10, starting transfers between devices, swapped(): return lax.ppermute(block, axis, [(i, i ^ bit) for i in range(count)])  12.3 us
    pallas_call x1, Pallas kernels, local(): pl.pallas_call(functools.partial(attend_kernel, rows // TILE, cols // TIL...  5.98 us
    pallas_call x2, Pallas kernels, values(): pl.pallas_call(functools.partial(value_kernel, first), out_shape=jax.Shap...  3.57 us
    ppermute x4, starting transfers between devices, pair_swapped(): got.append(lax.ppermute(block, axis, pairs + [(b, a) for a, b in pairs]))  3.29 us
    pallas_call x1, Pallas kernels, local(): pl.pallas_call(functools.partial(carrier_kernel, offsets), out_shape=(jax...  3.23 us
    pallas_call x1, Pallas kernels, local(): pl.pallas_call(functools.partial(late_kernel, numbered, triple_t.shape[0]...  3.19 us
    pallas_call x1, Pallas kernels, local(): pl.pallas_call(functools.partial(early_kernel, offsets), out_shape=(pltpu...  2.85 us
    ppermute x10, waiting for transfers between devices, swapped(): return lax.ppermute(block, axis, [(i, i ^ bit) for i in range(count)])  2.45 us
  transfers between devices with their start and end apart: 15, of which 5 were waited for; matrix products, arithmetic and copies ran while one was open for 0% of the time, Pallas kernels for 37%

profile of v5, /device:TPU:0, one launch (start us, length us, event | category | flops | bytes accessed | tf_op | source)
XLA Modules:
  0.0 51.6 jit_solution(9259957959963390734)
XLA Ops:
  0.6 0.5 %collective-permute-start.5 = (bf16[576,768]{1,0:T(8,128)(2,1)}, bf16[576,768]{1,0:T(8,128)(2,1)S(1)}, u32[]{:S(2)}, u32[]{:S(2)}) collective-permute-start(bf16[576,768]{1,0:T(8,128)(2,1)} %bitcast.12), channel_id=1, source_target_pairs={{0,4},{4,0},{8,12},{12,8},{1,5},{5,1},{9,13},{13,9},{2,6},{6,2},{1... | collective-permute-start | bytes 2654216 | tf_op jit(solution)/shard_map/ppermute | solution.py:48
  1.1 0.1 stack.67.place_ref
  1.2 2.1 %edge_rows.1 = (bf16[32,32,128]{2,1,0:T(8,128)(2,1)S(1)}, bf16[4,32,768]{2,1,0:T(8,128)(2,1)S(1)}, bf16[4,32,768]{2,1,0:T(8,128)(2,1)S(1)}, bf16[32,32,768]{2,1,0:T(8,128)(2,1)S(1)}) custom-call(s32[11]{0:T(128)S(1)} %stack.67.place_ref, s32[32,32]{1,0:T(8,128)} %flags_hbm.1, bf16[32,32,768]{2,1,0:T(8,128)(2,1)} %x_hbm.1), custom_call_target="tpu_custom_call" | custom-call | flops 1000000 | bytes 1000000 | tf_op jit(solution)/shard_map/edge_rows/pallas_call | solution.py:604
  3.3 0.1 collective-permute-start.1
  3.5 0.7 %collective-permute-start.2 = (bf16[4,32,768]{2,1,0:T(8,128)(2,1)S(1)}, bf16[4,32,768]{2,1,0:T(8,128)(2,1)S(1)}, u32[]{:S(2)}, u32[]{:S(2)}) collective-permute-start(bf16[4,32,768]{2,1,0:T(8,128)(2,1)S(1)} %get-tuple-element.39), channel_id=1, source_target_pairs={{4,8},{8,4},{5,9},{9,5},{6,10},{10,6},{7,11},{11,7},{20,24},{24,20... | collective-permute-start | bytes 589832 | tf_op jit(solution)/shard_map/ppermute | solution.py:42
  4.1 1.6 %pieces.1 = (bf16[176,768]{1,0:T(8,128)(2,1)S(1)}, bf16[224,768]{1,0:T(8,128)(2,1)S(1)}) custom-call(s32[11]{0:T(128)S(1)} %stack.67.place_ref, bf16[576,768]{1,0:T(8,128)(2,1)} %bitcast.13), custom_call_target="tpu_custom_call" | custom-call | flops 1000000 | bytes 1000000 | tf_op jit(solution)/shard_map/pieces/pallas_call | solution.py:623
  5.8 4.3 %collective-permute-start = (bf16[176,768]{1,0:T(8,128)(2,1)S(1)}, bf16[176,768]{1,0:T(8,128)(2,1)S(1)}, u32[]{:S(2)}, u32[]{:S(2)}) collective-permute-start(bf16[176,768]{1,0:T(8,128)(2,1)S(1)} %get-tuple-element.36), channel_id=1, source_target_pairs={{0,8},{4,12},{8,0},{12,4},{1,9},{5,13},{9,1},{13,5},{2,10},{6,14},... | collective-permute-start | bytes 811016 | tf_op jit(solution)/shard_map/ppermute | solution.py:48
  10.0 1.8 %own_norm.1.xq_ref.refs_2_.refs_9_ = bf16[1024,768]{1,0:T(8,128)(2,1)S(1)} custom-call(bf16[32,32,768]{2,1,0:T(8,128)(2,1)S(1)} %get-tuple-element.33.x_ref), custom_call_target="tpu_custom_call" | custom-call | flops 1000000 | bytes 1000000 | tf_op jit(solution)/shard_map/own_norm/pallas_call | solution.py:636
  11.9 0.9 %edge_columns.1 = (bf16[21,8,768]{2,1,0:T(8,128)(2,1)S(1)}, bf16[20,8,768]{2,1,0:T(8,128)(2,1)S(1)}) custom-call(s32[11]{0:T(128)S(1)} %stack.67.place_ref, bf16[32,32,768]{2,1,0:T(8,128)(2,1)S(1)} %get-tuple-element.33.x_ref, bf16[32,32,128]{2,1,0:T(8,128)(2,1)S(1)} %get-tuple-element.38.mark_ref, ...), custom_call_target="tpu_custom_call" | custom-call | flops 1000000 | bytes 2000000 | tf_op jit(solution)/shard_map/edge_columns/pallas_call | solution.py:654
  12.8 1.8 %collective-permute-start.3 = (bf16[21,8,768]{2,1,0:T(8,128)(2,1)S(1)}, bf16[21,8,768]{2,1,0:T(8,128)(2,1)S(1)}, u32[]{:S(2)}, u32[]{:S(2)}) collective-permute-start(bf16[21,8,768]{2,1,0:T(8,128)(2,1)S(1)} %get-tuple-element.40), channel_id=1, source_target_pairs={{0,1},{2,3},{1,0},{3,2},{4,5},{6,7},{5,4},{7,6},{8,9},{10,11},{9,8... | collective-permute-start | bytes 774152 | tf_op jit(solution)/shard_map/ppermute | solution.py:42
  14.6 0.7 %collective-permute-start.4 = (bf16[20,8,768]{2,1,0:T(8,128)(2,1)S(1)}, bf16[20,8,768]{2,1,0:T(8,128)(2,1)S(1)}, u32[]{:S(2)}, u32[]{:S(2)}) collective-permute-start(bf16[20,8,768]{2,1,0:T(8,128)(2,1)S(1)} %get-tuple-element.41), channel_id=1, source_target_pairs={{1,2},{2,1},{5,6},{6,5},{9,10},{10,9},{13,14},{14,13},{17,18},{18,... | collective-permute-start | bytes 737288 | tf_op jit(solution)/shard_map/ppermute | solution.py:42
  15.3 1.4 %collective-permute-start.10 = (bf16[224,768]{1,0:T(8,128)(2,1)S(1)}, bf16[224,768]{1,0:T(8,128)(2,1)S(1)}, u32[]{:S(2)}, u32[]{:S(2)}) collective-permute-start(bf16[224,768]{1,0:T(8,128)(2,1)S(1)} %get-tuple-element.49), channel_id=1, source_target_pairs={{0,8},{4,12},{8,0},{12,4},{1,9},{5,13},{9,1},{13,5},{2,10},{6,14},... | collective-permute-start | bytes 1032200 | tf_op jit(solution)/shard_map/ppermute | solution.py:48
  16.7 1.3 %middle_blocks.1.refs_3_.refs_10_.mid_ref = bf16[960,768]{1,0:T(8,128)(2,1)S(1)} custom-call(s32[11]{0:T(128)S(1)} %stack.67.place_ref, bf16[1024,768]{1,0:T(8,128)(2,1)S(1)} %own_norm.1.xq_ref.refs_2_.refs_9_, bf16[4,32,768]{2,1,0:T(8,128)(2,1)S(1)} %collective-permute-done.1.even_rows_ref, bf16[4,32,768]{2,1,0:T(8,128)(2,1)S(1)} %collective-permute-done.2.odd_rows_ref), custom_call_target="tpu_custom_call" | custom-call | flops 1000000 | bytes 1000000 | tf_op jit(solution)/shard_map/middle_blocks/pallas_call | solution.py:673
  18.0 2.9 %project_early.1 = (bf16[4,1024,256]{2,1,0:T(8,128)(2,1)S(1)}, bf16[960,128]{1,0:T(8,128)(2,1)S(1)}, bf16[1152,768]{1,0:T(8,128)(2,1)S(1)}) custom-call(s32[11]{0:T(128)S(1)} %stack.67.place_ref, bf16[576,768]{1,0:T(8,128)(2,1)S(1)} %bitcast.14, bf16[576,768]{1,0:T(8,128)(2,1)S(1)} %collective-permute-done.5.refs_1_, ...), custom_call_target="tpu_custom_call" | custom-call | flops 1000000 | bytes 1000000 | tf_op jit(solution)/shard_map/project_early/pallas_call | solution.py:683
  20.8 0.2 collective-permute-done.3.got_hbm.even_cols_ref
  21.1 1.6 %collective-permute-start.8 = (bf16[176,768]{1,0:T(8,128)(2,1)S(1)}, bf16[176,768]{1,0:T(8,128)(2,1)S(1)}, u32[]{:S(2)}, u32[]{:S(2)}) collective-permute-start(bf16[176,768]{1,0:T(8,128)(2,1)S(1)} %collective-permute-done.refs_0_), channel_id=1, source_target_pairs={{0,16},{16,0},{1,17},{17,1},{2,18},{18,2},{3,19},{19,3},{4,20},{20... | collective-permute-start | bytes 811016 | tf_op jit(solution)/shard_map/ppermute | solution.py:718
  22.7 3.6 %collective-permute-start.6 = (bf16[8,768]{1,0:T(8,128)(2,1)S(1)}, bf16[8,768]{1,0:T(8,128)(2,1)S(1)}, u32[]{:S(2)}, u32[]{:S(2)}) collective-permute-start(bf16[8,768]{1,0:T(8,128)(2,1)S(1)} %carrier_pair.1.refs_0_), channel_id=1, source_target_pairs={{0,3},{1,2},{2,1},{3,0},{4,7},{5,6},{6,5},{7,4},{8,11},{9,10},{10,... | collective-permute-start | bytes 36872 | tf_op jit(solution)/shard_map/ppermute | solution.py:48
  26.3 1.8 %outer_blocks.1 = (bf16[640,768]{1,0:T(8,128)(2,1)S(1)}, f32[16,8,256]{2,1,0:T(8,128)S(1)}) custom-call(s32[11]{0:T(128)S(1)} %stack.67.place_ref, bf16[1024,768]{1,0:T(8,128)(2,1)S(1)} %own_norm.1.xq_ref.refs_2_.refs_9_, bf16[32,32,128]{2,1,0:T(8,128)(2,1)S(1)} %get-tuple-element.38.mark_ref, bf16[4,32,768]{2,1,0:T(8,128)(2,1)S(1)} %collective-permute-done.1.even_rows_ref, ...), custom_call_target="tpu_custom_call" | custom-call | flops 10000000 | bytes 6000000 | tf_op jit(solution)/shard_map/outer_blocks/pallas_call | solution.py:724
  28.1 0.1 collective-permute-done.6.refs_1_
  28.2 1.8 %collective-permute-start.13 = (bf16[208,768]{1,0:T(8,128)(2,1)S(1)}, bf16[208,768]{1,0:T(8,128)(2,1)S(1)}, u32[]{:S(2)}, u32[]{:S(2)}) collective-permute-start(bf16[208,768]{1,0:T(8,128)(2,1)S(1)} %final_pack.1.refs_0_), channel_id=1, source_target_pairs={{0,8},{4,12},{8,0},{12,4},{1,9},{5,13},{9,1},{13,5},{2,10},{6,14},... | collective-permute-start | bytes 958472 | tf_op jit(solution)/shard_map/ppermute | solution.py:48
  30.0 0.2 collective-permute-start.7
  30.2 0.3 collective-permute-start.9
  30.5 0.2 collective-permute-start.12
  30.7 0.8 %collective-permute-done.7.refs_1_ = bf16[176,768]{1,0:T(8,128)(2,1)S(1)} collective-permute-done((bf16[176,768]{1,0:T(8,128)(2,1)S(1)}, bf16[176,768]{1,0:T(8,128)(2,1)S(1)}, u32[]{:S(2)}, u32[]{:S(2)}) %collective-permute-start.7) | collective-permute-done | bytes 270368 | tf_op jit(solution)/shard_map/ppermute | solution.py:48
  31.6 0.4 collective-permute-done.9.refs_3_
  31.9 3.2 %project_late.1 = (bf16[3,1024,256]{2,1,0:T(8,128)(2,1)S(1)}, bf16[3,1600,256]{2,1,0:T(8,128)(2,1)S(1)}, bf16[2304,768]{1,0:T(8,128)(2,1)S(1)}) custom-call(s32[11]{0:T(128)S(1)} %stack.67.place_ref, bf16[176,768]{1,0:T(8,128)(2,1)S(1)} %collective-permute-done.refs_0_, bf16[176,768]{1,0:T(8,128)(2,1)S(1)} %collective-permute-done.7.refs_1_, ...), custom_call_target="tpu_custom_call" | custom-call | flops 1000000 | bytes 1000000 | tf_op jit(solution)/shard_map/project_late/pallas_call | solution.py:766
  35.1 2.0 %values.2.v_low = bf16[2,1600,256]{2,1,0:T(8,128)(2,1)S(1)} custom-call(s32[11]{0:T(128)S(1)} %stack.67.place_ref, bf16[2304,768]{1,0:T(8,128)(2,1)S(1)} %get-tuple-element.56.wt, bf16[4,1024,256]{2,1,0:T(8,128)(2,1)S(1)} %get-tuple-element.51.refs_7_.whole_ref, bf16[960,768]{1,0:T(8,128)(2,1)S(1)} %middle_blocks.1.refs_3_.refs_10_.mid_ref, ...), custom_call_target="tpu_custom_call" | custom-call | flops 1000 | bytes 1000 | tf_op jit(solution)/shard_map/values/pallas_call | solution.py:782
  37.2 1.1 %collective-permute-done.13.refs_2_ = bf16[208,768]{1,0:T(8,128)(2,1)S(1)} collective-permute-done((bf16[208,768]{1,0:T(8,128)(2,1)S(1)}, bf16[208,768]{1,0:T(8,128)(2,1)S(1)}, u32[]{:S(2)}, u32[]{:S(2)}) %collective-permute-start.13) | collective-permute-done | bytes 319520 | tf_op jit(solution)/shard_map/ppermute | solution.py:48
  38.2 1.6 %values.3.v_high = bf16[1,1600,256]{2,1,0:T(8,128)(2,1)S(1)} custom-call(s32[11]{0:T(128)S(1)} %stack.67.place_ref, bf16[2304,768]{1,0:T(8,128)(2,1)S(1)} %get-tuple-element.56.wt, bf16[4,1024,256]{2,1,0:T(8,128)(2,1)S(1)} %get-tuple-element.51.refs_7_.whole_ref, bf16[960,768]{1,0:T(8,128)(2,1)S(1)} %middle_blocks.1.refs_3_.refs_10_.mid_ref, ...), custom_call_target="tpu_custom_call" | custom-call | flops 1000 | bytes 1000 | tf_op jit(solution)/shard_map/values/pallas_call | solution.py:782
  39.9 3.2 %carriers.1 = (bf16[2,2,768]{2,1,0:T(2,128)(2,1)}, bf16[768,768]{1,0:T(8,128)(2,1)S(1)}, bf16[12,256,256]{2,1,0:T(8,128)(2,1)S(1)}, f32[8,768]{1,0:T(8,128)S(1)}) custom-call(s32[11]{0:T(128)S(1)} %stack.67.place_ref, bf16[2304,768]{1,0:T(8,128)(2,1)S(1)} %get-tuple-element.56.wt, bf16[208,768]{1,0:T(8,128)(2,1)S(1)} %final_pack.1.refs_0_, ...), custom_call_target="tpu_custom_call" | custom-call | flops 500000000 | bytes 5000000 | tf_op jit(solution)/shard_map/carriers/pallas_call | solution.py:801
  43.1 6.0 %attend.1.mix_s = bf16[1024,768]{1,0:T(8,128)(2,1)S(1)} custom-call(bf16[3,1024,256]{2,1,0:T(8,128)(2,1)S(1)} %get-tuple-element.53.q_s, bf16[3,1600,256]{2,1,0:T(8,128)(2,1)S(1)} %get-tuple-element.54.k_s, bf16[2,1600,256]{2,1,0:T(8,128)(2,1)S(1)} %values.2.v_low, bf16[1,1600,256]{2,1,0:T(8,128)(2,1)S(1)} %values.3.v_high, ...), custom_call_target="tpu_custom_call" | custom-call | flops 4000000000 | bytes 12000000 | tf_op jit(solution)/shard_map/attend/pallas_call | solution.py:817
  49.1 2.4 %out.1 = bf16[32,32,768]{2,1,0:T(8,128)(2,1)} custom-call(bf16[32,32,768]{2,1,0:T(8,128)(2,1)S(1)} %get-tuple-element.33.x_ref, bf16[1024,768]{1,0:T(8,128)(2,1)S(1)} %attend.1.mix_s, bf16[768,768]{1,0:T(8,128)(2,1)S(1)} %get-tuple-element.62.wo), custom_call_target="tpu_custom_call" | custom-call | flops 1200000000 | bytes 6000000 | tf_op jit(solution)/shard_map/out/pallas_call | solution.py:832
  (20 shorter events, 0.1 us)
Async XLA Ops:
  0.6 17.3 %collective-permute-start.5 = (bf16[576,768]{1,0:T(8,128)(2,1)}, bf16[576,768]{1,0:T(8,128)(2,1)S(1)}, u32[]{:S(2)}, u32[]{:S(2)}) collective-permute-start(bf16[576,768]{1,0:T(8,128)(2,1)} %bitcast.12), channel_id=1, source_target_pairs={{0,4},{4,0},{8,12},{12,8},{1,5},{5,1},{9,13},{13,9},{2,6},{6,2},{1... | collective-permute-start | bytes 2654216 | tf_op jit(solution)/shard_map/ppermute | solution.py:48
  3.3 8.5 %collective-permute-start.1 = (bf16[4,32,768]{2,1,0:T(8,128)(2,1)S(1)}, bf16[4,32,768]{2,1,0:T(8,128)(2,1)S(1)}, u32[]{:S(2)}, u32[]{:S(2)}) collective-permute-start(bf16[4,32,768]{2,1,0:T(8,128)(2,1)S(1)} %get-tuple-element.34), channel_id=1, source_target_pairs={{0,4},{8,12},{4,0},{12,8},{1,5},{9,13},{5,1},{13,9},{2,6},{10,14},... | collective-permute-start | bytes 589832 | tf_op jit(solution)/shard_map/ppermute | solution.py:42
  3.5 8.4 %collective-permute-start.2 = (bf16[4,32,768]{2,1,0:T(8,128)(2,1)S(1)}, bf16[4,32,768]{2,1,0:T(8,128)(2,1)S(1)}, u32[]{:S(2)}, u32[]{:S(2)}) collective-permute-start(bf16[4,32,768]{2,1,0:T(8,128)(2,1)S(1)} %get-tuple-element.39), channel_id=1, source_target_pairs={{4,8},{8,4},{5,9},{9,5},{6,10},{10,6},{7,11},{11,7},{20,24},{24,20... | collective-permute-start | bytes 589832 | tf_op jit(solution)/shard_map/ppermute | solution.py:42
  5.8 15.3 %collective-permute-start = (bf16[176,768]{1,0:T(8,128)(2,1)S(1)}, bf16[176,768]{1,0:T(8,128)(2,1)S(1)}, u32[]{:S(2)}, u32[]{:S(2)}) collective-permute-start(bf16[176,768]{1,0:T(8,128)(2,1)S(1)} %get-tuple-element.36), channel_id=1, source_target_pairs={{0,8},{4,12},{8,0},{12,4},{1,9},{5,13},{9,1},{13,5},{2,10},{6,14},... | collective-permute-start | bytes 811016 | tf_op jit(solution)/shard_map/ppermute | solution.py:48
  10.0 1.8 %copy-start.2 = (bf16[2,2,768]{2,1,0:T(2,128)(2,1)S(1)}, bf16[2,2,768]{2,1,0:T(2,128)(2,1)}, u32[]{:S(2)}) copy-start(bf16[2,2,768]{2,1,0:T(2,128)(2,1)} %own_ref.1) | copy-start | bytes 18436
  12.8 8.3 %collective-permute-start.3 = (bf16[21,8,768]{2,1,0:T(8,128)(2,1)S(1)}, bf16[21,8,768]{2,1,0:T(8,128)(2,1)S(1)}, u32[]{:S(2)}, u32[]{:S(2)}) collective-permute-start(bf16[21,8,768]{2,1,0:T(8,128)(2,1)S(1)} %get-tuple-element.40), channel_id=1, source_target_pairs={{0,1},{2,3},{1,0},{3,2},{4,5},{6,7},{5,4},{7,6},{8,9},{10,11},{9,8... | collective-permute-start | bytes 774152 | tf_op jit(solution)/shard_map/ppermute | solution.py:42
  14.6 6.6 %collective-permute-start.4 = (bf16[20,8,768]{2,1,0:T(8,128)(2,1)S(1)}, bf16[20,8,768]{2,1,0:T(8,128)(2,1)S(1)}, u32[]{:S(2)}, u32[]{:S(2)}) collective-permute-start(bf16[20,8,768]{2,1,0:T(8,128)(2,1)S(1)} %get-tuple-element.41), channel_id=1, source_target_pairs={{1,2},{2,1},{5,6},{6,5},{9,10},{10,9},{13,14},{14,13},{17,18},{18,... | collective-permute-start | bytes 737288 | tf_op jit(solution)/shard_map/ppermute | solution.py:42
  15.2 2.7 %copy-start = (bf16[768,576]{0,1:T(8,128)(2,1)S(1)}, bf16[768,576]{0,1:T(8,128)(2,1)}, u32[]{:S(2)}) copy-start(bf16[768,576]{0,1:T(8,128)(2,1)} %param.7) | copy-start | bytes 2654212
  15.3 12.8 %collective-permute-start.10 = (bf16[224,768]{1,0:T(8,128)(2,1)S(1)}, bf16[224,768]{1,0:T(8,128)(2,1)S(1)}, u32[]{:S(2)}, u32[]{:S(2)}) collective-permute-start(bf16[224,768]{1,0:T(8,128)(2,1)S(1)} %get-tuple-element.49), channel_id=1, source_target_pairs={{0,8},{4,12},{8,0},{12,4},{1,9},{5,13},{9,1},{13,5},{2,10},{6,14},... | collective-permute-start | bytes 1032200 | tf_op jit(solution)/shard_map/ppermute | solution.py:48
  20.8 7.4 %copy-start.1 = (bf16[768,192]{0,1:T(8,128)(2,1)S(1)}, bf16[768,192]{0,1:T(8,128)(2,1)}, u32[]{:S(2)}) copy-start(bf16[768,192]{0,1:T(8,128)(2,1)} %param.8) | copy-start | bytes 884740
  21.1 9.1 %collective-permute-start.8 = (bf16[176,768]{1,0:T(8,128)(2,1)S(1)}, bf16[176,768]{1,0:T(8,128)(2,1)S(1)}, u32[]{:S(2)}, u32[]{:S(2)}) collective-permute-start(bf16[176,768]{1,0:T(8,128)(2,1)S(1)} %collective-permute-done.refs_0_), channel_id=1, source_target_pairs={{0,16},{16,0},{1,17},{17,1},{2,18},{18,2},{3,19},{19,3},{4,20},{20... | collective-permute-start | bytes 811016 | tf_op jit(solution)/shard_map/ppermute | solution.py:718
  22.7 5.5 %collective-permute-start.6 = (bf16[8,768]{1,0:T(8,128)(2,1)S(1)}, bf16[8,768]{1,0:T(8,128)(2,1)S(1)}, u32[]{:S(2)}, u32[]{:S(2)}) collective-permute-start(bf16[8,768]{1,0:T(8,128)(2,1)S(1)} %carrier_pair.1.refs_0_), channel_id=1, source_target_pairs={{0,3},{1,2},{2,1},{3,0},{4,7},{5,6},{6,5},{7,4},{8,11},{9,10},{10,... | collective-permute-start | bytes 36872 | tf_op jit(solution)/shard_map/ppermute | solution.py:48
  28.2 3.4 %collective-permute-start.11 = (bf16[224,768]{1,0:T(8,128)(2,1)S(1)}, bf16[224,768]{1,0:T(8,128)(2,1)S(1)}, u32[]{:S(2)}, u32[]{:S(2)}) collective-permute-start(bf16[224,768]{1,0:T(8,128)(2,1)S(1)} %collective-permute-done.10.refs_4_), channel_id=1, source_target_pairs={{0,4},{4,0},{8,12},{12,8},{1,5},{5,1},{9,13},{13,9},{2,6},{6,2},{1... | collective-permute-start | bytes 1032200 | tf_op jit(solution)/shard_map/ppermute | solution.py:48
  28.2 10.0 %collective-permute-start.13 = (bf16[208,768]{1,0:T(8,128)(2,1)S(1)}, bf16[208,768]{1,0:T(8,128)(2,1)S(1)}, u32[]{:S(2)}, u32[]{:S(2)}) collective-permute-start(bf16[208,768]{1,0:T(8,128)(2,1)S(1)} %final_pack.1.refs_0_), channel_id=1, source_target_pairs={{0,8},{4,12},{8,0},{12,4},{1,9},{5,13},{9,1},{13,5},{2,10},{6,14},... | collective-permute-start | bytes 958472 | tf_op jit(solution)/shard_map/ppermute | solution.py:48
  30.0 1.5 %collective-permute-start.7 = (bf16[176,768]{1,0:T(8,128)(2,1)S(1)}, bf16[176,768]{1,0:T(8,128)(2,1)S(1)}, u32[]{:S(2)}, u32[]{:S(2)}) collective-permute-start(bf16[176,768]{1,0:T(8,128)(2,1)S(1)} %collective-permute-done.refs_0_), channel_id=1, source_target_pairs={{0,4},{4,0},{8,12},{12,8},{1,5},{5,1},{9,13},{13,9},{2,6},{6,2},{1... | collective-permute-start | bytes 811016 | tf_op jit(solution)/shard_map/ppermute | solution.py:48
  30.2 1.7 %collective-permute-start.9 = (bf16[176,768]{1,0:T(8,128)(2,1)S(1)}, bf16[176,768]{1,0:T(8,128)(2,1)S(1)}, u32[]{:S(2)}, u32[]{:S(2)}) collective-permute-start(bf16[176,768]{1,0:T(8,128)(2,1)S(1)} %collective-permute-done.8.refs_2_), channel_id=1, source_target_pairs={{0,4},{4,0},{8,12},{12,8},{1,5},{5,1},{9,13},{13,9},{2,6},{6,2},{1... | collective-permute-start | bytes 811016 | tf_op jit(solution)/shard_map/ppermute | solution.py:48
  30.5 9.3 %collective-permute-start.12 = (bf16[208,768]{1,0:T(8,128)(2,1)S(1)}, bf16[208,768]{1,0:T(8,128)(2,1)S(1)}, u32[]{:S(2)}, u32[]{:S(2)}) collective-permute-start(bf16[208,768]{1,0:T(8,128)(2,1)S(1)} %final_pack.1.refs_0_), channel_id=1, source_target_pairs={{0,4},{4,0},{8,12},{12,8},{1,5},{5,1},{9,13},{13,9},{2,6},{6,2},{1... | collective-permute-start | bytes 958472 | tf_op jit(solution)/shard_map/ppermute | solution.py:48
  38.2 1.6 %collective-permute-start.14 = (bf16[208,768]{1,0:T(8,128)(2,1)S(1)}, bf16[208,768]{1,0:T(8,128)(2,1)S(1)}, u32[]{:S(2)}, u32[]{:S(2)}) collective-permute-start(bf16[208,768]{1,0:T(8,128)(2,1)S(1)} %collective-permute-done.13.refs_2_), channel_id=1, source_target_pairs={{0,4},{4,0},{8,12},{12,8},{1,5},{5,1},{9,13},{13,9},{2,6},{6,2},{1... | collective-permute-start | bytes 958472 | tf_op jit(solution)/shard_map/ppermute | solution.py:48

commit v6 on v5

--- a/solution.py
+++ b/solution.py
@@ -557,7 +557,7 @@
         finish(t + 1, odd_s)
         return 0
 
-    lax.fori_loop(0, tiles // 2, two, 0, unroll=2)
+    lax.fori_loop(0, tiles // 2, two, 0, unroll=4)
 
 
 def out_kernel(x_ref, mix_s, wo, out_hbm, out_ref, out_sems):

time: 52 us -> 51.6 us (level)
  no operation moved by 1% of the time
where the time goes in v6:
time: 51.6 us; the launch traced here: 51.2 us
  Pallas kernels  30.2 us (59%)
  starting transfers between devices  17.1 us (33%)
  waiting for transfers between devices  2.71 us (5%)
  between operations  0.99 us (2%)
    ppermute x10, starting transfers between devices, swapped(): return lax.ppermute(block, axis, [(i, i ^ bit) for i in range(count)])  12.3 us
    pallas_call x1, Pallas kernels, local(): pl.pallas_call(functools.partial(attend_kernel, rows // TILE, cols // TIL...  5.55 us
    pallas_call x2, Pallas kernels, values(): pl.pallas_call(functools.partial(value_kernel, first), out_shape=jax.Shap...  3.57 us
    ppermute x4, starting transfers between devices, pair_swapped(): got.append(lax.ppermute(block, axis, pairs + [(b, a) for a, b in pairs]))  3.29 us
    pallas_call x1, Pallas kernels, local(): pl.pallas_call(functools.partial(carrier_kernel, offsets), out_shape=(jax...  3.23 us
    pallas_call x1, Pallas kernels, local(): pl.pallas_call(functools.partial(late_kernel, numbered, triple_t.shape[0]...  3.19 us
    pallas_call x1, Pallas kernels, local(): pl.pallas_call(functools.partial(early_kernel, offsets), out_shape=(pltpu...  2.85 us
    ppermute x10, waiting for transfers between devices, swapped(): return lax.ppermute(block, axis, [(i, i ^ bit) for i in range(count)])  2.45 us
  transfers between devices with their start and end apart: 15, of which 5 were waited for; matrix products, arithmetic and copies ran while one was open for 0% of the time, Pallas kernels for 37%

profile of v6, /device:TPU:0, one launch (start us, length us, event | category | flops | bytes accessed | tf_op | source)
XLA Modules:
  0.0 51.2 jit_solution(9048224521922881437)
XLA Ops:
  0.6 0.5 %collective-permute-start.5 = (bf16[576,768]{1,0:T(8,128)(2,1)}, bf16[576,768]{1,0:T(8,128)(2,1)S(1)}, u32[]{:S(2)}, u32[]{:S(2)}) collective-permute-start(bf16[576,768]{1,0:T(8,128)(2,1)} %bitcast.12), channel_id=1, source_target_pairs={{0,4},{4,0},{8,12},{12,8},{1,5},{5,1},{9,13},{13,9},{2,6},{6,2},{1... | collective-permute-start | bytes 2654216 | tf_op jit(solution)/shard_map/ppermute | solution.py:48
  1.1 0.1 stack.67.place_ref
  1.2 2.1 %edge_rows.1 = (bf16[32,32,128]{2,1,0:T(8,128)(2,1)S(1)}, bf16[4,32,768]{2,1,0:T(8,128)(2,1)S(1)}, bf16[4,32,768]{2,1,0:T(8,128)(2,1)S(1)}, bf16[32,32,768]{2,1,0:T(8,128)(2,1)S(1)}) custom-call(s32[11]{0:T(128)S(1)} %stack.67.place_ref, s32[32,32]{1,0:T(8,128)} %flags_hbm.1, bf16[32,32,768]{2,1,0:T(8,128)(2,1)} %x_hbm.1), custom_call_target="tpu_custom_call" | custom-call | flops 1000000 | bytes 1000000 | tf_op jit(solution)/shard_map/edge_rows/pallas_call | solution.py:604
  3.3 0.1 collective-permute-start.1
  3.5 0.7 %collective-permute-start.2 = (bf16[4,32,768]{2,1,0:T(8,128)(2,1)S(1)}, bf16[4,32,768]{2,1,0:T(8,128)(2,1)S(1)}, u32[]{:S(2)}, u32[]{:S(2)}) collective-permute-start(bf16[4,32,768]{2,1,0:T(8,128)(2,1)S(1)} %get-tuple-element.39), channel_id=1, source_target_pairs={{4,8},{8,4},{5,9},{9,5},{6,10},{10,6},{7,11},{11,7},{20,24},{24,20... | collective-permute-start | bytes 589832 | tf_op jit(solution)/shard_map/ppermute | solution.py:42
  4.1 1.6 %pieces.1 = (bf16[176,768]{1,0:T(8,128)(2,1)S(1)}, bf16[224,768]{1,0:T(8,128)(2,1)S(1)}) custom-call(s32[11]{0:T(128)S(1)} %stack.67.place_ref, bf16[576,768]{1,0:T(8,128)(2,1)} %bitcast.13), custom_call_target="tpu_custom_call" | custom-call | flops 1000000 | bytes 1000000 | tf_op jit(solution)/shard_map/pieces/pallas_call | solution.py:623
  5.8 4.3 %collective-permute-start = (bf16[176,768]{1,0:T(8,128)(2,1)S(1)}, bf16[176,768]{1,0:T(8,128)(2,1)S(1)}, u32[]{:S(2)}, u32[]{:S(2)}) collective-permute-start(bf16[176,768]{1,0:T(8,128)(2,1)S(1)} %get-tuple-element.36), channel_id=1, source_target_pairs={{0,8},{4,12},{8,0},{12,4},{1,9},{5,13},{9,1},{13,5},{2,10},{6,14},... | collective-permute-start | bytes 811016 | tf_op jit(solution)/shard_map/ppermute | solution.py:48
  10.0 1.8 %own_norm.1.xq_ref.refs_2_.refs_9_ = bf16[1024,768]{1,0:T(8,128)(2,1)S(1)} custom-call(bf16[32,32,768]{2,1,0:T(8,128)(2,1)S(1)} %get-tuple-element.33.x_ref), custom_call_target="tpu_custom_call" | custom-call | flops 1000000 | bytes 1000000 | tf_op jit(solution)/shard_map/own_norm/pallas_call | solution.py:636
  11.9 0.9 %edge_columns.1 = (bf16[21,8,768]{2,1,0:T(8,128)(2,1)S(1)}, bf16[20,8,768]{2,1,0:T(8,128)(2,1)S(1)}) custom-call(s32[11]{0:T(128)S(1)} %stack.67.place_ref, bf16[32,32,768]{2,1,0:T(8,128)(2,1)S(1)} %get-tuple-element.33.x_ref, bf16[32,32,128]{2,1,0:T(8,128)(2,1)S(1)} %get-tuple-element.38.mark_ref, ...), custom_call_target="tpu_custom_call" | custom-call | flops 1000000 | bytes 2000000 | tf_op jit(solution)/shard_map/edge_columns/pallas_call | solution.py:654
  12.8 1.8 %collective-permute-start.3 = (bf16[21,8,768]{2,1,0:T(8,128)(2,1)S(1)}, bf16[21,8,768]{2,1,0:T(8,128)(2,1)S(1)}, u32[]{:S(2)}, u32[]{:S(2)}) collective-permute-start(bf16[21,8,768]{2,1,0:T(8,128)(2,1)S(1)} %get-tuple-element.40), channel_id=1, source_target_pairs={{0,1},{2,3},{1,0},{3,2},{4,5},{6,7},{5,4},{7,6},{8,9},{10,11},{9,8... | collective-permute-start | bytes 774152 | tf_op jit(solution)/shard_map/ppermute | solution.py:42
  14.6 0.7 %collective-permute-start.4 = (bf16[20,8,768]{2,1,0:T(8,128)(2,1)S(1)}, bf16[20,8,768]{2,1,0:T(8,128)(2,1)S(1)}, u32[]{:S(2)}, u32[]{:S(2)}) collective-permute-start(bf16[20,8,768]{2,1,0:T(8,128)(2,1)S(1)} %get-tuple-element.41), channel_id=1, source_target_pairs={{1,2},{2,1},{5,6},{6,5},{9,10},{10,9},{13,14},{14,13},{17,18},{18,... | collective-permute-start | bytes 737288 | tf_op jit(solution)/shard_map/ppermute | solution.py:42
  15.3 1.4 %collective-permute-start.10 = (bf16[224,768]{1,0:T(8,128)(2,1)S(1)}, bf16[224,768]{1,0:T(8,128)(2,1)S(1)}, u32[]{:S(2)}, u32[]{:S(2)}) collective-permute-start(bf16[224,768]{1,0:T(8,128)(2,1)S(1)} %get-tuple-element.49), channel_id=1, source_target_pairs={{0,8},{4,12},{8,0},{12,4},{1,9},{5,13},{9,1},{13,5},{2,10},{6,14},... | collective-permute-start | bytes 1032200 | tf_op jit(solution)/shard_map/ppermute | solution.py:48
  16.7 1.3 %middle_blocks.1.refs_3_.refs_10_.mid_ref = bf16[960,768]{1,0:T(8,128)(2,1)S(1)} custom-call(s32[11]{0:T(128)S(1)} %stack.67.place_ref, bf16[1024,768]{1,0:T(8,128)(2,1)S(1)} %own_norm.1.xq_ref.refs_2_.refs_9_, bf16[4,32,768]{2,1,0:T(8,128)(2,1)S(1)} %collective-permute-done.1.even_rows_ref, bf16[4,32,768]{2,1,0:T(8,128)(2,1)S(1)} %collective-permute-done.2.odd_rows_ref), custom_call_target="tpu_custom_call" | custom-call | flops 1000000 | bytes 1000000 | tf_op jit(solution)/shard_map/middle_blocks/pallas_call | solution.py:673
  18.0 2.9 %project_early.1 = (bf16[4,1024,256]{2,1,0:T(8,128)(2,1)S(1)}, bf16[960,128]{1,0:T(8,128)(2,1)S(1)}, bf16[1152,768]{1,0:T(8,128)(2,1)S(1)}) custom-call(s32[11]{0:T(128)S(1)} %stack.67.place_ref, bf16[576,768]{1,0:T(8,128)(2,1)S(1)} %bitcast.14, bf16[576,768]{1,0:T(8,128)(2,1)S(1)} %collective-permute-done.5.refs_1_, ...), custom_call_target="tpu_custom_call" | custom-call | flops 1000000 | bytes 1000000 | tf_op jit(solution)/shard_map/project_early/pallas_call | solution.py:683
  20.8 0.2 collective-permute-done.3.got_hbm.even_cols_ref
  21.1 1.6 %collective-permute-start.8 = (bf16[176,768]{1,0:T(8,128)(2,1)S(1)}, bf16[176,768]{1,0:T(8,128)(2,1)S(1)}, u32[]{:S(2)}, u32[]{:S(2)}) collective-permute-start(bf16[176,768]{1,0:T(8,128)(2,1)S(1)} %collective-permute-done.refs_0_), channel_id=1, source_target_pairs={{0,16},{16,0},{1,17},{17,1},{2,18},{18,2},{3,19},{19,3},{4,20},{20... | collective-permute-start | bytes 811016 | tf_op jit(solution)/shard_map/ppermute | solution.py:718
  22.7 3.6 %collective-permute-start.6 = (bf16[8,768]{1,0:T(8,128)(2,1)S(1)}, bf16[8,768]{1,0:T(8,128)(2,1)S(1)}, u32[]{:S(2)}, u32[]{:S(2)}) collective-permute-start(bf16[8,768]{1,0:T(8,128)(2,1)S(1)} %carrier_pair.1.refs_0_), channel_id=1, source_target_pairs={{0,3},{1,2},{2,1},{3,0},{4,7},{5,6},{6,5},{7,4},{8,11},{9,10},{10,... | collective-permute-start | bytes 36872 | tf_op jit(solution)/shard_map/ppermute | solution.py:48
  26.3 1.8 %outer_blocks.1 = (bf16[640,768]{1,0:T(8,128)(2,1)S(1)}, f32[16,8,256]{2,1,0:T(8,128)S(1)}) custom-call(s32[11]{0:T(128)S(1)} %stack.67.place_ref, bf16[1024,768]{1,0:T(8,128)(2,1)S(1)} %own_norm.1.xq_ref.refs_2_.refs_9_, bf16[32,32,128]{2,1,0:T(8,128)(2,1)S(1)} %get-tuple-element.38.mark_ref, bf16[4,32,768]{2,1,0:T(8,128)(2,1)S(1)} %collective-permute-done.1.even_rows_ref, ...), custom_call_target="tpu_custom_call" | custom-call | flops 10000000 | bytes 6000000 | tf_op jit(solution)/shard_map/outer_blocks/pallas_call | solution.py:724
  28.1 0.1 collective-permute-done.6.refs_1_
  28.2 1.8 %collective-permute-start.13 = (bf16[208,768]{1,0:T(8,128)(2,1)S(1)}, bf16[208,768]{1,0:T(8,128)(2,1)S(1)}, u32[]{:S(2)}, u32[]{:S(2)}) collective-permute-start(bf16[208,768]{1,0:T(8,128)(2,1)S(1)} %final_pack.1.refs_0_), channel_id=1, source_target_pairs={{0,8},{4,12},{8,0},{12,4},{1,9},{5,13},{9,1},{13,5},{2,10},{6,14},... | collective-permute-start | bytes 958472 | tf_op jit(solution)/shard_map/ppermute | solution.py:48
  30.0 0.2 collective-permute-start.7
  30.2 0.3 collective-permute-start.9
  30.5 0.2 collective-permute-start.12
  30.7 0.8 %collective-permute-done.7.refs_1_ = bf16[176,768]{1,0:T(8,128)(2,1)S(1)} collective-permute-done((bf16[176,768]{1,0:T(8,128)(2,1)S(1)}, bf16[176,768]{1,0:T(8,128)(2,1)S(1)}, u32[]{:S(2)}, u32[]{:S(2)}) %collective-permute-start.7) | collective-permute-done | bytes 270368 | tf_op jit(solution)/shard_map/ppermute | solution.py:48
  31.6 0.4 collective-permute-done.9.refs_3_
  31.9 3.2 %project_late.1 = (bf16[3,1024,256]{2,1,0:T(8,128)(2,1)S(1)}, bf16[3,1600,256]{2,1,0:T(8,128)(2,1)S(1)}, bf16[2304,768]{1,0:T(8,128)(2,1)S(1)}) custom-call(s32[11]{0:T(128)S(1)} %stack.67.place_ref, bf16[176,768]{1,0:T(8,128)(2,1)S(1)} %collective-permute-done.refs_0_, bf16[176,768]{1,0:T(8,128)(2,1)S(1)} %collective-permute-done.7.refs_1_, ...), custom_call_target="tpu_custom_call" | custom-call | flops 1000000 | bytes 1000000 | tf_op jit(solution)/shard_map/project_late/pallas_call | solution.py:766
  35.1 2.0 %values.2.v_low = bf16[2,1600,256]{2,1,0:T(8,128)(2,1)S(1)} custom-call(s32[11]{0:T(128)S(1)} %stack.67.place_ref, bf16[2304,768]{1,0:T(8,128)(2,1)S(1)} %get-tuple-element.56.wt, bf16[4,1024,256]{2,1,0:T(8,128)(2,1)S(1)} %get-tuple-element.51.refs_7_.whole_ref, bf16[960,768]{1,0:T(8,128)(2,1)S(1)} %middle_blocks.1.refs_3_.refs_10_.mid_ref, ...), custom_call_target="tpu_custom_call" | custom-call | flops 1000 | bytes 1000 | tf_op jit(solution)/shard_map/values/pallas_call | solution.py:782
  37.2 1.1 %collective-permute-done.13.refs_2_ = bf16[208,768]{1,0:T(8,128)(2,1)S(1)} collective-permute-done((bf16[208,768]{1,0:T(8,128)(2,1)S(1)}, bf16[208,768]{1,0:T(8,128)(2,1)S(1)}, u32[]{:S(2)}, u32[]{:S(2)}) %collective-permute-start.13) | collective-permute-done | bytes 319520 | tf_op jit(solution)/shard_map/ppermute | solution.py:48
  38.2 1.6 %values.3.v_high = bf16[1,1600,256]{2,1,0:T(8,128)(2,1)S(1)} custom-call(s32[11]{0:T(128)S(1)} %stack.67.place_ref, bf16[2304,768]{1,0:T(8,128)(2,1)S(1)} %get-tuple-element.56.wt, bf16[4,1024,256]{2,1,0:T(8,128)(2,1)S(1)} %get-tuple-element.51.refs_7_.whole_ref, bf16[960,768]{1,0:T(8,128)(2,1)S(1)} %middle_blocks.1.refs_3_.refs_10_.mid_ref, ...), custom_call_target="tpu_custom_call" | custom-call | flops 1000 | bytes 1000 | tf_op jit(solution)/shard_map/values/pallas_call | solution.py:782
  39.9 3.2 %carriers.1 = (bf16[2,2,768]{2,1,0:T(2,128)(2,1)}, bf16[768,768]{1,0:T(8,128)(2,1)S(1)}, bf16[12,256,256]{2,1,0:T(8,128)(2,1)S(1)}, f32[8,768]{1,0:T(8,128)S(1)}) custom-call(s32[11]{0:T(128)S(1)} %stack.67.place_ref, bf16[2304,768]{1,0:T(8,128)(2,1)S(1)} %get-tuple-element.56.wt, bf16[208,768]{1,0:T(8,128)(2,1)S(1)} %final_pack.1.refs_0_, ...), custom_call_target="tpu_custom_call" | custom-call | flops 500000000 | bytes 5000000 | tf_op jit(solution)/shard_map/carriers/pallas_call | solution.py:801
  43.1 5.6 %attend.1.mix_s = bf16[1024,768]{1,0:T(8,128)(2,1)S(1)} custom-call(bf16[3,1024,256]{2,1,0:T(8,128)(2,1)S(1)} %get-tuple-element.53.q_s, bf16[3,1600,256]{2,1,0:T(8,128)(2,1)S(1)} %get-tuple-element.54.k_s, bf16[2,1600,256]{2,1,0:T(8,128)(2,1)S(1)} %values.2.v_low, bf16[1,1600,256]{2,1,0:T(8,128)(2,1)S(1)} %values.3.v_high, ...), custom_call_target="tpu_custom_call" | custom-call | flops 4000000000 | bytes 12000000 | tf_op jit(solution)/shard_map/attend/pallas_call | solution.py:817
  48.6 2.4 %out.1 = bf16[32,32,768]{2,1,0:T(8,128)(2,1)} custom-call(bf16[32,32,768]{2,1,0:T(8,128)(2,1)S(1)} %get-tuple-element.33.x_ref, bf16[1024,768]{1,0:T(8,128)(2,1)S(1)} %attend.1.mix_s, bf16[768,768]{1,0:T(8,128)(2,1)S(1)} %get-tuple-element.62.wo), custom_call_target="tpu_custom_call" | custom-call | flops 1200000000 | bytes 6000000 | tf_op jit(solution)/shard_map/out/pallas_call | solution.py:832
  (20 shorter events, 0.1 us)
Async XLA Ops:
  0.6 17.3 %collective-permute-start.5 = (bf16[576,768]{1,0:T(8,128)(2,1)}, bf16[576,768]{1,0:T(8,128)(2,1)S(1)}, u32[]{:S(2)}, u32[]{:S(2)}) collective-permute-start(bf16[576,768]{1,0:T(8,128)(2,1)} %bitcast.12), channel_id=1, source_target_pairs={{0,4},{4,0},{8,12},{12,8},{1,5},{5,1},{9,13},{13,9},{2,6},{6,2},{1... | collective-permute-start | bytes 2654216 | tf_op jit(solution)/shard_map/ppermute | solution.py:48
  3.3 8.5 %collective-permute-start.1 = (bf16[4,32,768]{2,1,0:T(8,128)(2,1)S(1)}, bf16[4,32,768]{2,1,0:T(8,128)(2,1)S(1)}, u32[]{:S(2)}, u32[]{:S(2)}) collective-permute-start(bf16[4,32,768]{2,1,0:T(8,128)(2,1)S(1)} %get-tuple-element.34), channel_id=1, source_target_pairs={{0,4},{8,12},{4,0},{12,8},{1,5},{9,13},{5,1},{13,9},{2,6},{10,14},... | collective-permute-start | bytes 589832 | tf_op jit(solution)/shard_map/ppermute | solution.py:42
  3.5 8.4 %collective-permute-start.2 = (bf16[4,32,768]{2,1,0:T(8,128)(2,1)S(1)}, bf16[4,32,768]{2,1,0:T(8,128)(2,1)S(1)}, u32[]{:S(2)}, u32[]{:S(2)}) collective-permute-start(bf16[4,32,768]{2,1,0:T(8,128)(2,1)S(1)} %get-tuple-element.39), channel_id=1, source_target_pairs={{4,8},{8,4},{5,9},{9,5},{6,10},{10,6},{7,11},{11,7},{20,24},{24,20... | collective-permute-start | bytes 589832 | tf_op jit(solution)/shard_map/ppermute | solution.py:42
  5.8 15.3 %collective-permute-start = (bf16[176,768]{1,0:T(8,128)(2,1)S(1)}, bf16[176,768]{1,0:T(8,128)(2,1)S(1)}, u32[]{:S(2)}, u32[]{:S(2)}) collective-permute-start(bf16[176,768]{1,0:T(8,128)(2,1)S(1)} %get-tuple-element.36), channel_id=1, source_target_pairs={{0,8},{4,12},{8,0},{12,4},{1,9},{5,13},{9,1},{13,5},{2,10},{6,14},... | collective-permute-start | bytes 811016 | tf_op jit(solution)/shard_map/ppermute | solution.py:48
  10.0 1.8 %copy-start.2 = (bf16[2,2,768]{2,1,0:T(2,128)(2,1)S(1)}, bf16[2,2,768]{2,1,0:T(2,128)(2,1)}, u32[]{:S(2)}) copy-start(bf16[2,2,768]{2,1,0:T(2,128)(2,1)} %own_ref.1) | copy-start | bytes 18436
  12.8 8.3 %collective-permute-start.3 = (bf16[21,8,768]{2,1,0:T(8,128)(2,1)S(1)}, bf16[21,8,768]{2,1,0:T(8,128)(2,1)S(1)}, u32[]{:S(2)}, u32[]{:S(2)}) collective-permute-start(bf16[21,8,768]{2,1,0:T(8,128)(2,1)S(1)} %get-tuple-element.40), channel_id=1, source_target_pairs={{0,1},{2,3},{1,0},{3,2},{4,5},{6,7},{5,4},{7,6},{8,9},{10,11},{9,8... | collective-permute-start | bytes 774152 | tf_op jit(solution)/shard_map/ppermute | solution.py:42
  14.6 6.6 %collective-permute-start.4 = (bf16[20,8,768]{2,1,0:T(8,128)(2,1)S(1)}, bf16[20,8,768]{2,1,0:T(8,128)(2,1)S(1)}, u32[]{:S(2)}, u32[]{:S(2)}) collective-permute-start(bf16[20,8,768]{2,1,0:T(8,128)(2,1)S(1)} %get-tuple-element.41), channel_id=1, source_target_pairs={{1,2},{2,1},{5,6},{6,5},{9,10},{10,9},{13,14},{14,13},{17,18},{18,... | collective-permute-start | bytes 737288 | tf_op jit(solution)/shard_map/ppermute | solution.py:42
  15.2 2.7 %copy-start = (bf16[768,576]{0,1:T(8,128)(2,1)S(1)}, bf16[768,576]{0,1:T(8,128)(2,1)}, u32[]{:S(2)}) copy-start(bf16[768,576]{0,1:T(8,128)(2,1)} %param.7) | copy-start | bytes 2654212
  15.3 12.8 %collective-permute-start.10 = (bf16[224,768]{1,0:T(8,128)(2,1)S(1)}, bf16[224,768]{1,0:T(8,128)(2,1)S(1)}, u32[]{:S(2)}, u32[]{:S(2)}) collective-permute-start(bf16[224,768]{1,0:T(8,128)(2,1)S(1)} %get-tuple-element.49), channel_id=1, source_target_pairs={{0,8},{4,12},{8,0},{12,4},{1,9},{5,13},{9,1},{13,5},{2,10},{6,14},... | collective-permute-start | bytes 1032200 | tf_op jit(solution)/shard_map/ppermute | solution.py:48
  20.8 7.4 %copy-start.1 = (bf16[768,192]{0,1:T(8,128)(2,1)S(1)}, bf16[768,192]{0,1:T(8,128)(2,1)}, u32[]{:S(2)}) copy-start(bf16[768,192]{0,1:T(8,128)(2,1)} %param.8) | copy-start | bytes 884740
  21.1 9.1 %collective-permute-start.8 = (bf16[176,768]{1,0:T(8,128)(2,1)S(1)}, bf16[176,768]{1,0:T(8,128)(2,1)S(1)}, u32[]{:S(2)}, u32[]{:S(2)}) collective-permute-start(bf16[176,768]{1,0:T(8,128)(2,1)S(1)} %collective-permute-done.refs_0_), channel_id=1, source_target_pairs={{0,16},{16,0},{1,17},{17,1},{2,18},{18,2},{3,19},{19,3},{4,20},{20... | collective-permute-start | bytes 811016 | tf_op jit(solution)/shard_map/ppermute | solution.py:718
  22.7 5.5 %collective-permute-start.6 = (bf16[8,768]{1,0:T(8,128)(2,1)S(1)}, bf16[8,768]{1,0:T(8,128)(2,1)S(1)}, u32[]{:S(2)}, u32[]{:S(2)}) collective-permute-start(bf16[8,768]{1,0:T(8,128)(2,1)S(1)} %carrier_pair.1.refs_0_), channel_id=1, source_target_pairs={{0,3},{1,2},{2,1},{3,0},{4,7},{5,6},{6,5},{7,4},{8,11},{9,10},{10,... | collective-permute-start | bytes 36872 | tf_op jit(solution)/shard_map/ppermute | solution.py:48
  28.2 3.4 %collective-permute-start.11 = (bf16[224,768]{1,0:T(8,128)(2,1)S(1)}, bf16[224,768]{1,0:T(8,128)(2,1)S(1)}, u32[]{:S(2)}, u32[]{:S(2)}) collective-permute-start(bf16[224,768]{1,0:T(8,128)(2,1)S(1)} %collective-permute-done.10.refs_4_), channel_id=1, source_target_pairs={{0,4},{4,0},{8,12},{12,8},{1,5},{5,1},{9,13},{13,9},{2,6},{6,2},{1... | collective-permute-start | bytes 1032200 | tf_op jit(solution)/shard_map/ppermute | solution.py:48
  28.2 10.0 %collective-permute-start.13 = (bf16[208,768]{1,0:T(8,128)(2,1)S(1)}, bf16[208,768]{1,0:T(8,128)(2,1)S(1)}, u32[]{:S(2)}, u32[]{:S(2)}) collective-permute-start(bf16[208,768]{1,0:T(8,128)(2,1)S(1)} %final_pack.1.refs_0_), channel_id=1, source_target_pairs={{0,8},{4,12},{8,0},{12,4},{1,9},{5,13},{9,1},{13,5},{2,10},{6,14},... | collective-permute-start | bytes 958472 | tf_op jit(solution)/shard_map/ppermute | solution.py:48
  30.0 1.5 %collective-permute-start.7 = (bf16[176,768]{1,0:T(8,128)(2,1)S(1)}, bf16[176,768]{1,0:T(8,128)(2,1)S(1)}, u32[]{:S(2)}, u32[]{:S(2)}) collective-permute-start(bf16[176,768]{1,0:T(8,128)(2,1)S(1)} %collective-permute-done.refs_0_), channel_id=1, source_target_pairs={{0,4},{4,0},{8,12},{12,8},{1,5},{5,1},{9,13},{13,9},{2,6},{6,2},{1... | collective-permute-start | bytes 811016 | tf_op jit(solution)/shard_map/ppermute | solution.py:48
  30.2 1.7 %collective-permute-start.9 = (bf16[176,768]{1,0:T(8,128)(2,1)S(1)}, bf16[176,768]{1,0:T(8,128)(2,1)S(1)}, u32[]{:S(2)}, u32[]{:S(2)}) collective-permute-start(bf16[176,768]{1,0:T(8,128)(2,1)S(1)} %collective-permute-done.8.refs_2_), channel_id=1, source_target_pairs={{0,4},{4,0},{8,12},{12,8},{1,5},{5,1},{9,13},{13,9},{2,6},{6,2},{1... | collective-permute-start | bytes 811016 | tf_op jit(solution)/shard_map/ppermute | solution.py:48
  30.5 9.3 %collective-permute-start.12 = (bf16[208,768]{1,0:T(8,128)(2,1)S(1)}, bf16[208,768]{1,0:T(8,128)(2,1)S(1)}, u32[]{:S(2)}, u32[]{:S(2)}) collective-permute-start(bf16[208,768]{1,0:T(8,128)(2,1)S(1)} %final_pack.1.refs_0_), channel_id=1, source_target_pairs={{0,4},{4,0},{8,12},{12,8},{1,5},{5,1},{9,13},{13,9},{2,6},{6,2},{1... | collective-permute-start | bytes 958472 | tf_op jit(solution)/shard_map/ppermute | solution.py:48
  38.2 1.6 %collective-permute-start.14 = (bf16[208,768]{1,0:T(8,128)(2,1)S(1)}, bf16[208,768]{1,0:T(8,128)(2,1)S(1)}, u32[]{:S(2)}, u32[]{:S(2)}) collective-permute-start(bf16[208,768]{1,0:T(8,128)(2,1)S(1)} %collective-permute-done.13.refs_2_), channel_id=1, source_target_pairs={{0,4},{4,0},{8,12},{12,8},{1,5},{5,1},{9,13},{13,9},{2,6},{6,2},{1... | collective-permute-start | bytes 958472 | tf_op jit(solution)/shard_map/ppermute | solution.py:48
